TPU v7x, 256 devices: a whole 4x4x8 slice. The times are simulated.
256 devices in a mesh: rows: 32 (over x, z), cols: 8 (over y, core).
Axes of the slice: x: 4, y: 4, z: 8, core: 2. Of those that a mesh axis runs over, the one named last changes fastest.
Arguments:
- features: bfloat16 [128, 131072], P('cols', 'rows'), may hold values from -6 to 6
- node_order: int32 [131072], P('rows'), may hold values from 0 to 131071, as said below
- tile_row: int32 [4096], P('rows'), may hold values from 0 to 1023, as said below
- tile_col: int32 [4096], P('rows'), may hold values from 0 to 1023, as said below
- tile_vals: bfloat16 [4096, 128, 128], P('rows'), may hold values from 0 to 0.099609375
- weight: bfloat16 [128, 128], replicated, may hold values from -0.5 to 0.5
- grad_out: bfloat16 [128, 131072], P('cols', 'rows'), may hold values from -6 to 6
Outputs:
- activated: bfloat16 [128, 131072], P('cols', 'rows')
- feat_grads: bfloat16 [128, 131072], P('cols', 'rows')
- weight_grad: float32 [128, 128], P(None, 'cols')
Inputs may be any that keep to these rules, and one draw needn't show every extreme that they name: Within each aligned run of 4096 entries, node_order is a permutation of the node numbers of that run. Tile t lies in the row blocks of its own index of rows: tile_row[t] // 32 == t // 128. Among the 128 tiles of one index of rows, the column blocks that belong to any one other index (tile_col // 32) are at most 8 distinct ones; every index of rows reaches 8 for some other index. Every row block has a tile on its own diagonal.
All inputs are finite; a program needn't handle non-finite values.
Results may differ from a plain program's by a relative error of at most 0.014.
Values may be sent and summed in bfloat16 or wider, within the bound.
No kernel may reach another device: no remote copies, remote signals or barrier semaphores. Data moves between devices by JAX's collectives and lax.ppermute only.
A program may use at most 128 MiB of HBM per device.

v0:
```python
import jax
import jax.numpy as jnp
from jax import lax
from jax.sharding import PartitionSpec as P


def shards(features, node_order, tile_row, tile_col, tile_vals, weight, grad_out):
    feat_cols, node_span = features.shape
    tile_size = tile_vals.shape[1]
    dev_blocks = node_span // tile_size
    row_peers = lax.axis_size("rows")
    all_blocks = row_peers * dev_blocks
    row_index = lax.axis_index("rows")
    local_order = node_order - row_index * node_span
    permuted = jnp.take(features, local_order, axis=1)
    local_row = tile_row - row_index * dev_blocks
    gathered = lax.all_gather(permuted, "rows", axis=1, tiled=True)
    tile_feats = jnp.take(gathered.reshape(feat_cols, all_blocks, tile_size), tile_col, axis=1)
    products = jnp.einsum("ftm,tnm->ftn", tile_feats, tile_vals, preferred_element_type=jnp.float32)
    summed = (
        jnp.zeros((feat_cols, dev_blocks, tile_size), jnp.float32).at[:, local_row].add(products)
    )
    aggregated = summed.reshape(feat_cols, node_span).astype(jnp.bfloat16)
    offset = lax.axis_index("cols") * feat_cols
    all_inputs = lax.all_gather(aggregated, "cols", axis=0, tiled=True)
    out_weight = lax.dynamic_slice_in_dim(weight, offset, feat_cols, 1)
    pre_act = lax.dot_general(
        out_weight, all_inputs, (((0,), (0,)), ((), ())), preferred_element_type=jnp.float32
    )
    activated = jax.nn.silu(pre_act).astype(jnp.bfloat16)
    logistic = jax.nn.sigmoid(pre_act)
    pre_grad = (
        grad_out.astype(jnp.float32) * logistic * (1.0 + pre_act * (1.0 - logistic))
    ).astype(jnp.bfloat16)
    weight_part = lax.dot_general(
        all_inputs, pre_grad, (((1,), (1,)), ((), ())), preferred_element_type=jnp.float32
    )
    weight_grad = lax.psum(weight_part, "rows") * float(all_blocks * tile_size) ** (-0.5)
    all_grads = lax.all_gather(pre_grad, "cols", axis=0, tiled=True)
    in_weight = lax.dynamic_slice_in_dim(weight, offset, feat_cols, 0)
    agg_grad = jnp.dot(in_weight, all_grads, preferred_element_type=jnp.float32).astype(
        jnp.bfloat16
    )
    grad_blocks = agg_grad.reshape(feat_cols, dev_blocks, tile_size)
    row_grads = jnp.take(grad_blocks, local_row, axis=1)
    back_terms = jnp.einsum(
        "ftn,tnm->ftm", row_grads, tile_vals, preferred_element_type=jnp.float32
    )
    partial_value = (
        jnp.zeros((feat_cols, all_blocks, tile_size), jnp.float32).at[:, tile_col].add(back_terms)
    )
    node_grads = lax.psum_scatter(
        partial_value.reshape(feat_cols, all_blocks * tile_size).astype(jnp.bfloat16),
        "rows",
        scatter_dimension=1,
        tiled=True,
    ).astype(jnp.float32)
    feat_grads = (
        jnp.zeros((feat_cols, node_span), jnp.float32)
        .at[:, local_order]
        .set(node_grads)
        .astype(jnp.bfloat16)
    )
    return (activated, feat_grads, weight_grad)


def solution(mesh):
    in_specs = (
        P("cols", "rows"),
        P("rows"),
        P("rows"),
        P("rows"),
        P("rows", None, None),
        P(),
        P("cols", "rows"),
    )
    out_specs = (P("cols", "rows"), P("cols", "rows"), P(None, "cols"))
    return jax.shard_map(shards, mesh=mesh, in_specs=in_specs, out_specs=out_specs, check_vma=False)
```

profile of v0, /device:TPU:2, one launch (start us, length us, event | category | flops | bytes accessed | tf_op | source)
XLA Modules:
  0.0 622.3 jit_solution(10570641069579119246)
XLA Ops:
  7.3 0.7 compare_and_fusion
  8.0 1.4 copy.12
  9.4 12.1 %gather_fusion = bf16[4096,16]{1,0:T(8,128)(2,1)S(1)} fusion(bf16[16,4096]{0,1:T(8,128)(2,1)S(1)} %copy.12, s32[4096]{0:T(1024)S(1)} %broadcast_clamp_fusion), kind=kCustom, calls=%fused_computation | custom fusion | bytes 278528 | tf_op jit(solution)/shard_map/jit(_take)/gather | solution.py:15
  21.5 2.9 select_bitcast_fusion
  24.5 0.0 all-gather.6.cloned.1.call-start
  24.6 235.0 %all-gather.4.cloned.1.call-done = bf16[16,131072]{0,1:T(8,128)(2,1)} async-done(((bf16[16,4096]{0,1:T(8,128)(2,1)}), bf16[16,131072]{0,1:T(8,128)(2,1)}) %all-gather.4.cloned.1.call-update) | async-done | bytes 4194320 | tf_op jit(solution)/shard_map/all_gather | solution.py:17
  259.6 25.0 %copy.13 = bf16[16,1024,128]{2,0,1:T(8,128)(2,1)} copy(bf16[16,1024,128]{0,2,1:T(8,128)(2,1)} %bitcast.32) | data formatting | bytes 8388608 | tf_op jit(solution)/shard_map/reshape | solution.py:18
  284.6 2.9 gather_fusion.1
  287.5 4.5 fusion.5
  292.1 5.2 scatter_fusion
  297.3 0.7 copy_bitcast_fusion.1
  298.0 0.0 all-gather.8.cloned.1.call-start
  298.1 24.4 %all-gather.6.cloned.1.call-done = bf16[128,4096]{1,0:T(8,128)(2,1)} async-done(((bf16[16,4096]{1,0:T(8,128)(2,1)}), bf16[128,4096]{1,0:T(8,128)(2,1)}) %all-gather.6.cloned.1.call-update) | async-done | bytes 1048592 | tf_op jit(solution)/shard_map/all_gather | solution.py:25
  322.4 2.3 multiply_convert_fusion
  324.8 0.0 reduce-scatter.2.cloned.1.call-start
  324.8 25.9 %all-gather.8.cloned.1.call-done = bf16[128,4096]{1,0:T(8,128)(2,1)} async-done(((bf16[16,4096]{1,0:T(8,128)(2,1)}), bf16[128,4096]{1,0:T(8,128)(2,1)}) %all-gather.8.cloned.1.call-update) | async-done | bytes 1048592 | tf_op jit(solution)/shard_map/all_gather | solution.py:39
  350.7 1.5 fusion
  352.2 0.7 gather_fusion.2
  353.0 3.4 fusion.3
  356.4 3.8 broadcast_in_dim.55
  360.2 14.4 %scatter_fusion.1 = f32[16,1024,128]{2,0,1:T(8,128)} fusion(f32[16,1024,128]{2,0,1:T(8,128)} %broadcast_in_dim.55, s32[128]{0:T(128)S(1)} %compare_select_fusion.1, f32[128,16,128]{2,1,0:T(8,128)S(1)} %fusion.3), kind=kCustom, calls=%fused_computation.4 | custom fusion | flops 262144 | bytes 3146240 | tf_op jit(solution)/shard_map/scatter-add | solution.py:50
  374.6 5.7 copy_bitcast_fusion
  380.4 1.2 copy-done.1
  381.6 0.4 fusion.20
  382.0 64.6 %psum.7 = f32[128,16]{0,1:T(8,128)S(1)} all-reduce(f32[128,16]{0,1:T(8,128)S(1)} %fusion.20), channel_id=1, replica_groups=mesh['rows'=32,'cols'=8] {'rows'}, use_global_device_ids=true, to_apply=%region_4.5 | all-reduce | flops 2048 | bytes 16384 | tf_op jit(solution)/shard_map/psum | solution.py:38
  446.5 0.6 broadcast_multiply_fusion
  447.1 153.3 %reduce-scatter.2.cloned.1.call-done = bf16[16,4096]{1,0:T(8,128)(2,1)} async-done(((bf16[16,131072]{1,0:T(8,128)(2,1)}), bf16[16,4096]{1,0:T(8,128)(2,1)}) %reduce-scatter.2.cloned.1.call-update) | async-done | bytes 131088 | tf_op jit(solution)/shard_map/reduce_scatter | solution.py:52
  600.4 0.9 convert_bitcast_fusion.1
  601.3 2.0 copy.17
  603.3 11.4 %scatter_custom_fusion.2 = f32[16,4096]{0,1:T(8,128)S(1)} fusion(s32[4096]{0:T(1024)S(1)} %get-tuple-element.12, f32[4096,16]{1,0:T(8,128)} %copy.17, f32[]{:T(128)} %constant.32.clone.1), kind=kCustom, calls=%fused_computation.11 | custom fusion | bytes 262656 | tf_op jit(solution)/shard_map/scatter | solution.py:61
  614.7 0.1 convert_element_type.39
  614.8 1.0 copy.18
  (23 shorter events, 0.2 us)
Async XLA Ops:
  7.2 315.3 %copy-start = (bf16[128,128]{1,0:T(8,128)(2,1)S(1)}, bf16[128,128]{1,0:T(8,128)(2,1)}, u32[]{:S(2)}) copy-start(bf16[128,128]{1,0:T(8,128)(2,1)} %param.12) | copy-start | bytes 98308
  7.2 17.3 %copy-start.4 = (s32[128]{0:T(128)S(1)}, s32[128]{0:T(128)}, u32[]{:S(2)}) copy-start(s32[128]{0:T(128)} %param.10) | copy-start | bytes 1540
  7.2 17.4 %copy-start.3 = (s32[128]{0:T(128)S(1)}, s32[128]{0:T(128)}, u32[]{:S(2)}) copy-start(s32[128]{0:T(128)} %param.9) | copy-start | bytes 1540
  7.2 252.4 %all-gather.4.cloned.1.call-start = ((), (), s32[]{:S(2)}) async-start(), calls=%async_computation.1 | async-start | bytes 34603008 | tf_op jit(solution)/shard_map/all_gather | solution.py:17
  24.5 298.0 %all-gather.6.cloned.1.call-start = ((), (), s32[]{:S(2)}) async-start(), calls=%async_computation.2 | async-start | bytes 1179648 | tf_op jit(solution)/shard_map/all_gather | solution.py:25
  287.5 35.0 %copy-start.5 = (bf16[16,4096]{1,0:T(8,128)(2,1)S(1)}, bf16[16,4096]{1,0:T(8,128)(2,1)}, u32[]{:S(2)}) copy-start(bf16[16,4096]{1,0:T(8,128)(2,1)} %param.13) | copy-start | bytes 393220
  298.0 52.7 %all-gather.8.cloned.1.call-start = ((), (), s32[]{:S(2)}) async-start(), calls=%async_computation.3 | async-start | bytes 1179648 | tf_op jit(solution)/shard_map/all_gather | solution.py:39
  324.8 275.6 %reduce-scatter.2.cloned.1.call-start = ((), (), s32[]{:S(2)}) async-start(), calls=%async_computation.4 | async-start | bytes 4325376 | tf_op jit(solution)/shard_map/reduce_scatter | solution.py:52
  380.4 1.2 copy-start.1
  380.4 1.2 copy-start.2
Sparse Core Ops, SparseCore 0:
  24.6 234.9 all-gather.3
  298.1 24.2 all-gather.5
  324.9 25.7 all-gather.7
  380.5 219.8 reduce-scatter.1
where the time goes:
time: 625 us; the launch traced here: 622 us
  waiting for transfers between devices  439 us (70%)
  blocking collectives  64.6 us (10%)
  local copies, waits for them, and re-layouts  61.6 us (10%)
  other arithmetic  31.4 us (5%)
  between operations  13.9 us (2%)
  matrix products  12.1 us (2%)
    all_gather x1, waiting for transfers between devices, shards(): gathered = lax.all_gather(permuted, 'rows', axis=1, tiled=True)  235 us
    reduce_scatter x1, waiting for transfers between devices, shards(): lax.psum_scatter(partial_value.reshape(feat_cols, all_blocks * tile_size)...  153 us
    psum x1, blocking collectives, shards(): lax.psum(weight_part, 'rows') * float(all_blocks * tile_size) ** (-0.5)  64.6 us
    all_gather x1, waiting for transfers between devices, shards(): all_grads = lax.all_gather(pre_grad, 'cols', axis=0, tiled=True)  25.9 us
    reshape x1, local copies, waits for them, and re-layouts, shards(): gathered.reshape(feat_cols, all_blocks, tile_size)  25 us
    all_gather x1, waiting for transfers between devices, shards(): all_inputs = lax.all_gather(aggregated, 'cols', axis=0, tiled=True)  24.4 us
    scatter-add x1, other arithmetic, shards(): jnp.zeros((feat_cols, all_blocks, tile_size), jnp.float32).at[:, tile_col]  14.4 us
  transfers between devices with their start and end apart: 4, of which 4 were waited for; matrix products, arithmetic and copies ran while one was open for 0% of the time, Pallas kernels for 0%

commit v1 on v0

v1 whole, which is shorter than its diff:
```python
import functools

import jax
import jax.numpy as jnp
from jax import lax
from jax.experimental import pallas as pl
from jax.experimental.pallas import tpu as pltpu
from jax.sharding import PartitionSpec as P

BF16 = jnp.bfloat16
F32 = jnp.float32
I32 = jnp.int32
SLOTS = 8
STEP = 16
VMEM = pl.BlockSpec(memory_space=pltpu.VMEM)
SMEM = pl.BlockSpec(memory_space=pltpu.SMEM)
NN = (((1,), (0,)), ((), ()))
NT = (((1,), (1,)), ((), ()))
TN = (((0,), (0,)), ((), ()))


def params(**kw):
    return pltpu.CompilerParams(vmem_limit_bytes=48 << 20, **kw)


def cost(flops, bytes_accessed):
    return pl.CostEstimate(flops=flops, bytes_accessed=bytes_accessed, transcendentals=0)


def dot(a, b, dims):
    return lax.dot_general(a, b, dims, preferred_element_type=F32)


def index_kernel(row_ref, col_ref, want_ref, place_ref, local_ref):
    peers = want_ref.shape[0]
    blocks = 32
    col = col_ref[...]
    row = row_ref[...]
    peer, block = col >> 5, col & 31
    tiles = col.shape[1]
    of_peer = (lax.broadcasted_iota(I32, (peers, tiles), 0) == peer).astype(F32)
    of_block = (lax.broadcasted_iota(I32, (blocks, tiles), 0) == block).astype(F32)
    counts = dot(of_peer.astype(BF16), of_block.astype(BF16), NT)
    present = (counts > 0.5).astype(F32)
    before = (
        lax.broadcasted_iota(I32, (blocks, blocks), 0)
        < lax.broadcasted_iota(I32, (blocks, blocks), 1)
    ).astype(F32)
    rank = dot(present.astype(BF16), before.astype(BF16), NN)
    number = lax.broadcasted_iota(I32, (peers, blocks), 1).astype(F32)
    lane = lax.broadcasted_iota(I32, (peers, 128), 1)
    want = jnp.zeros((peers, 128), F32)
    for s in range(SLOTS):
        chosen = jnp.sum(
            jnp.where(rank == float(s), present * number, 0.0), axis=1, keepdims=True
        )
        want = jnp.where(lane == s, chosen, want)
    want_ref[...] = want.astype(I32).reshape(peers, 1, 128)
    rank_of = dot(rank.astype(BF16), of_peer.astype(BF16), TN)
    tile_rank = jnp.sum(rank_of * of_block, axis=0, keepdims=True).astype(I32)
    own = peer == (row >> 5)
    place_ref[...] = jnp.where(own, peers * SLOTS + block, peer * SLOTS + tile_rank)
    local_ref[...] = row & 31


def permute_kernel(features_ref, order_ref, out_ref, blocked):
    count = order_ref.shape[0]
    width = features_ref.shape[0]
    for s in range(count):
        blocked[s * width : (s + 1) * width, :] = features_ref[:, s * 128 : (s + 1) * 128]
    low = lax.broadcasted_iota(I32, (128, 256), 0)
    for j in range(0, count, 2):
        o = jnp.concatenate([order_ref[j : j + 1, :], order_ref[j + 1 : j + 2, :]], axis=1)
        o = o & (count * 128 - 1)
        pick = jnp.where(low == (o & 127), 1.0, 0.0).astype(BF16)
        high = o >> 7
        spread = dot(blocked[...], pick, NN)
        total = jnp.zeros((width, 256), F32)
        for s in range(count):
            total = total + jnp.where(high == s, spread[s * width : (s + 1) * width], 0.0)
        total = total.astype(BF16)
        out_ref[j] = total[:, :128]
        out_ref[j + 1] = total[:, 128:]


def pack_kernel(asked_ref, blocks_ref, send_ref):
    for p in range(send_ref.shape[0]):
        for s in range(SLOTS):
            send_ref[p, s] = blocks_ref[asked_ref[p, 0, s]]


def forward_kernel(place_ref, local_ref, got_ref, own_ref, grad_ref, tiles_ref, out_ref, feats, prod, total):
    step = pl.program_id(0)
    slots = got_ref.shape[0] * SLOTS
    groups = out_ref.shape[0]
    per = out_ref.shape[1] // 2

    @pl.when(step == 0)
    def _():
        total[...] = jnp.zeros_like(total)
        for p in range(got_ref.shape[0]):
            feats[p * SLOTS : (p + 1) * SLOTS] = got_ref[p]
        feats[slots:] = own_ref[...]
        for c in range(groups):
            for b in range(per):
                at = (c * per + b) * 128
                out_ref[c, per + b] = grad_ref[:, at : at + 128]

    for t in range(STEP):
        prod[t] = dot(feats[place_ref[0, step * STEP + t]], tiles_ref[t], NT)
    for t in range(STEP):
        r = local_ref[0, step * STEP + t]
        total[r] = total[r] + prod[t]

    @pl.when(step == pl.num_programs(0) - 1)
    def _():
        for c in range(groups):
            for b in range(per):
                out_ref[c, b] = total[c * per + b].astype(BF16)


def dense_kernel(weight_ref, got_ref, out_ref):
    groups, _, width, _ = got_ref.shape
    per = got_ref.shape[1] // 2
    inputs = groups * width
    weight = weight_ref[...]
    weight_t = weight.astype(F32).T.astype(BF16)
    part = jnp.zeros((inputs, inputs), F32)
    for b in range(per):
        agg = got_ref[:, b].reshape(inputs, 128)
        grad = got_ref[:, per + b].reshape(inputs, 128).astype(F32)
        pre = dot(weight_t, agg, NN)
        logistic = jax.nn.sigmoid(pre)
        act = (pre * logistic).astype(BF16)
        pre_grad = (grad * logistic * (1.0 + pre * (1.0 - logistic))).astype(BF16)
        agg_grad = dot(weight, pre_grad, NN).astype(BF16)
        part = part + dot(pre_grad, agg, NT)
        out_ref[:, b] = agg_grad.reshape(groups, width, 128)
        out_ref[:, per + b] = act.reshape(groups, width, 128)
    high = part.astype(BF16)
    out_ref[:, 2 * per] = high.reshape(groups, width, 128)
    out_ref[:, 2 * per + 1] = (part - high.astype(F32)).astype(BF16).reshape(groups, width, 128)


def backward_kernel(place_ref, local_ref, got_ref, tiles_ref, send_ref, own_ref, act_ref, prod, total):
    step = pl.program_id(0)
    groups = got_ref.shape[0]
    per = (got_ref.shape[1] - 2) // 2
    peers = send_ref.shape[0]

    @pl.when(step == 0)
    def _():
        total[...] = jnp.zeros_like(total)
        part = got_ref[0, 2 * per].astype(F32) + got_ref[0, 2 * per + 1].astype(F32)
        for c in range(1, groups):
            part = part + got_ref[c, 2 * per].astype(F32) + got_ref[c, 2 * per + 1].astype(F32)
        part = part.astype(BF16)
        for p in range(peers):
            send_ref[p, SLOTS] = part
        for c in range(groups):
            for b in range(per):
                at = (c * per + b) * 128
                act_ref[:, at : at + 128] = got_ref[c, per + b]

    for t in range(STEP):
        r = local_ref[0, step * STEP + t]
        prod[t] = dot(got_ref[r // per, r % per], tiles_ref[t], NN)
    for t in range(STEP):
        d = place_ref[0, step * STEP + t]
        total[d] = total[d] + prod[t]

    @pl.when(step == pl.num_programs(0) - 1)
    def _():
        for p in range(peers):
            send_ref[p, :SLOTS] = total[p * SLOTS : (p + 1) * SLOTS].astype(BF16)
        own_ref[...] = total[peers * SLOTS :]


def final_kernel(scale, asked_ref, got_ref, own_ref, order_ref, grads_ref, weight_ref, total, spread, pick):
    peers = got_ref.shape[0]
    count = order_ref.shape[0]
    width = grads_ref.shape[0]
    total[...] = own_ref[...]
    part = got_ref[0, SLOTS].astype(F32)
    for p in range(1, peers):
        part = part + got_ref[p, SLOTS].astype(F32)
    weight_ref[...] = (part * scale).T
    for p in range(peers):
        for s in range(SLOTS):
            at = asked_ref[p, 0, s]
            total[at] = total[at] + got_ref[p, s].astype(F32)
    low = lax.broadcasted_iota(I32, (128, 128), 0)
    for j in range(count):
        o = order_ref[j : j + 1, :] & (count * 128 - 1)
        lanes = slice(j * 128, (j + 1) * 128)
        pick[:, lanes] = jnp.where(low == (o & 127), 1.0, 0.0).astype(BF16)
        high = o >> 7
        value = total[j]
        for s in range(count):
            spread[s * width : (s + 1) * width, lanes] = jnp.where(high == s, value, 0.0).astype(BF16)
    result = dot(spread[...], pick[...], NT).astype(BF16)
    for s in range(count):
        grads_ref[:, s * 128 : (s + 1) * 128] = result[s * width : (s + 1) * width, :]


def shards(features, node_order, tile_row, tile_col, tile_vals, weight, grad_out):
    width, span = features.shape
    tiles, size, _ = tile_vals.shape
    count = span // size
    peers = lax.axis_size("rows")
    groups = lax.axis_size("cols")
    per = count // groups
    order = node_order.reshape(count, size)
    steps = tiles // STEP

    with jax.named_scope("index"):
        want, place, local = pl.pallas_call(
            index_kernel,
            out_shape=(
                jax.ShapeDtypeStruct((peers, 1, 128), I32),
                jax.ShapeDtypeStruct((1, tiles), I32),
                jax.ShapeDtypeStruct((1, tiles), I32),
            ),
            in_specs=[VMEM, VMEM],
            out_specs=(VMEM, VMEM, VMEM),
            compiler_params=params(),
        )(tile_row.reshape(1, tiles), tile_col.reshape(1, tiles))
        asked = lax.all_to_all(want, "rows", 0, 0, tiled=True)

    with jax.named_scope("permute"):
        own = pl.pallas_call(
            permute_kernel,
            out_shape=jax.ShapeDtypeStruct((count, width, size), BF16),
            in_specs=[VMEM, VMEM],
            out_specs=VMEM,
            scratch_shapes=[pltpu.VMEM((count * width, size), BF16)],
            compiler_params=params(),
            cost_estimate=cost(2 * 512 * 128 * 4096, 1 << 20),
        )(features, order)

    with jax.named_scope("pack"):
        send = pl.pallas_call(
            pack_kernel,
            out_shape=jax.ShapeDtypeStruct((peers, SLOTS, width, size), BF16),
            in_specs=[SMEM, VMEM],
            out_specs=VMEM,
            compiler_params=params(),
        )(asked, own)
        got = lax.all_to_all(send, "rows", 0, 0, tiled=True)

    whole = lambda *shape: pl.BlockSpec(shape, lambda i: (0,) * len(shape))
    tile_spec = pl.BlockSpec((STEP, size, size), lambda i: (i, 0, 0))

    with jax.named_scope("forward"):
        mixed = pl.pallas_call(
            forward_kernel,
            out_shape=jax.ShapeDtypeStruct((groups, 2 * per, width, size), BF16),
            grid=(steps,),
            in_specs=[
                SMEM,
                SMEM,
                whole(peers, SLOTS, width, size),
                whole(count, width, size),
                whole(width, span),
                tile_spec,
            ],
            out_specs=whole(groups, 2 * per, width, size),
            scratch_shapes=[
                pltpu.VMEM((peers * SLOTS + count, width, size), BF16),
                pltpu.VMEM((STEP, width, size), F32),
                pltpu.VMEM((count, width, size), F32),
            ],
            compiler_params=params(dimension_semantics=("arbitrary",)),
            cost_estimate=cost(2 * tiles * width * size * size, 6 << 20),
        )(place, local, got, own, grad_out, tile_vals)
        mixed = lax.all_to_all(mixed, "cols", 0, 0, tiled=True)

    with jax.named_scope("dense"):
        back = pl.pallas_call(
            dense_kernel,
            out_shape=jax.ShapeDtypeStruct((groups, 2 * per + 2, width, size), BF16),
            in_specs=[VMEM, VMEM],
            out_specs=VMEM,
            compiler_params=params(),
        )(weight, mixed)
        back = lax.all_to_all(back, "cols", 0, 0, tiled=True)

    with jax.named_scope("backward"):
        parts, kept, activated = pl.pallas_call(
            backward_kernel,
            out_shape=(
                jax.ShapeDtypeStruct((peers, SLOTS + 1, width, size), BF16),
                jax.ShapeDtypeStruct((count, width, size), F32),
                jax.ShapeDtypeStruct((width, span), BF16),
            ),
            grid=(steps,),
            in_specs=[SMEM, SMEM, whole(groups, 2 * per + 2, width, size), tile_spec],
            out_specs=(
                whole(peers, SLOTS + 1, width, size),
                whole(count, width, size),
                whole(width, span),
            ),
            scratch_shapes=[
                pltpu.VMEM((STEP, width, size), F32),
                pltpu.VMEM((peers * SLOTS + count, width, size), F32),
            ],
            compiler_params=params(dimension_semantics=("arbitrary",)),
            cost_estimate=cost(2 * tiles * width * size * size, 6 << 20),
        )(place, local, back, tile_vals)
        parts = lax.all_to_all(parts, "rows", 0, 0, tiled=True)

    with jax.named_scope("final"):
        feat_grads, weight_grad = pl.pallas_call(
            functools.partial(final_kernel, float(peers * span) ** -0.5),
            out_shape=(
                jax.ShapeDtypeStruct((width, span), BF16),
                jax.ShapeDtypeStruct((size, width), F32),
            ),
            in_specs=[SMEM, VMEM, VMEM, VMEM],
            out_specs=(VMEM, VMEM),
            scratch_shapes=[
                pltpu.VMEM((count, width, size), F32),
                pltpu.VMEM((count * width, span), BF16),
                pltpu.VMEM((size, span), BF16),
            ],
            compiler_params=params(),
        )(asked, parts, kept, order)
    return activated, feat_grads, weight_grad


def solution(mesh):
    in_specs = (
        P("cols", "rows"),
        P("rows"),
        P("rows"),
        P("rows"),
        P("rows", None, None),
        P(),
        P("cols", "rows"),
    )
    out_specs = (P("cols", "rows"), P("cols", "rows"), P(None, "cols"))
    return jax.shard_map(shards, mesh=mesh, in_specs=in_specs, out_specs=out_specs, check_vma=False)
```

time: 625 us -> 132 us (0.21)
  waiting for transfers between devices: 439 us -> 5.51 us
  local copies, waits for them, and re-layouts: 61.6 us -> 5.79 us
  other arithmetic: 31.4 us -> 0 us
  blocking collectives: 64.6 us -> 91.4 us
  Pallas kernels: 0 us -> 16.9 us
  between operations: 13.9 us -> 0.71 us
  matrix products: 12.1 us -> 0 us
  starting transfers between devices: 0.16 us -> 11.6 us
    all_gather x3 -> x0, waiting for transfers between devices: 285 us -> none  [the longest x1 235 us: shards(): gathered = lax.all_gather(permuted, 'rows', axis=1, tiled=True)]
    reduce_scatter x1 -> x0, waiting for transfers between devices: 153 us -> none  [shards(): lax.psum_scatter(partial_value.reshape(feat_cols, all_blocks * tile_size)...]
    all_to_all x0 -> x4, blocking collectives: none -> 91.4 us  [the longest x1 38.9 us: shards(): parts = lax.all_to_all(parts, 'rows', 0, 0, tiled=True)]
    psum x1 -> x0, blocking collectives: 64.6 us -> none  [shards(): lax.psum(weight_part, 'rows') * float(all_blocks * tile_size) ** (-0.5)]
    reshape x2 -> x0, local copies, waits for them, and re-layouts: 25 us -> none  [the longest x1 25 us: shards(): gathered.reshape(feat_cols, all_blocks, tile_size)]
    scatter-add x2 -> x0, other arithmetic: 19.7 us -> none  [the longest x1 14.4 us: shards(): jnp.zeros((feat_cols, all_blocks, tile_size), jnp.float32).at[:, tile_col]]
    pallas_call x0 -> x7, Pallas kernels: none -> 16.9 us  [the longest x1 5.25 us: shards(): pl.pallas_call(functools.partial(final_kernel, float(peers * span) ** (-0...]
    gather x3 -> x0, local copies, waits for them, and re-layouts: 15.7 us -> none  [the longest x1 12.1 us: shards(): permuted = jnp.take(features, local_order, axis=1)]
  transfers between devices with their start and end apart: 4 -> 1, of which waited for: 4 -> 1; matrix products, arithmetic and copies ran while one was open for 0% -> 0% of each run, Pallas kernels for 0% -> 1%
where the time goes in v1:
time: 132 us
  blocking collectives  91.4 us (69%)
  Pallas kernels  16.9 us (13%)
  starting transfers between devices  11.6 us (9%)
  local copies, waits for them, and re-layouts  5.79 us (4%)
  waiting for transfers between devices  5.51 us (4%)
    all_to_all x1, blocking collectives, shards(): parts = lax.all_to_all(parts, 'rows', 0, 0, tiled=True)  38.9 us
    all_to_all x1, blocking collectives, shards(): got = lax.all_to_all(send, 'rows', 0, 0, tiled=True)  30 us
    all_to_all x1, blocking collectives, shards(): mixed = lax.all_to_all(mixed, 'cols', 0, 0, tiled=True)  11.8 us
    all_to_all x1, starting transfers between devices, shards(): asked = lax.all_to_all(want, 'rows', 0, 0, tiled=True)  11.6 us
    all_to_all x1, blocking collectives, shards(): back = lax.all_to_all(back, 'cols', 0, 0, tiled=True)  10.6 us
    unnamed x19, local copies, waits for them, and re-layouts  5.79 us
    all_to_all x1, waiting for transfers between devices, shards(): asked = lax.all_to_all(want, 'rows', 0, 0, tiled=True)  5.51 us
    pallas_call x1, Pallas kernels, shards(): pl.pallas_call(functools.partial(final_kernel, float(peers * span) ** (-0...  5.25 us
  transfers between devices with their start and end apart: 1, of which 1 were waited for; matrix products, arithmetic and copies ran while one was open for 0% of the time, Pallas kernels for 1%

profile of v1, /device:TPU:2, one launch (start us, length us, event | category | flops | bytes accessed | tf_op | source)
XLA Modules:
  0.0 131.9 jit_solution(18351562299694075836)
XLA Ops:
  0.6 0.0 copy-start.7
  0.6 0.6 copy-done.7
  1.3 0.0 copy-start.8
  1.3 0.7 copy-done.8
  1.9 1.0 index.1
  2.9 11.6 %all-to-all-start = ((s32[32,1,128]{2,1,0:T(1,128)}), s32[32,1,128]{2,1,0:T(1,128)S(1)}, u32[]{:S(2)}, u32[]{:S(2)}) async-start(s32[32,1,128]{2,1,0:T(1,128)} %get-tuple-element.13), calls=%async_computation | async-start | bytes 32768 | tf_op jit(solution)/shard_map/index/all_to_all | solution.py:228
  14.5 0.0 copy-start.4
  14.6 0.7 copy-done.4
  15.3 0.0 copy-start.6
  15.3 0.9 copy-done.6
  16.2 1.4 %permute.1.blocks_ref.own_ref = bf16[32,16,128]{2,1,0:T(8,128)(2,1)S(1)} custom-call(bf16[16,4096]{1,0:T(8,128)(2,1)S(1)} %copy-done.6, s32[32,128]{1,0:T(8,128)S(1)} %bitcast.3), custom_call_target="tpu_custom_call" | custom-call | flops 536870912 | bytes 1048576 | tf_op jit(solution)/shard_map/permute/pallas_call | solution.py:231
  17.6 5.5 %all-to-all-done.asked_ref = s32[32,1,128]{2,1,0:T(1,128)S(1)} async-done(((s32[32,1,128]{2,1,0:T(1,128)}), s32[32,1,128]{2,1,0:T(1,128)S(1)}, u32[]{:S(2)}, u32[]{:S(2)}) %all-to-all-start) | async-done | bytes 16416 | tf_op jit(solution)/shard_map/index/all_to_all | solution.py:228
  23.1 1.0 pack.1
  24.1 0.0 copy-start.2
  24.1 30.0 %all_to_all.25.got_ref = bf16[32,8,16,128]{3,2,1,0:T(8,128)(2,1)S(1)} all-to-all(bf16[32,8,16,128]{3,2,1,0:T(8,128)(2,1)S(1)} %pack.1), channel_id=1, replica_groups=mesh['rows'=32,'cols'=8] {'rows'}, dimensions={0} | all-to-all | bytes 2097152 | tf_op jit(solution)/shard_map/pack/all_to_all | solution.py:249
  54.1 0.0 copy-done.2
  54.1 0.0 copy-start
  54.2 2.2 %copy-done = bf16[128,128,128]{2,1,0:T(8,128)(2,1)S(1)} copy-done((bf16[128,128,128]{2,1,0:T(8,128)(2,1)S(1)}, bf16[128,128,128]{2,1,0:T(8,128)(2,1)}, u32[]{:S(2)}) %copy-start) | copy-done | bytes 4194328
  56.3 0.0 copy-start.3
  56.3 0.0 copy-start.1
  56.3 3.9 %forward.1 = bf16[8,8,16,128]{3,2,1,0:T(8,128)(2,1)S(1)} custom-call(s32[1,128]{1,0:T(1,128)S(1)} %get-tuple-element.11.place_ref, s32[1,128]{1,0:T(1,128)S(1)} %get-tuple-element.12.local_ref, bf16[32,8,16,128]{3,2,1,0:T(8,128)(2,1)S(1)} %all_to_all.25.got_ref, bf16[32,16,128]{2,1,0:T(8,128)(2,1)S(1)} %permute.1.blocks_ref.own_ref, ...), custom_call_target="tpu_custom_call" | custom-call | flops 67108864 | bytes 6291456 | tf_op jit(solution)/shard_map/forward/pallas_call | solution.py:255
  60.2 11.8 %all_to_all.26.got_ref = bf16[8,8,16,128]{3,2,1,0:T(8,128)(2,1)S(1)} all-to-all(bf16[8,8,16,128]{3,2,1,0:T(8,128)(2,1)S(1)} %forward.1), channel_id=1, replica_groups=mesh['rows'=32,'cols'=8] {'cols'}, dimensions={0} | all-to-all | bytes 524288 | tf_op jit(solution)/shard_map/forward/all_to_all | solution.py:276
  72.0 0.0 copy-done.3
  72.0 0.7 dense.1
  72.8 10.6 %all_to_all.27.got_ref = bf16[8,10,16,128]{3,2,1,0:T(8,128)(2,1)S(1)} all-to-all(bf16[8,10,16,128]{3,2,1,0:T(8,128)(2,1)S(1)} %dense.1), channel_id=1, replica_groups=mesh['rows'=32,'cols'=8] {'cols'}, dimensions={0} | all-to-all | bytes 655360 | tf_op jit(solution)/shard_map/dense/all_to_all | solution.py:286
  83.4 0.0 copy-done.1
  83.4 3.6 %backward.1 = (bf16[32,9,16,128]{3,2,1,0:T(8,128)(2,1)S(1)}, f32[32,16,128]{2,1,0:T(8,128)S(1)}, bf16[16,4096]{1,0:T(8,128)(2,1)}) custom-call(s32[1,128]{1,0:T(1,128)S(1)} %get-tuple-element.11.place_ref, s32[1,128]{1,0:T(1,128)S(1)} %get-tuple-element.12.local_ref, bf16[8,10,16,128]{3,2,1,0:T(8,128)(2,1)S(1)} %all_to_all.27.got_ref, ...), custom_call_target="tpu_custom_call" | custom-call | flops 67108864 | bytes 6291456 | tf_op jit(solution)/shard_map/backward/pallas_call | solution.py:289
  87.0 0.0 copy-start.5
  87.0 38.9 %all_to_all.28.got_ref = bf16[32,9,16,128]{3,2,1,0:T(8,128)(2,1)S(1)} all-to-all(bf16[32,9,16,128]{3,2,1,0:T(8,128)(2,1)S(1)} %get-tuple-element.15), channel_id=1, replica_groups=mesh['rows'=32,'cols'=8] {'rows'}, dimensions={0} | all-to-all | bytes 2359296 | tf_op jit(solution)/shard_map/backward/all_to_all | solution.py:310
  126.0 0.0 copy-done.5
  126.0 5.3 %final.1 = (bf16[16,4096]{1,0:T(8,128)(2,1)}, f32[128,16]{1,0:T(8,128)S(1)}) custom-call(s32[32,1,128]{2,1,0:T(1,128)S(1)} %all-to-all-done.asked_ref, bf16[32,9,16,128]{3,2,1,0:T(8,128)(2,1)S(1)} %all_to_all.28.got_ref, f32[32,16,128]{2,1,0:T(8,128)S(1)} %get-tuple-element.16.own_ref, s32[32,128]{1,0:T(8,128)S(1)} %bitcast.4), custom_call_target="tpu_custom_call" | custom-call | tf_op jit(solution)/shard_map/final/pallas_call | solution.py:313
  131.2 0.7 copy.10
Async XLA Ops:
  0.6 0.7 copy-start.7
  1.3 0.7 copy-start.8
  2.9 20.2 %all-to-all-start = ((s32[32,1,128]{2,1,0:T(1,128)}), s32[32,1,128]{2,1,0:T(1,128)S(1)}, u32[]{:S(2)}, u32[]{:S(2)}) async-start(s32[32,1,128]{2,1,0:T(1,128)} %get-tuple-element.13), calls=%async_computation | async-start | bytes 32768 | tf_op jit(solution)/shard_map/index/all_to_all | solution.py:228
  14.5 0.7 copy-start.4
  15.3 0.9 copy-start.6
  24.1 30.1 %copy-start.2 = (bf16[16,4096]{1,0:T(8,128)(2,1)S(1)}, bf16[16,4096]{1,0:T(8,128)(2,1)}, u32[]{:S(2)}) copy-start(bf16[16,4096]{1,0:T(8,128)(2,1)} %grad_ref.1) | copy-start | bytes 393220
  54.1 2.2 %copy-start = (bf16[128,128,128]{2,1,0:T(8,128)(2,1)S(1)}, bf16[128,128,128]{2,1,0:T(8,128)(2,1)}, u32[]{:S(2)}) copy-start(bf16[128,128,128]{2,1,0:T(8,128)(2,1)} %tiles_ref.3) | copy-start | bytes 12582916
  56.3 15.7 %copy-start.3 = (bf16[128,128]{1,0:T(8,128)(2,1)S(1)}, bf16[128,128]{1,0:T(8,128)(2,1)}, u32[]{:S(2)}) copy-start(bf16[128,128]{1,0:T(8,128)(2,1)} %weight_ref.1) | copy-start | bytes 98308
  56.3 27.1 %copy-start.1 = (bf16[128,128,128]{2,1,0:T(8,128)(2,1)S(1)}, bf16[128,128,128]{2,1,0:T(8,128)(2,1)}, u32[]{:S(2)}) copy-start(bf16[128,128,128]{2,1,0:T(8,128)(2,1)} %tiles_ref.3) | copy-start | bytes 12582916
  87.0 38.9 %copy-start.5 = (s32[4096]{0:T(1024)S(1)}, s32[4096]{0:T(1024)}, u32[]{:S(2)}) copy-start(s32[4096]{0:T(1024)} %param.8) | copy-start | bytes 49156

commit v2 on v1

v2 whole, which is shorter than its diff:
```python
import functools

import jax
import jax.numpy as jnp
from jax import lax
from jax.experimental import pallas as pl
from jax.experimental.pallas import tpu as pltpu
from jax.sharding import PartitionSpec as P

BF16 = jnp.bfloat16
F32 = jnp.float32
I32 = jnp.int32
SLOTS = 8
STEP = 16
WAYS = 2
VMEM = pl.BlockSpec(memory_space=pltpu.VMEM)
SMEM = pl.BlockSpec(memory_space=pltpu.SMEM)
NN = (((1,), (0,)), ((), ()))
NT = (((1,), (1,)), ((), ()))
TN = (((0,), (0,)), ((), ()))


def params(**kw):
    return pltpu.CompilerParams(vmem_limit_bytes=20 << 20, **kw)


def cost(flops, bytes_accessed):
    return pl.CostEstimate(flops=flops, bytes_accessed=bytes_accessed, transcendentals=0)


def dot(a, b, dims):
    return lax.dot_general(a, b, dims, preferred_element_type=F32)


def index_kernel(row_hbm, col_hbm, want_ref, plan_ref, row_buf, col_buf, sems):
    copies = [
        pltpu.make_async_copy(row_hbm, row_buf, sems.at[0]),
        pltpu.make_async_copy(col_hbm, col_buf, sems.at[1]),
    ]
    for c in copies:
        c.start()
    for c in copies:
        c.wait()
    peers = want_ref.shape[0]
    blocks = 32
    col = col_buf[...]
    row = row_buf[...]
    peer, block = col >> 5, col & 31
    tiles = col.shape[1]
    of_peer = (lax.broadcasted_iota(I32, (peers, tiles), 0) == peer).astype(F32)
    of_block = (lax.broadcasted_iota(I32, (blocks, tiles), 0) == block).astype(F32)
    counts = dot(of_peer.astype(BF16), of_block.astype(BF16), NT)
    present = (counts > 0.5).astype(F32)
    before = (
        lax.broadcasted_iota(I32, (blocks, blocks), 0)
        < lax.broadcasted_iota(I32, (blocks, blocks), 1)
    ).astype(F32)
    rank = dot(present.astype(BF16), before.astype(BF16), NN)
    number = lax.broadcasted_iota(I32, (peers, blocks), 1).astype(F32)
    lane = lax.broadcasted_iota(I32, (peers, 128), 1)
    want = jnp.zeros((peers, 128), F32)
    for s in range(SLOTS):
        chosen = jnp.sum(
            jnp.where(rank == float(s), present * number, 0.0), axis=1, keepdims=True
        )
        want = jnp.where(lane == s, chosen, want)
    want_ref[...] = want.astype(I32).reshape(peers, 1, 128)
    rank_of = dot(rank.astype(BF16), of_peer.astype(BF16), TN)
    tile_rank = jnp.sum(rank_of * of_block, axis=0, keepdims=True)
    own = (peer == (row >> 5)).astype(F32)
    block_f, peer_f = block.astype(F32), peer.astype(F32)
    earlier = (
        lax.broadcasted_iota(I32, (tiles, tiles), 0) < lax.broadcasted_iota(I32, (tiles, tiles), 1)
    ).astype(F32)
    both = jnp.concatenate([own, 1.0 - own, jnp.zeros((6, tiles), F32)], axis=0)
    ahead = dot(both.astype(BF16), earlier.astype(BF16), NN)
    own_count = jnp.sum(own, axis=1, keepdims=True)
    spot = jnp.where(own > 0.5, ahead[0:1], own_count + ahead[1:2])
    moved = (lax.broadcasted_iota(I32, (tiles, tiles), 0).astype(F32) == spot).astype(F32)
    tile_f = lax.broadcasted_iota(I32, (1, tiles), 1).astype(F32)
    values = jnp.concatenate(
        [
            tile_f,
            jnp.where(own > 0.5, float(peers), peer_f),
            jnp.where(own > 0.5, block_f, tile_rank),
            (row & 31).astype(F32),
            jnp.zeros((4, tiles), F32),
        ],
        axis=0,
    )
    ordered = dot(values.astype(BF16), moved.astype(BF16), NT)
    place = ordered[1:2] * float(SLOTS) + ordered[2:3]
    plan = jnp.concatenate(
        [
            ordered[0:1],
            place,
            ordered[3:4],
            jnp.broadcast_to(own_count, (1, tiles)),
            jnp.zeros((4, tiles), F32),
        ],
        axis=0,
    )
    plan_ref[...] = plan.astype(I32)


def pick_lanes(blocked, pick, high):
    width = 16
    spread = dot(blocked, pick, NN)
    total = jnp.zeros((width, pick.shape[1]), F32)
    for s in range(blocked.shape[0] // width):
        total = total + jnp.where(high == s, spread[s * width : (s + 1) * width], 0.0)
    return total.astype(BF16)


def permute_kernel(features_ref, order_ref, out_ref, blocked):
    count = order_ref.shape[0]
    width = features_ref.shape[0]
    for s in range(count):
        blocked[s * width : (s + 1) * width, :] = features_ref[:, s * 128 : (s + 1) * 128]
    low = lax.broadcasted_iota(I32, (128, 256), 0)
    for j in range(0, count, 2):
        o = jnp.concatenate([order_ref[j : j + 1, :], order_ref[j + 1 : j + 2, :]], axis=1)
        o = o & (count * 128 - 1)
        pick = jnp.where(low == (o & 127), 1.0, 0.0).astype(BF16)
        total = pick_lanes(blocked[...], pick, o >> 7)
        out_ref[j] = total[:, :128]
        out_ref[j + 1] = total[:, 128:]


def pack_kernel(asked_ref, blocks_ref, send_ref):
    for p in range(send_ref.shape[0]):
        for s in range(SLOTS):
            send_ref[p, s] = blocks_ref[asked_ref[p, 0, s]]


def add_products(plan_ref, first, last, left, tiles_ref, dims, into, spare, prod, total):
    def step(i, carry):
        for u in range(STEP):
            k = i * STEP + u
            prod[u] = dot(left(k), tiles_ref[plan_ref[0, k]], dims)
        for u in range(STEP):
            k = i * STEP + u
            at = jnp.where((k >= first) & (k < last), into(k), spare)
            total[at] = total[at] + prod[u]
        return carry

    lax.fori_loop(first // STEP, (last + STEP - 1) // STEP, step, 0)


def forward_own_kernel(base, plan_ref, own_ref, tiles_ref, out_ref, prod, total):
    count = own_ref.shape[0]
    total[...] = jnp.zeros_like(total)
    add_products(
        plan_ref,
        0,
        plan_ref[3, 0],
        lambda k: own_ref[jnp.maximum(plan_ref[1, k] - base, 0)],
        tiles_ref,
        NT,
        lambda k: plan_ref[2, k],
        count,
        prod,
        total,
    )
    out_ref[...] = total[:count]


def forward_kernel(plan_ref, got_ref, part_ref, grad_ref, tiles_ref, out_ref, prod, total):
    groups = out_ref.shape[0]
    per = out_ref.shape[1] // 2
    count = part_ref.shape[0]
    slots = got_ref.shape[0]
    total[:count] = part_ref[...]
    add_products(
        plan_ref,
        plan_ref[3, 0],
        tiles_ref.shape[0],
        lambda k: got_ref[jnp.minimum(plan_ref[1, k], slots - 1)],
        tiles_ref,
        NT,
        lambda k: plan_ref[2, k],
        count,
        prod,
        total,
    )
    for c in range(groups):
        for b in range(per):
            at = (c * per + b) * 128
            out_ref[c, b] = total[c * per + b].astype(BF16)
            out_ref[c, per + b] = grad_ref[:, at : at + 128]


def dense_kernel(weight_ref, got_ref, out_ref):
    groups, _, width, _ = got_ref.shape
    per = got_ref.shape[1] // 2
    inputs = groups * width
    weight = weight_ref[...]
    weight_t = weight.astype(F32).T.astype(BF16)
    part = jnp.zeros((inputs, inputs), F32)
    for b in range(per):
        agg = got_ref[:, b].reshape(inputs, 128)
        grad = got_ref[:, per + b].reshape(inputs, 128).astype(F32)
        pre = dot(weight_t, agg, NN)
        logistic = jax.nn.sigmoid(pre)
        act = (pre * logistic).astype(BF16)
        pre_grad = (grad * logistic * (1.0 + pre * (1.0 - logistic))).astype(BF16)
        agg_grad = dot(weight, pre_grad, NN).astype(BF16)
        part = part + dot(pre_grad, agg, NT)
        out_ref[:, b] = agg_grad.reshape(groups, width, 128)
        out_ref[:, per + b] = act.reshape(groups, width, 128)
    high = part.astype(BF16)
    out_ref[:, 2 * per] = high.reshape(groups, width, 128)
    out_ref[:, 2 * per + 1] = (part - high.astype(F32)).astype(BF16).reshape(groups, width, 128)


def backward_kernel(plan_ref, got_ref, tiles_ref, send_ref, prod, total):
    groups = got_ref.shape[0]
    per = (got_ref.shape[1] - 2) // 2
    peers = send_ref.shape[0]
    slots = peers * SLOTS
    total[...] = jnp.zeros_like(total)
    add_products(
        plan_ref,
        plan_ref[3, 0],
        tiles_ref.shape[0],
        lambda k: got_ref[plan_ref[2, k] // per, plan_ref[2, k] % per],
        tiles_ref,
        NN,
        lambda k: jnp.minimum(plan_ref[1, k], slots),
        slots,
        prod,
        total,
    )
    part = got_ref[0, 2 * per].astype(F32) + got_ref[0, 2 * per + 1].astype(F32)
    for c in range(1, groups):
        part = part + got_ref[c, 2 * per].astype(F32) + got_ref[c, 2 * per + 1].astype(F32)
    part = part.astype(BF16)
    for p in range(peers):
        send_ref[p, :SLOTS] = total[p * SLOTS : (p + 1) * SLOTS].astype(BF16)
        send_ref[p, SLOTS] = part


def backward_own_kernel(base, plan_ref, got_ref, tiles_ref, order_ref, out_ref, act_ref, inverse_ref, pick_ref, prod, total, spots):
    count, width = out_ref.shape[:2]
    groups = got_ref.shape[0]
    per = (got_ref.shape[1] - 2) // 2
    total[...] = jnp.zeros_like(total)
    add_products(
        plan_ref,
        0,
        plan_ref[3, 0],
        lambda k: got_ref[plan_ref[2, k] // per, plan_ref[2, k] % per],
        tiles_ref,
        NN,
        lambda k: jnp.maximum(plan_ref[1, k] - base, 0),
        count,
        prod,
        total,
    )
    out_ref[...] = total[:count]
    for c in range(groups):
        for b in range(per):
            at = (c * per + b) * 128
            act_ref[:, at : at + 128] = got_ref[c, per + b]
    low = lax.broadcasted_iota(I32, (128, 128), 0)
    source = lax.broadcasted_iota(I32, (count, 128), 0)
    lane = lax.broadcasted_iota(I32, (count, 128), 1).astype(F32)
    for j in range(count):
        o = order_ref[j : j + 1, :] & (count * 128 - 1)
        lanes = slice(j * 128, (j + 1) * 128)
        pick_ref[:, lanes] = jnp.where(low == (o & 127), 1.0, 0.0).astype(BF16)
        here = source == (o >> 7)
        spots[:count, lanes] = jnp.where(here, float(j), 0.0).astype(BF16)
        spots[count:, lanes] = jnp.where(here, lane, 0.0).astype(BF16)
    inverse = dot(spots[...], pick_ref[...], NT).astype(I32)
    inverse_ref[...] = inverse[:count]
    for j in range(count):
        pick_ref[:, j * 128 : (j + 1) * 128] = jnp.where(
            low == inverse[count + j : count + j + 1, :], 1.0, 0.0
        ).astype(BF16)


def final_kernel(scale, asked_ref, got_ref, own_ref, inverse_ref, pick_ref, grads_ref, weight_ref, *totals):
    peers = got_ref.shape[0]
    count, width = own_ref.shape[:2]
    ways = len(totals)
    for w, total in enumerate(totals):
        total[...] = own_ref[...] if w == 0 else jnp.zeros_like(total)
    part = got_ref[0, SLOTS].astype(F32)
    for p in range(1, peers):
        part = part + got_ref[p, SLOTS].astype(F32)
    weight_ref[...] = part * scale
    for p in range(0, peers, ways):
        for s in range(SLOTS):
            for w, total in enumerate(totals):
                at = asked_ref[p + w, 0, s]
                total[at] = total[at] + got_ref[p + w, s].astype(F32)
    node = totals[0][...]
    for total in totals[1:]:
        node = node + total[...]
    blocked = node.astype(BF16).reshape(count * width, 128)
    for j in range(0, count, 2):
        high = jnp.concatenate([inverse_ref[j : j + 1, :], inverse_ref[j + 1 : j + 2, :]], axis=1)
        lanes = slice(j * 128, (j + 2) * 128)
        grads_ref[:, lanes] = pick_lanes(blocked, pick_ref[:, lanes], high)


def shards(features, node_order, tile_row, tile_col, tile_vals, weight, grad_out):
    width, span = features.shape
    tiles, size, _ = tile_vals.shape
    count = span // size
    peers = lax.axis_size("rows")
    groups = lax.axis_size("cols")
    per = count // groups
    order = node_order.reshape(count, size)
    shape = jax.ShapeDtypeStruct
    prod = pltpu.VMEM((STEP, width, size), F32)
    sums = lambda n: pltpu.VMEM((n + 1, width, size), F32)

    with jax.named_scope("index"):
        want, plan = pl.pallas_call(
            index_kernel,
            out_shape=(shape((peers, 1, 128), I32), shape((8, tiles), I32)),
            in_specs=[pl.BlockSpec(memory_space=pltpu.HBM)] * 2,
            out_specs=(VMEM, VMEM),
            scratch_shapes=[
                pltpu.VMEM((1, tiles), I32),
                pltpu.VMEM((1, tiles), I32),
                pltpu.SemaphoreType.DMA((2,)),
            ],
            compiler_params=params(),
        )(tile_row.reshape(1, tiles), tile_col.reshape(1, tiles))
        asked = lax.all_to_all(want, "rows", 0, 0, tiled=True)

    with jax.named_scope("permute"):
        own = pl.pallas_call(
            permute_kernel,
            out_shape=shape((count, width, size), BF16),
            in_specs=[VMEM, VMEM],
            out_specs=VMEM,
            scratch_shapes=[pltpu.VMEM((count * width, size), BF16)],
            compiler_params=params(),
            cost_estimate=cost(1 << 31, 1 << 22),
        )(features, order)

    with jax.named_scope("pack"):
        send = pl.pallas_call(
            pack_kernel,
            out_shape=shape((peers, SLOTS, width, size), BF16),
            in_specs=[SMEM, VMEM],
            out_specs=VMEM,
            compiler_params=params(),
        )(asked, own)
        got = lax.all_to_all(send, "rows", 0, 0, tiled=True)

    with jax.named_scope("forward_own"):
        part = pl.pallas_call(
            functools.partial(forward_own_kernel, peers * SLOTS),
            out_shape=shape((count, width, size), F32),
            in_specs=[SMEM, VMEM, VMEM],
            out_specs=VMEM,
            scratch_shapes=[prod, sums(count)],
            compiler_params=params(),
            cost_estimate=cost(1 << 31, 1 << 22),
        )(plan, own, tile_vals)

    with jax.named_scope("forward"):
        mixed = pl.pallas_call(
            forward_kernel,
            out_shape=shape((groups, 2 * per, width, size), BF16),
            in_specs=[SMEM, VMEM, VMEM, VMEM, VMEM],
            out_specs=VMEM,
            scratch_shapes=[prod, sums(count)],
            compiler_params=params(),
            cost_estimate=cost(1 << 30, 1 << 22),
        )(plan, got.reshape(peers * SLOTS, width, size), part, grad_out, tile_vals)
        mixed = lax.all_to_all(mixed, "cols", 0, 0, tiled=True)

    with jax.named_scope("dense"):
        back = pl.pallas_call(
            dense_kernel,
            out_shape=shape((groups, 2 * per + 2, width, size), BF16),
            in_specs=[VMEM, VMEM],
            out_specs=VMEM,
            compiler_params=params(),
        )(weight, mixed)
        back = lax.all_to_all(back, "cols", 0, 0, tiled=True)

    with jax.named_scope("backward"):
        parts = pl.pallas_call(
            backward_kernel,
            out_shape=shape((peers, SLOTS + 1, width, size), BF16),
            in_specs=[SMEM, VMEM, VMEM],
            out_specs=VMEM,
            scratch_shapes=[prod, sums(peers * SLOTS)],
            compiler_params=params(),
            cost_estimate=cost(1 << 30, 1 << 22),
        )(plan, back, tile_vals)
        parts = lax.all_to_all(parts, "rows", 0, 0, tiled=True)

    with jax.named_scope("backward_own"):
        kept, activated, inverse, pick = pl.pallas_call(
            functools.partial(backward_own_kernel, peers * SLOTS),
            out_shape=(
                shape((count, width, size), F32),
                shape((width, span), BF16),
                shape((count, size), I32),
                shape((size, span), BF16),
            ),
            in_specs=[SMEM, VMEM, VMEM, VMEM],
            out_specs=(VMEM, VMEM, VMEM, VMEM),
            scratch_shapes=[prod, sums(count), pltpu.VMEM((2 * count, span), BF16)],
            compiler_params=params(),
            cost_estimate=cost(1 << 31, 1 << 22),
        )(plan, back, tile_vals, order)

    with jax.named_scope("final"):
        feat_grads, weight_grad = pl.pallas_call(
            functools.partial(final_kernel, float(peers * span) ** -0.5),
            out_shape=(shape((width, span), BF16), shape((width, size), F32)),
            in_specs=[SMEM, VMEM, VMEM, VMEM, VMEM],
            out_specs=(VMEM, VMEM),
            scratch_shapes=[pltpu.VMEM((count, width, size), F32)] * WAYS,
            compiler_params=params(),
        )(asked, parts, kept, inverse, pick)
    return activated, feat_grads, weight_grad.T


def solution(mesh):
    in_specs = (
        P("cols", "rows"),
        P("rows"),
        P("rows"),
        P("rows"),
        P("rows", None, None),
        P(),
        P("cols", "rows"),
    )
    out_specs = (P("cols", "rows"), P("cols", "rows"), P(None, "cols"))
    return jax.shard_map(shards, mesh=mesh, in_specs=in_specs, out_specs=out_specs, check_vma=False)
```

time: 132 us -> 128 us (0.970); the launches traced: 132 us -> 126 us
  blocking collectives: 91.4 us -> 22.4 us
  waiting for transfers between devices: 5.51 us -> 48.6 us
  starting transfers between devices: 11.6 us -> 24.4 us
  local copies, waits for them, and re-layouts: 5.79 us -> 9.49 us
  Pallas kernels: 16.9 us -> 20.2 us
    all_to_all x2 -> x0, blocking collectives: 69 us -> none  [the longest x1 38.9 us: shards(): parts = lax.all_to_all(parts, 'rows', 0, 0, tiled=True)]
    all_to_all x0 -> x2, waiting for transfers between devices: none -> 43.1 us  [the longest x1 22.9 us: shards(): parts = lax.all_to_all(parts, 'rows', 0, 0, tiled=True)]
    all_to_all x0 -> x2, starting transfers between devices: none -> 12.8 us  [the longest x1 7.75 us: shards(): parts = lax.all_to_all(parts, 'rows', 0, 0, tiled=True)]
    pallas_call x6 -> x8, Pallas kernels: 11.6 us -> 16.7 us  [the longest x1 3.65 us: shards(): pl.pallas_call(functools.partial(backward_own_kernel, peers * SLOTS), out...]
    unnamed x19 -> x22, local copies, waits for them, and re-layouts: 5.79 us -> 9.49 us
    pallas_call x1, Pallas kernels: 5.25 us -> 3.56 us  [shards(): pl.pallas_call(functools.partial(final_kernel, float(peers * span) ** (-0...]
  transfers between devices with their start and end apart: 1 -> 3, of which waited for: 1 -> 3; matrix products, arithmetic and copies ran while one was open for 0% -> 0% of each run, Pallas kernels for 1% -> 6%
where the time goes in v2:
time: 128 us; the launch traced here: 126 us
  waiting for transfers between devices  48.6 us (38%)
  starting transfers between devices  24.4 us (19%)
  blocking collectives  22.4 us (18%)
  Pallas kernels  20.2 us (16%)
  local copies, waits for them, and re-layouts  9.49 us (7%)
    all_to_all x1, waiting for transfers between devices, shards(): parts = lax.all_to_all(parts, 'rows', 0, 0, tiled=True)  22.9 us
    all_to_all x1, waiting for transfers between devices, shards(): got = lax.all_to_all(send, 'rows', 0, 0, tiled=True)  20.2 us
    all_to_all x1, blocking collectives, shards(): mixed = lax.all_to_all(mixed, 'cols', 0, 0, tiled=True)  11.8 us
    all_to_all x1, starting transfers between devices, shards(): asked = lax.all_to_all(want, 'rows', 0, 0, tiled=True)  11.6 us
    all_to_all x1, blocking collectives, shards(): back = lax.all_to_all(back, 'cols', 0, 0, tiled=True)  10.6 us
    unnamed x22, local copies, waits for them, and re-layouts  9.49 us
    all_to_all x1, starting transfers between devices, shards(): parts = lax.all_to_all(parts, 'rows', 0, 0, tiled=True)  7.75 us
    all_to_all x1, waiting for transfers between devices, shards(): asked = lax.all_to_all(want, 'rows', 0, 0, tiled=True)  5.51 us
  transfers between devices with their start and end apart: 3, of which 3 were waited for; matrix products, arithmetic and copies ran while one was open for 0% of the time, Pallas kernels for 6%

profile of v2, /device:TPU:2, one launch (start us, length us, event | category | flops | bytes accessed | tf_op | source)
XLA Modules:
  0.0 125.9 jit_solution(13653414582456677212)
XLA Ops:
  0.6 0.0 copy-start.9
  0.6 0.6 copy-done.9
  1.3 0.7 copy-done.10
  1.9 1.0 index.1
  2.9 11.6 %all-to-all-start = ((s32[32,1,128]{2,1,0:T(1,128)}), s32[32,1,128]{2,1,0:T(1,128)S(1)}, u32[]{:S(2)}, u32[]{:S(2)}) async-start(s32[32,1,128]{2,1,0:T(1,128)} %get-tuple-element.12), calls=%async_computation | async-start | bytes 32768 | tf_op jit(solution)/shard_map/index/all_to_all | solution.py:333
  14.6 0.0 copy-start.6
  14.6 0.9 copy-done.6
  15.5 0.7 copy-done.7
  16.2 1.4 %permute.1.blocks_ref.own_ref = bf16[32,16,128]{2,1,0:T(8,128)(2,1)S(1)} custom-call(bf16[16,4096]{1,0:T(8,128)(2,1)S(1)} %copy-done.6, s32[32,128]{1,0:T(8,128)S(1)} %bitcast.6), custom_call_target="tpu_custom_call" | custom-call | flops 2147483648 | bytes 4194304 | tf_op jit(solution)/shard_map/permute/pallas_call | solution.py:336
  17.6 5.5 %all-to-all-done.asked_ref = s32[32,1,128]{2,1,0:T(1,128)S(1)} async-done(((s32[32,1,128]{2,1,0:T(1,128)}), s32[32,1,128]{2,1,0:T(1,128)S(1)}, u32[]{:S(2)}, u32[]{:S(2)}) %all-to-all-start) | async-done | bytes 16416 | tf_op jit(solution)/shard_map/index/all_to_all | solution.py:333
  23.1 2.0 %pack.1 = bf16[32,8,16,128]{3,2,1,0:T(8,128)(2,1)} custom-call(s32[32,1,128]{2,1,0:T(1,128)S(1)} %all-to-all-done.asked_ref, bf16[32,16,128]{2,1,0:T(8,128)(2,1)S(1)} %permute.1.blocks_ref.own_ref), custom_call_target="tpu_custom_call" | custom-call | tf_op jit(solution)/shard_map/pack/pallas_call | solution.py:347
  25.1 5.0 %all-to-all-start.1 = ((bf16[32,8,16,128]{3,2,1,0:T(8,128)(2,1)}), bf16[32,8,16,128]{3,2,1,0:T(8,128)(2,1)S(1)}, u32[]{:S(2)}, u32[]{:S(2)}) async-start(bf16[32,8,16,128]{3,2,1,0:T(8,128)(2,1)} %pack.1), calls=%async_computation.1 | async-start | bytes 2097152 | tf_op jit(solution)/shard_map/pack/all_to_all | solution.py:354
  30.2 0.0 copy-start
  30.2 2.2 %copy-done = bf16[128,128,128]{2,1,0:T(8,128)(2,1)S(1)} copy-done((bf16[128,128,128]{2,1,0:T(8,128)(2,1)S(1)}, bf16[128,128,128]{2,1,0:T(8,128)(2,1)}, u32[]{:S(2)}) %copy-start) | copy-done | bytes 4194328
  32.3 2.6 %forward_own.1.part_ref = f32[32,16,128]{2,1,0:T(8,128)S(1)} custom-call(s32[8,128]{1,0:T(8,128)S(1)} %get-tuple-element.11.plan_ref, bf16[32,16,128]{2,1,0:T(8,128)(2,1)S(1)} %permute.1.blocks_ref.own_ref, bf16[128,128,128]{2,1,0:T(8,128)(2,1)S(1)} %copy-done), custom_call_target="tpu_custom_call" | custom-call | flops 2147483648 | bytes 4194304 | tf_op jit(solution)/shard_map/forward_own/pallas_call | solution.py:357
  34.9 20.2 %all-to-all-done.1 = bf16[32,8,16,128]{3,2,1,0:T(8,128)(2,1)S(1)} async-done(((bf16[32,8,16,128]{3,2,1,0:T(8,128)(2,1)}), bf16[32,8,16,128]{3,2,1,0:T(8,128)(2,1)S(1)}, u32[]{:S(2)}, u32[]{:S(2)}) %all-to-all-start.1) | async-done | bytes 1048608 | tf_op jit(solution)/shard_map/pack/all_to_all | solution.py:354
  55.2 0.0 copy-done.4
  55.2 2.2 %copy-done.1 = bf16[128,128,128]{2,1,0:T(8,128)(2,1)S(1)} copy-done((bf16[128,128,128]{2,1,0:T(8,128)(2,1)S(1)}, bf16[128,128,128]{2,1,0:T(8,128)(2,1)}, u32[]{:S(2)}) %copy-start.1) | copy-done | bytes 4194328
  57.4 2.2 %forward.1 = bf16[8,8,16,128]{3,2,1,0:T(8,128)(2,1)S(1)} custom-call(s32[8,128]{1,0:T(8,128)S(1)} %get-tuple-element.11.plan_ref, bf16[256,16,128]{2,1,0:T(8,128)(2,1)S(1)} %bitcast.5, f32[32,16,128]{2,1,0:T(8,128)S(1)} %forward_own.1.part_ref, bf16[16,4096]{1,0:T(8,128)(2,1)S(1)} %copy-done.4, bf16[128,128,128]{2,1,0:T(8,128)(2,1)S(1)} %copy-done.1), custom_call_target="tpu_custom_call" | custom-call | flops 1073741824 | bytes 4194304 | tf_op jit(solution)/shard_map/forward/pallas_call | solution.py:368
  59.6 11.8 %all_to_all.25.got_ref = bf16[8,8,16,128]{3,2,1,0:T(8,128)(2,1)S(1)} all-to-all(bf16[8,8,16,128]{3,2,1,0:T(8,128)(2,1)S(1)} %forward.1), channel_id=1, replica_groups=mesh['rows'=32,'cols'=8] {'cols'}, dimensions={0} | all-to-all | bytes 524288 | tf_op jit(solution)/shard_map/forward/all_to_all | solution.py:377
  71.4 0.0 copy-done.5
  71.4 0.7 dense.1
  72.2 10.6 %all_to_all.26.got_ref = bf16[8,10,16,128]{3,2,1,0:T(8,128)(2,1)S(1)} all-to-all(bf16[8,10,16,128]{3,2,1,0:T(8,128)(2,1)S(1)} %dense.1), channel_id=1, replica_groups=mesh['rows'=32,'cols'=8] {'cols'}, dimensions={0} | all-to-all | bytes 655360 | tf_op jit(solution)/shard_map/dense/all_to_all | solution.py:387
  82.8 0.0 copy-done.2
  82.8 3.1 %backward.1 = bf16[32,9,16,128]{3,2,1,0:T(8,128)(2,1)} custom-call(s32[8,128]{1,0:T(8,128)S(1)} %get-tuple-element.11.plan_ref, bf16[8,10,16,128]{3,2,1,0:T(8,128)(2,1)S(1)} %all_to_all.26.got_ref, bf16[128,128,128]{2,1,0:T(8,128)(2,1)S(1)} %copy-done.2), custom_call_target="tpu_custom_call" | custom-call | flops 1073741824 | bytes 4194304 | tf_op jit(solution)/shard_map/backward/pallas_call | solution.py:390
  85.9 7.8 %all-to-all-start.4 = ((bf16[32,9,16,128]{3,2,1,0:T(8,128)(2,1)}), bf16[32,9,16,128]{3,2,1,0:T(8,128)(2,1)S(1)}, u32[]{:S(2)}, u32[]{:S(2)}) async-start(bf16[32,9,16,128]{3,2,1,0:T(8,128)(2,1)} %backward.1), calls=%async_computation.4 | async-start | bytes 2359296 | tf_op jit(solution)/shard_map/backward/all_to_all | solution.py:399
  93.6 0.0 copy-done.8
  93.6 0.0 copy-start.3
  93.6 2.2 %copy-done.3 = bf16[128,128,128]{2,1,0:T(8,128)(2,1)S(1)} copy-done((bf16[128,128,128]{2,1,0:T(8,128)(2,1)S(1)}, bf16[128,128,128]{2,1,0:T(8,128)(2,1)}, u32[]{:S(2)}) %copy-start.3) | copy-done | bytes 4194328
  95.8 3.7 %backward_own.1 = (f32[32,16,128]{2,1,0:T(8,128)S(1)}, bf16[16,4096]{1,0:T(8,128)(2,1)}, s32[32,128]{1,0:T(8,128)S(1)}, bf16[128,4096]{1,0:T(8,128)(2,1)S(1)}) custom-call(s32[8,128]{1,0:T(8,128)S(1)} %get-tuple-element.11.plan_ref, bf16[8,10,16,128]{3,2,1,0:T(8,128)(2,1)S(1)} %all_to_all.26.got_ref, bf16[128,128,128]{2,1,0:T(8,128)(2,1)S(1)} %copy-done.3, ...), custom_call_target="tpu_custom_call" | custom-call | flops 2147483648 | bytes 4194304 | tf_op jit(solution)/shard_map/backward_own/pallas_call | solution.py:402
  99.5 22.9 %all-to-all-done.4.got_ref = bf16[32,9,16,128]{3,2,1,0:T(8,128)(2,1)S(1)} async-done(((bf16[32,9,16,128]{3,2,1,0:T(8,128)(2,1)}), bf16[32,9,16,128]{3,2,1,0:T(8,128)(2,1)S(1)}, u32[]{:S(2)}, u32[]{:S(2)}) %all-to-all-start.4) | async-done | bytes 1179680 | tf_op jit(solution)/shard_map/backward/all_to_all | solution.py:399
  122.3 3.6 %final.1 = (bf16[16,4096]{1,0:T(8,128)(2,1)}, f32[16,128]{1,0:T(8,128)}) custom-call(s32[32,1,128]{2,1,0:T(1,128)S(1)} %all-to-all-done.asked_ref, bf16[32,9,16,128]{3,2,1,0:T(8,128)(2,1)S(1)} %all-to-all-done.4.got_ref, f32[32,16,128]{2,1,0:T(8,128)S(1)} %get-tuple-element.14.own_ref, s32[32,128]{1,0:T(8,128)S(1)} %get-tuple-element.15.inverse_ref, ...), custom_call_target="tpu_custom_call" | custom-call | tf_op jit(solution)/shard_map/final/pallas_call | solution.py:418
  (7 shorter events, 0.0 us)
Async XLA Ops:
  0.6 0.7 copy-start.9
  1.3 0.7 copy-start.10
  2.9 20.2 %all-to-all-start = ((s32[32,1,128]{2,1,0:T(1,128)}), s32[32,1,128]{2,1,0:T(1,128)S(1)}, u32[]{:S(2)}, u32[]{:S(2)}) async-start(s32[32,1,128]{2,1,0:T(1,128)} %get-tuple-element.12), calls=%async_computation | async-start | bytes 32768 | tf_op jit(solution)/shard_map/index/all_to_all | solution.py:333
  14.6 0.9 copy-start.6
  15.5 0.7 copy-start.7
  25.1 30.1 %all-to-all-start.1 = ((bf16[32,8,16,128]{3,2,1,0:T(8,128)(2,1)}), bf16[32,8,16,128]{3,2,1,0:T(8,128)(2,1)S(1)}, u32[]{:S(2)}, u32[]{:S(2)}) async-start(bf16[32,8,16,128]{3,2,1,0:T(8,128)(2,1)} %pack.1), calls=%async_computation.1 | async-start | bytes 2097152 | tf_op jit(solution)/shard_map/pack/all_to_all | solution.py:354
  30.2 2.2 %copy-start = (bf16[128,128,128]{2,1,0:T(8,128)(2,1)S(1)}, bf16[128,128,128]{2,1,0:T(8,128)(2,1)}, u32[]{:S(2)}) copy-start(bf16[128,128,128]{2,1,0:T(8,128)(2,1)} %tiles_ref.7) | copy-start | bytes 12582916
  32.3 22.8 %copy-start.4 = (bf16[16,4096]{1,0:T(8,128)(2,1)S(1)}, bf16[16,4096]{1,0:T(8,128)(2,1)}, u32[]{:S(2)}) copy-start(bf16[16,4096]{1,0:T(8,128)(2,1)} %grad_ref.1) | copy-start | bytes 393220
  55.2 2.2 %copy-start.1 = (bf16[128,128,128]{2,1,0:T(8,128)(2,1)S(1)}, bf16[128,128,128]{2,1,0:T(8,128)(2,1)}, u32[]{:S(2)}) copy-start(bf16[128,128,128]{2,1,0:T(8,128)(2,1)} %tiles_ref.7) | copy-start | bytes 12582916
  57.4 14.0 %copy-start.5 = (bf16[128,128]{1,0:T(8,128)(2,1)S(1)}, bf16[128,128]{1,0:T(8,128)(2,1)}, u32[]{:S(2)}) copy-start(bf16[128,128]{1,0:T(8,128)(2,1)} %weight_ref.1) | copy-start | bytes 98308
  57.4 25.4 %copy-start.2 = (bf16[128,128,128]{2,1,0:T(8,128)(2,1)S(1)}, bf16[128,128,128]{2,1,0:T(8,128)(2,1)}, u32[]{:S(2)}) copy-start(bf16[128,128,128]{2,1,0:T(8,128)(2,1)} %tiles_ref.7) | copy-start | bytes 12582916
  85.8 7.8 %copy-start.8 = (s32[4096]{0:T(1024)S(1)}, s32[4096]{0:T(1024)}, u32[]{:S(2)}) copy-start(s32[4096]{0:T(1024)} %param.8) | copy-start | bytes 49156
  85.9 36.5 %all-to-all-start.4 = ((bf16[32,9,16,128]{3,2,1,0:T(8,128)(2,1)}), bf16[32,9,16,128]{3,2,1,0:T(8,128)(2,1)S(1)}, u32[]{:S(2)}, u32[]{:S(2)}) async-start(bf16[32,9,16,128]{3,2,1,0:T(8,128)(2,1)} %backward.1), calls=%async_computation.4 | async-start | bytes 2359296 | tf_op jit(solution)/shard_map/backward/all_to_all | solution.py:399
  93.6 2.2 %copy-start.3 = (bf16[128,128,128]{2,1,0:T(8,128)(2,1)S(1)}, bf16[128,128,128]{2,1,0:T(8,128)(2,1)}, u32[]{:S(2)}) copy-start(bf16[128,128,128]{2,1,0:T(8,128)(2,1)} %tiles_ref.7) | copy-start | bytes 12582916

commit v3 on v2

v3 whole, which is shorter than its diff:
```python
import functools

import jax
import jax.numpy as jnp
from jax import lax
from jax.experimental import pallas as pl
from jax.experimental.pallas import tpu as pltpu
from jax.sharding import PartitionSpec as P

BF16 = jnp.bfloat16
F32 = jnp.float32
I32 = jnp.int32
SLOTS = 8
STEP = 16
WAYS = 4
PIECES = 8
VMEM = pl.BlockSpec(memory_space=pltpu.VMEM)
HBM = pl.BlockSpec(memory_space=pltpu.HBM)
SMEM = pl.BlockSpec(memory_space=pltpu.SMEM)
NN = (((1,), (0,)), ((), ()))
NT = (((1,), (1,)), ((), ()))
TN = (((0,), (0,)), ((), ()))


def params(**kw):
    return pltpu.CompilerParams(vmem_limit_bytes=20 << 20, **kw)


def cost(flops, bytes_accessed):
    return pl.CostEstimate(flops=flops, bytes_accessed=bytes_accessed, transcendentals=0)


def send_out(buf, out_hbm, sems, piece):
    size = buf.shape[0] // sems.shape[0]
    at = pl.ds(piece * size, size)
    return pltpu.make_async_copy(buf.at[at], out_hbm.at[at], sems.at[piece])


def over_cols(value, here):
    groups = value.shape[0]
    rings = groups // 2
    value = value.reshape(rings, 2, *value.shape[1:])
    core, ring = here % 2, here // 2
    kept = lax.dynamic_index_in_dim(value, core, 1, keepdims=False)
    passed = lax.dynamic_index_in_dim(value, 1 - core, 1, keepdims=False)
    passed = lax.ppermute(passed, "cols", [(i, i ^ 1) for i in range(groups)])
    both = jnp.stack([kept, passed], axis=1)
    parts = []
    for far in range(rings):
        part = lax.dynamic_index_in_dim(both, (ring + far) % rings, 0, keepdims=False)
        if far:
            pairs = [(i, (i + 2 * far) % groups) for i in range(groups)]
            part = lax.ppermute(part, "cols", pairs)
        parts.append(part)
    return jnp.stack(parts)


def in_hbm(x):
    return pltpu.with_memory_space_constraint(x, pltpu.HBM)


def dot(a, b, dims):
    return lax.dot_general(a, b, dims, preferred_element_type=F32)


def ranks(col, peers):
    peer, block = col >> 5, col & 31
    of_peer = (lax.broadcasted_iota(I32, (peers, col.shape[1]), 0) == peer).astype(F32)
    of_block = (lax.broadcasted_iota(I32, (32, col.shape[1]), 0) == block).astype(F32)
    counts = dot(of_peer.astype(BF16), of_block.astype(BF16), NT)
    present = (counts > 0.5).astype(F32)
    before = lower(32).astype(F32)
    return of_peer, of_block, present, dot(present.astype(BF16), before.astype(BF16), NN)


def lower(n):
    return lax.broadcasted_iota(I32, (n, n), 0) < lax.broadcasted_iota(I32, (n, n), 1)


def want_kernel(col_hbm, want_ref, col_buf, sem):
    copy = pltpu.make_async_copy(col_hbm, col_buf, sem)
    copy.start()
    copy.wait()
    peers = want_ref.shape[0]
    _, _, present, rank = ranks(col_buf[...], peers)
    number = lax.broadcasted_iota(I32, (peers, 32), 1).astype(F32)
    lane = lax.broadcasted_iota(I32, (peers, 128), 1)
    want = jnp.zeros((peers, 128), F32)
    for s in range(SLOTS):
        chosen = jnp.sum(
            jnp.where(rank == float(s), present * number, 0.0), axis=1, keepdims=True
        )
        want = jnp.where(lane == s, chosen, want)
    want_ref[...] = want.astype(I32).reshape(peers, 1, 128)


def plan_kernel(peers, row_ref, col_ref, plan_ref):
    col, row = col_ref[...], row_ref[...]
    tiles = col.shape[1]
    of_peer, of_block, _, rank = ranks(col, peers)
    rank_of = dot(rank.astype(BF16), of_peer.astype(BF16), TN)
    tile_rank = jnp.sum(rank_of * of_block, axis=0, keepdims=True)
    own = ((col >> 5) == (row >> 5)).astype(F32)
    own_count = jnp.sum(own, axis=1, keepdims=True)
    earlier = lower(tiles).astype(F32).astype(BF16)
    far_peer = of_peer * (1.0 - own)
    same = dot(far_peer.astype(BF16), earlier, NN)
    totals = jnp.sum(far_peer, axis=1, keepdims=True)
    upper = (
        lax.broadcasted_iota(I32, (peers, peers), 0) > lax.broadcasted_iota(I32, (peers, peers), 1)
    ).astype(F32)
    wide = jnp.broadcast_to(totals, (peers, tiles))
    starts = dot(upper.astype(BF16), wide.astype(BF16), NN)
    ahead = jnp.sum(far_peer * (same + starts), axis=0, keepdims=True)
    own_ahead = dot(jnp.broadcast_to(own, (8, tiles)).astype(BF16), earlier, NN)[0:1]
    spot = jnp.where(own > 0.5, own_ahead, own_count + ahead)
    moved = (lax.broadcasted_iota(I32, (tiles, tiles), 0).astype(F32) == spot).astype(F32)
    values = jnp.concatenate(
        [
            lax.broadcasted_iota(I32, (1, tiles), 1).astype(F32),
            jnp.where(own > 0.5, float(peers), (col >> 5).astype(F32)),
            jnp.where(own > 0.5, (col & 31).astype(F32), tile_rank),
            (row & 31).astype(F32),
            jnp.zeros((4, tiles), F32),
        ],
        axis=0,
    )
    ordered = dot(values.astype(BF16), moved.astype(BF16), NT)
    lanes = lax.broadcasted_iota(I32, (peers, tiles), 1)
    diagonal = (lanes == lax.broadcasted_iota(I32, (peers, tiles), 0)).astype(F32)
    firsts = own_count + jnp.sum(starts * diagonal, axis=0, keepdims=True)
    plan = jnp.concatenate(
        [
            ordered[0:1],
            ordered[1:2] * float(SLOTS) + ordered[2:3],
            ordered[3:4],
            jnp.broadcast_to(own_count, (1, tiles)),
            firsts,
            jnp.zeros((3, tiles), F32),
        ],
        axis=0,
    )
    plan_ref[...] = plan.astype(I32)


def pick_lanes(blocked, pick, high):
    width = 16
    spread = dot(blocked, pick, NN)
    total = jnp.zeros((width, pick.shape[1]), F32)
    for s in range(blocked.shape[0] // width):
        total = total + jnp.where(high == s, spread[s * width : (s + 1) * width], 0.0)
    return total.astype(BF16)


def permute_kernel(features_ref, order_ref, out_ref, blocked):
    count = order_ref.shape[0]
    width = features_ref.shape[0]
    for s in range(count):
        blocked[s * width : (s + 1) * width, :] = features_ref[:, s * 128 : (s + 1) * 128]
    low = lax.broadcasted_iota(I32, (128, 256), 0)
    for j in range(0, count, 2):
        o = jnp.concatenate([order_ref[j : j + 1, :], order_ref[j + 1 : j + 2, :]], axis=1)
        o = o & (count * 128 - 1)
        pick = jnp.where(low == (o & 127), 1.0, 0.0).astype(BF16)
        total = pick_lanes(blocked[...], pick, o >> 7)
        out_ref[j] = total[:, :128]
        out_ref[j + 1] = total[:, 128:]


def pack_kernel(asked_ref, blocks_ref, buf):
    for p in range(buf.shape[0]):
        for s in range(SLOTS):
            buf[p, s] = blocks_ref[asked_ref[p, 0, s]]


def chunk_copy(tiles_hbm, tiles, sems, i):
    at = pl.ds(i * STEP, STEP)
    return pltpu.make_async_copy(tiles_hbm.at[at], tiles.at[at], sems.at[i])


def fetch_tiles(first, last, tiles_hbm, tiles, sems):
    def start(i, carry):
        chunk_copy(tiles_hbm, tiles, sems, i).start()
        return carry

    lax.fori_loop(first, last, start, 0)


def add_products(plan_ref, first, last, left, tile, dims, into, spare, prod, total, arrive=None):
    def step(i, carry):
        if arrive is not None:
            arrive(i)
        for u in range(STEP):
            k = i * STEP + u
            prod[u] = dot(left(k), tile(k), dims)
        for u in range(STEP):
            k = i * STEP + u
            at = jnp.where((k >= first) & (k < last), into(k), spare)
            total[at] = total[at] + prod[u]
        return carry

    lax.fori_loop(first // STEP, (last + STEP - 1) // STEP, step, 0)


def forward_own_kernel(base, plan_ref, own_ref, tiles_hbm, out_ref, list_hbm, prod, total, tiles, sem, out_sem):
    count = own_ref.shape[0]
    for k in range(tiles.shape[0]):
        pltpu.make_async_copy(tiles_hbm.at[plan_ref[0, k]], tiles.at[k], sem).start()
    pltpu.make_async_copy(tiles_hbm, tiles, sem).wait()
    store = pltpu.make_async_copy(tiles, list_hbm, out_sem)
    store.start()
    total[...] = jnp.zeros_like(total)
    add_products(
        plan_ref,
        0,
        plan_ref[3, 0],
        lambda k: own_ref[jnp.maximum(plan_ref[1, k] - base, 0)],
        lambda k: tiles[k],
        NT,
        lambda k: plan_ref[2, k],
        count,
        prod,
        total,
    )
    out_ref[...] = total[:count]
    store.wait()


def forward_kernel(plan_ref, got_ref, part_ref, tiles_hbm, out_ref, prod, total, tiles, sems):
    first = plan_ref[3, 0]

    fetch_tiles(first // STEP, tiles.shape[0] // STEP, tiles_hbm, tiles, sems)
    groups, per = out_ref.shape[:2]
    count = part_ref.shape[0]
    slots = got_ref.shape[0]
    total[:count] = part_ref[...]
    add_products(
        plan_ref,
        first,
        tiles.shape[0],
        lambda k: got_ref[jnp.minimum(plan_ref[1, k], slots - 1)],
        lambda k: tiles[k],
        NT,
        lambda k: plan_ref[2, k],
        count,
        prod,
        total,
        lambda i: chunk_copy(tiles_hbm, tiles, sems, i).wait(),
    )
    for c in range(groups):
        for b in range(per):
            out_ref[c, b] = total[c * per + b].astype(BF16)


def source(here, far, core):
    rings = 4
    y, c = here // 2, here % 2
    return (y + rings - far) % rings * 2 + (c + core) % 2


def dense_kernel(here_ref, weight_ref, got_ref, grad_ref, out_ref, act_hbm, grads, act_ref, sems):
    groups, per, width, _ = got_ref.shape
    for far in range(groups // 2):
        for core in range(2):
            grads[source(here_ref[0], far, core)] = grad_ref[far, core]
    inputs = groups * width
    weight = weight_ref[...]
    weight_t = weight.astype(F32).T.astype(BF16)
    part = jnp.zeros((inputs, inputs), F32)
    stores = []
    for b in range(per):
        agg = got_ref[:, b].reshape(inputs, 128)
        grad = grads[:, b].reshape(inputs, 128).astype(F32)
        pre = dot(weight_t, agg, NN)
        logistic = jax.nn.sigmoid(pre)
        act = (pre * logistic).astype(BF16)
        pre_grad = (grad * logistic * (1.0 + pre * (1.0 - logistic))).astype(BF16)
        agg_grad = dot(weight, pre_grad, NN).astype(BF16)
        part = part + dot(pre_grad, agg, NT)
        out_ref[:, b] = agg_grad.reshape(groups, width, 128)
        act_ref[:, b] = act.reshape(groups, width, 128)
        store = pltpu.make_async_copy(act_ref.at[:, b], act_hbm.at[:, b], sems.at[b])
        store.start()
        stores.append(store)
    high = part.astype(BF16)
    out_ref[:, per] = high.reshape(groups, width, 128)
    out_ref[:, per + 1] = (part - high.astype(F32)).astype(BF16).reshape(groups, width, 128)
    for store in stores:
        store.wait()


def backward_kernel(plan_ref, got_ref, tiles_hbm, send_hbm, prod, total, buf, sems, tiles, tile_sems):
    last = tiles.shape[0] // STEP
    begin = jnp.minimum(plan_ref[3, 0] // STEP, last - 1)

    fetch_tiles(begin, last, tiles_hbm, tiles, tile_sems)
    groups = got_ref.shape[0]
    per = got_ref.shape[1] - 2
    peers = buf.shape[0]
    pieces = sems.shape[0]
    share = peers // pieces
    slots = peers * SLOTS
    total[...] = jnp.zeros_like(total)
    part = got_ref[0, per].astype(F32) + got_ref[0, per + 1].astype(F32)
    for c in range(1, groups):
        part = part + got_ref[c, per].astype(F32) + got_ref[c, per + 1].astype(F32)
    part = part.astype(BF16)
    for p in range(peers):
        buf[p, SLOTS] = part

    def step(i, carry):
        chunk_copy(tiles_hbm, tiles, tile_sems, i).wait()
        for u in range(STEP):
            r = plan_ref[2, i * STEP + u]
            prod[u] = dot(got_ref[r // per, r % per], tiles[i * STEP + u], NN)
        for u in range(STEP):
            k = i * STEP + u
            at = jnp.where(k >= plan_ref[3, 0], jnp.minimum(plan_ref[1, k], slots), slots)
            total[at] = total[at] + prod[u]
        done = (i + 1) * STEP
        for piece in range(pieces):
            until = plan_ref[4, (piece + 1) * share] if piece + 1 < pieces else last * STEP

            @pl.when((until <= done) & ((until > i * STEP) | (i == begin)))
            def _():
                for p in range(piece * share, (piece + 1) * share):
                    buf[p, :SLOTS] = total[p * SLOTS : (p + 1) * SLOTS].astype(BF16)
                send_out(buf, send_hbm, sems, piece).start()

        return carry

    lax.fori_loop(begin, last, step, 0)
    for piece in range(pieces):
        send_out(buf, send_hbm, sems, piece).wait()


def backward_own_kernel(
    base, plan_ref, got_ref, tiles_hbm, order_ref, asked_ref, out_hbm, inverse_ref, pick_ref, flat_ref, prod, total, tiles, sems, spots, low_pick, out_sem
):
    fetch_tiles(0, (plan_ref[3, 0] + STEP - 1) // STEP, tiles_hbm, tiles, sems)
    count, width = out_hbm.shape[:2]
    per = got_ref.shape[1] - 2
    total[...] = jnp.zeros_like(total)
    add_products(
        plan_ref,
        0,
        plan_ref[3, 0],
        lambda k: got_ref[plan_ref[2, k] // per, plan_ref[2, k] % per],
        lambda k: tiles[k],
        NN,
        lambda k: jnp.maximum(plan_ref[1, k] - base, 0),
        count,
        prod,
        total,
        lambda i: chunk_copy(tiles_hbm, tiles, sems, i).wait(),
    )
    store = pltpu.make_async_copy(total.at[pl.ds(0, count)], out_hbm, out_sem)
    store.start()
    low = lax.broadcasted_iota(I32, (128, 128), 0)
    source = lax.broadcasted_iota(I32, (count, 128), 0)
    lane = lax.broadcasted_iota(I32, (count, 128), 1).astype(F32)
    for j in range(count):
        o = order_ref[j : j + 1, :] & (count * 128 - 1)
        lanes = slice(j * 128, (j + 1) * 128)
        low_pick[:, lanes] = jnp.where(low == (o & 127), 1.0, 0.0).astype(BF16)
        here = source == (o >> 7)
        spots[:count, lanes] = jnp.where(here, float(j), 0.0).astype(BF16)
        spots[count:, lanes] = jnp.where(here, lane, 0.0).astype(BF16)
    inverse = dot(spots[...], low_pick[...], NT).astype(I32)
    odd = lax.broadcasted_iota(I32, (256, 128), 0)
    for j in range(count):
        at = inverse[count + j : count + j + 1, :] + (inverse[j : j + 1, :] & 1) * 128
        pick_ref[:, j * 128 : (j + 1) * 128] = jnp.where(odd == at, 1.0, 0.0).astype(BF16)
    inverse_ref[...] = inverse[:count] >> 1
    peers = asked_ref.shape[0]
    spread = dot(
        asked_ref[...].reshape(peers, 128).astype(F32).astype(BF16),
        (
            lax.broadcasted_iota(I32, (128, 256), 0) == lax.broadcasted_iota(I32, (128, 256), 1) % SLOTS
        ).astype(F32).astype(BF16),
        NN,
    )
    mine = lax.broadcasted_iota(I32, (peers, 256), 0) == lax.broadcasted_iota(I32, (peers, 256), 1) // SLOTS
    flat_ref[...] = jnp.sum(jnp.where(mine, spread, 0.0), axis=0, keepdims=True).astype(I32)
    store.wait()


def blocks_kernel(grad_ref, out_ref):
    groups, per = out_ref.shape[:2]
    for c in range(groups):
        for b in range(per):
            at = (c * per + b) * 128
            out_ref[c, b] = grad_ref[:, at : at + 128]


def lanes_kernel(here_ref, got_ref, out_ref):
    for far in range(got_ref.shape[0]):
        for core in range(2):
            at = source(here_ref[0], far, core) * got_ref.shape[2]
            for b in range(got_ref.shape[2]):
                out_ref[:, pl.ds(pl.multiple_of((at + b) * 128, 128), 128)] = got_ref[far, core, b]


def final_kernel(scale, asked_ref, got_ref, own_hbm, inverse_ref, pick_ref, grads_ref, weight_ref, own, sem, *totals):
    fetch = pltpu.make_async_copy(own_hbm, own, sem)
    fetch.start()
    peers = got_ref.shape[0]
    count, width = own.shape[:2]
    ways = len(totals)
    for total in totals:
        total[...] = jnp.zeros_like(total)
    part = got_ref[0, SLOTS].astype(F32)
    for p in range(1, peers):
        part = part + got_ref[p, SLOTS].astype(F32)
    weight_ref[...] = part * scale
    for p in range(0, peers, ways):
        for s in range(SLOTS):
            for w, total in enumerate(totals):
                at = asked_ref[0, (p + w) * SLOTS + s]
                total[at] = total[at] + got_ref[p + w, s].astype(F32)
    fetch.wait()
    node = own[...]
    for total in totals:
        node = node + total[...]
    node = node.astype(BF16)
    blocked = jnp.concatenate(
        [jnp.concatenate([node[j], node[j + 1]], axis=1) for j in range(0, count, 2)], axis=0
    )
    for j in range(0, count, 2):
        high = jnp.concatenate([inverse_ref[j : j + 1, :], inverse_ref[j + 1 : j + 2, :]], axis=1)
        lanes = slice(j * 128, (j + 2) * 128)
        grads_ref[:, lanes] = pick_lanes(blocked, pick_ref[:, lanes], high)


def shards(features, node_order, tile_row, tile_col, tile_vals, weight, grad_out):
    width, span = features.shape
    tiles, size, _ = tile_vals.shape
    count = span // size
    peers = lax.axis_size("rows")
    groups = lax.axis_size("cols")
    per = count // groups
    order = node_order.reshape(count, size)
    shape = jax.ShapeDtypeStruct
    prod = pltpu.VMEM((STEP, width, size), F32)
    tile_buf = pltpu.VMEM(tile_vals.shape, BF16)
    sums = lambda n: pltpu.VMEM((n + 1, width, size), F32)

    with jax.named_scope("index"):
        rows, cols = tile_row.reshape(1, tiles), tile_col.reshape(1, tiles)
        want = pl.pallas_call(
            want_kernel,
            out_shape=shape((peers, 1, 128), I32),
            in_specs=[HBM],
            out_specs=VMEM,
            scratch_shapes=[pltpu.VMEM((1, tiles), I32), pltpu.SemaphoreType.DMA],
            compiler_params=params(),
        )(in_hbm(cols))
        asked = lax.all_to_all(want, "rows", 0, 0, tiled=True)
        plan = pl.pallas_call(
            functools.partial(plan_kernel, peers),
            out_shape=shape((8, tiles), I32),
            in_specs=[VMEM, VMEM],
            out_specs=VMEM,
            compiler_params=params(),
            cost_estimate=cost(1 << 30, 1 << 21),
        )(rows, cols)

    with jax.named_scope("permute"):
        own = pl.pallas_call(
            permute_kernel,
            out_shape=shape((count, width, size), BF16),
            in_specs=[VMEM, VMEM],
            out_specs=VMEM,
            scratch_shapes=[pltpu.VMEM((count * width, size), BF16)],
            compiler_params=params(),
            cost_estimate=cost(1 << 31, 1 << 22),
        )(features, order)

    with jax.named_scope("pack"):
        send = pl.pallas_call(
            pack_kernel,
            out_shape=pltpu.VMEM((peers, SLOTS, width, size), BF16),
            in_specs=[SMEM, VMEM],
            out_specs=VMEM,
            compiler_params=params(),
        )(asked, own)
        got = lax.all_to_all(send, "rows", 0, 0, tiled=True)

    with jax.named_scope("forward_own"):
        part, tile_list = pl.pallas_call(
            functools.partial(forward_own_kernel, peers * SLOTS),
            out_shape=(shape((count, width, size), F32), pltpu.HBM(tile_vals.shape, BF16)),
            in_specs=[SMEM, VMEM, HBM],
            out_specs=(VMEM, HBM),
            scratch_shapes=[prod, sums(count), tile_buf, pltpu.SemaphoreType.DMA, pltpu.SemaphoreType.DMA],
            compiler_params=params(),
            cost_estimate=cost(1 << 31, 1 << 22),
        )(plan, own, in_hbm(tile_vals))

    with jax.named_scope("grads"):
        here = lax.axis_index("cols")
        grad_out, part = lax.optimization_barrier((grad_out, part))
        grads = pl.pallas_call(
            blocks_kernel,
            out_shape=shape((groups, per, width, size), BF16),
            in_specs=[VMEM],
            out_specs=VMEM,
            compiler_params=params(),
        )(grad_out)
        grads, part = lax.optimization_barrier((over_cols(grads, here), part))
        here_at = here.reshape(1)

    with jax.named_scope("forward"):
        mixed = pl.pallas_call(
            forward_kernel,
            out_shape=shape((groups, per, width, size), BF16),
            in_specs=[SMEM, VMEM, VMEM, HBM],
            out_specs=VMEM,
            scratch_shapes=[prod, sums(count), tile_buf, pltpu.SemaphoreType.DMA((tiles // STEP,))],
            compiler_params=params(),
            cost_estimate=cost(1 << 30, 1 << 22),
        )(plan, got.reshape(peers * SLOTS, width, size), part, in_hbm(tile_list))
        mixed = lax.all_to_all(mixed, "cols", 0, 0, tiled=True)

    with jax.named_scope("dense"):
        back, act = pl.pallas_call(
            dense_kernel,
            out_shape=(
                shape((groups, per + 2, width, size), BF16),
                pltpu.HBM((groups, per, width, size), BF16),
            ),
            in_specs=[SMEM, VMEM, VMEM, VMEM],
            out_specs=(VMEM, HBM),
            scratch_shapes=[pltpu.VMEM((groups, per, width, size), BF16)] * 2
            + [pltpu.SemaphoreType.DMA((per,))],
            compiler_params=params(),
        )(here_at, weight, mixed, grads)
        back = lax.all_to_all(back, "cols", 0, 0, tiled=True)

    with jax.named_scope("backward"):
        parts = pl.pallas_call(
            backward_kernel,
            out_shape=shape((peers, SLOTS + 1, width, size), BF16),
            in_specs=[SMEM, VMEM, HBM],
            out_specs=HBM,
            scratch_shapes=[
                prod,
                sums(peers * SLOTS),
                pltpu.VMEM((peers, SLOTS + 1, width, size), BF16),
                pltpu.SemaphoreType.DMA((min(4, peers),)),
                tile_buf,
                pltpu.SemaphoreType.DMA((tiles // STEP,)),
            ],
            compiler_params=params(),
            cost_estimate=cost(1 << 30, 1 << 22),
        )(plan, back, in_hbm(tile_list))
        parts = lax.all_to_all(parts, "rows", 0, 0, tiled=True)

    with jax.named_scope("backward_own"):
        kept, inverse, pick, flat = pl.pallas_call(
            functools.partial(backward_own_kernel, peers * SLOTS),
            out_shape=(
                pltpu.HBM((count, width, size), F32),
                shape((count, size), I32),
                shape((2 * size, span), BF16),
                shape((1, 256), I32),
            ),
            in_specs=[SMEM, VMEM, HBM, VMEM, VMEM],
            out_specs=(HBM, VMEM, VMEM, VMEM),
            scratch_shapes=[
                prod,
                sums(count),
                tile_buf,
                pltpu.SemaphoreType.DMA((tiles // STEP,)),
                pltpu.VMEM((2 * count, span), BF16),
                pltpu.VMEM((size, span), BF16),
                pltpu.SemaphoreType.DMA,
            ],
            compiler_params=params(),
            cost_estimate=cost(1 << 31, 1 << 22),
        )(plan, back, in_hbm(tile_list), order, asked)

    with jax.named_scope("activated"):
        act, kept = lax.optimization_barrier((act, kept))
        activated = pl.pallas_call(
            lanes_kernel,
            out_shape=shape((width, span), BF16),
            in_specs=[SMEM, VMEM],
            out_specs=VMEM,
            compiler_params=params(),
        )(here_at, over_cols(act, here))

    with jax.named_scope("final"):
        feat_grads, weight_grad = pl.pallas_call(
            functools.partial(final_kernel, float(peers * span) ** -0.5),
            out_shape=(shape((width, span), BF16), shape((width, size), F32)),
            in_specs=[SMEM, VMEM, HBM, VMEM, VMEM],
            out_specs=(VMEM, VMEM),
            scratch_shapes=[pltpu.VMEM((count, width, size), F32), pltpu.SemaphoreType.DMA]
            + [pltpu.VMEM((count, width, size), F32)] * WAYS,
            compiler_params=params(),
        )(flat, parts, in_hbm(kept), inverse, pick)
    return activated, feat_grads, weight_grad.T


def solution(mesh):
    in_specs = (
        P("cols", "rows"),
        P("rows"),
        P("rows"),
        P("rows"),
        P("rows", None, None),
        P(),
        P("cols", "rows"),
    )
    out_specs = (P("cols", "rows"), P("cols", "rows"), P(None, "cols"))
    return jax.shard_map(shards, mesh=mesh, in_specs=in_specs, out_specs=out_specs, check_vma=False)
```

time: 128 us -> 124 us (0.969)
  the two profiles are of different devices: /device:TPU:2 before, /device:TPU:32 now
where the time goes in v3:
time: 124 us; the launch traced here: 123 us
  waiting for transfers between devices  44.5 us (36%)
  starting transfers between devices  29.1 us (23%)
  Pallas kernels  27.4 us (22%)
  blocking collectives  19.6 us (16%)
  local copies, waits for them, and re-layouts  1.68 us (1%)
    all_to_all x1, waiting for transfers between devices, shards(): parts = lax.all_to_all(parts, 'rows', 0, 0, tiled=True)  15.8 us
    all_to_all x1, waiting for transfers between devices, shards(): got = lax.all_to_all(send, 'rows', 0, 0, tiled=True)  11.5 us
    all_to_all x1, starting transfers between devices, shards(): asked = lax.all_to_all(want, 'rows', 0, 0, tiled=True)  11.2 us
    all_to_all x1, blocking collectives, shards(): mixed = lax.all_to_all(mixed, 'cols', 0, 0, tiled=True)  10.4 us
    ppermute x6, waiting for transfers between devices, over_cols(): part = lax.ppermute(part, 'cols', pairs)  9.29 us
    all_to_all x1, blocking collectives, shards(): back = lax.all_to_all(back, 'cols', 0, 0, tiled=True)  9.23 us
    ppermute x6, starting transfers between devices, over_cols(): part = lax.ppermute(part, 'cols', pairs)  7.41 us
    all_to_all x1, waiting for transfers between devices, shards(): asked = lax.all_to_all(want, 'rows', 0, 0, tiled=True)  5.49 us
  transfers between devices with their start and end apart: 11, of which 11 were waited for; matrix products, arithmetic and copies ran while one was open for 0% of the time, Pallas kernels for 10%

profile of v3, /device:TPU:32, one launch (start us, length us, event | category | flops | bytes accessed | tf_op | source)
XLA Modules:
  0.0 123.3 jit_solution(6682479957002431001)
XLA Ops:
  0.6 1.6 %index.3 = s32[32,1,128]{2,1,0:T(1,128)} custom-call(s32[1,128]{1,0:T(1,128)} %bitcast.34), custom_call_target="tpu_custom_call" | custom-call | tf_op jit(solution)/shard_map/index/pallas_call | solution.py:450
  2.3 11.2 %all-to-all-start = ((s32[32,1,128]{2,1,0:T(1,128)}), s32[32,1,128]{2,1,0:T(1,128)S(1)}, u32[]{:S(2)}, u32[]{:S(2)}) async-start(s32[32,1,128]{2,1,0:T(1,128)} %index.3), calls=%async_computation | async-start | bytes 32768 | tf_op jit(solution)/shard_map/index/all_to_all | solution.py:458
  13.5 0.9 copy-done.3
  14.4 0.7 copy-done.4
  15.1 1.4 %permute.1.blocks_ref.own_ref = bf16[32,16,128]{2,1,0:T(8,128)(2,1)S(1)} custom-call(bf16[16,4096]{1,0:T(8,128)(2,1)S(1)} %copy-done.3, s32[32,128]{1,0:T(8,128)S(1)} %bitcast.36), custom_call_target="tpu_custom_call" | custom-call | flops 2147483648 | bytes 4194304 | tf_op jit(solution)/shard_map/permute/pallas_call | solution.py:469
  16.5 5.5 %all-to-all-done.asked_ref = s32[32,1,128]{2,1,0:T(1,128)S(1)} async-done(((s32[32,1,128]{2,1,0:T(1,128)}), s32[32,1,128]{2,1,0:T(1,128)S(1)}, u32[]{:S(2)}, u32[]{:S(2)}) %all-to-all-start) | async-done | bytes 16416 | tf_op jit(solution)/shard_map/index/all_to_all | solution.py:458
  22.0 2.0 %pack.1 = bf16[32,8,16,128]{3,2,1,0:T(8,128)(2,1)} custom-call(s32[32,1,128]{2,1,0:T(1,128)S(1)} %all-to-all-done.asked_ref, bf16[32,16,128]{2,1,0:T(8,128)(2,1)S(1)} %permute.1.blocks_ref.own_ref), custom_call_target="tpu_custom_call" | custom-call | tf_op jit(solution)/shard_map/pack/pallas_call | solution.py:480
  24.0 5.0 %all-to-all-start.1 = ((bf16[32,8,16,128]{3,2,1,0:T(8,128)(2,1)}), bf16[32,8,16,128]{3,2,1,0:T(8,128)(2,1)S(1)}, u32[]{:S(2)}, u32[]{:S(2)}) async-start(bf16[32,8,16,128]{3,2,1,0:T(8,128)(2,1)} %pack.1), calls=%async_computation.1 | async-start | bytes 2097152 | tf_op jit(solution)/shard_map/pack/all_to_all | solution.py:487
  29.1 0.5 index.2.plan_ref
  29.6 5.1 %forward_own.1 = (f32[32,16,128]{2,1,0:T(8,128)S(1)}, bf16[128,128,128]{2,1,0:T(8,128)(2,1)}) custom-call(s32[8,128]{1,0:T(8,128)S(1)} %index.2.plan_ref, bf16[32,16,128]{2,1,0:T(8,128)(2,1)S(1)} %permute.1.blocks_ref.own_ref, bf16[128,128,128]{2,1,0:T(8,128)(2,1)} %tiles_hbm.1), custom_call_target="tpu_custom_call" | custom-call | flops 2147483648 | bytes 4194304 | tf_op jit(solution)/shard_map/forward_own/pallas_call | solution.py:490
  35.0 1.1 collective-permute-done
  36.2 3.1 %collective-permute-start.3 = (bf16[2,4,16,128]{3,2,1,0:T(8,128)(2,1)S(1)}, bf16[2,4,16,128]{3,2,1,0:T(8,128)(2,1)S(1)}, u32[]{:S(2)}, u32[]{:S(2)}) collective-permute-start(bf16[2,4,16,128]{3,2,1,0:T(8,128)(2,1)S(1)} %get-tuple-element.44), channel_id=1, source_target_pairs={{0,6},{1,7},{2,0},{3,1},{4,2},{5,3},{6,4},{7,5},{8,14},{9,15},{10,... | collective-permute-start | bytes 98312 | tf_op jit(solution)/shard_map/grads/ppermute | solution.py:53
  39.3 0.6 collective-permute-start.2
  39.9 1.0 collective-permute-start.1
  41.0 3.7 %collective-permute-done.2 = bf16[2,4,16,128]{3,2,1,0:T(8,128)(2,1)S(1)} collective-permute-done((bf16[2,4,16,128]{3,2,1,0:T(8,128)(2,1)S(1)}, bf16[2,4,16,128]{3,2,1,0:T(8,128)(2,1)S(1)}, u32[]{:S(2)}, u32[]{:S(2)}) %collective-permute-start.2) | collective-permute-done | bytes 32800 | tf_op jit(solution)/shard_map/grads/ppermute | solution.py:53
  45.1 11.5 %all-to-all-done.1 = bf16[32,8,16,128]{3,2,1,0:T(8,128)(2,1)S(1)} async-done(((bf16[32,8,16,128]{3,2,1,0:T(8,128)(2,1)}), bf16[32,8,16,128]{3,2,1,0:T(8,128)(2,1)S(1)}, u32[]{:S(2)}, u32[]{:S(2)}) %all-to-all-start.1) | async-done | bytes 1048608 | tf_op jit(solution)/shard_map/pack/all_to_all | solution.py:487
  56.6 2.9 %forward.1 = bf16[8,4,16,128]{3,2,1,0:T(8,128)(2,1)S(1)} custom-call(s32[8,128]{1,0:T(8,128)S(1)} %index.2.plan_ref, bf16[256,16,128]{2,1,0:T(8,128)(2,1)S(1)} %bitcast.32, f32[32,16,128]{2,1,0:T(8,128)S(1)} %get-tuple-element.22.part_ref, bf16[128,128,128]{2,1,0:T(8,128)(2,1)} %get-tuple-element.23.tiles_hbm), custom_call_target="tpu_custom_call" | custom-call | flops 1073741824 | bytes 4194304 | tf_op jit(solution)/shard_map/forward/pallas_call | solution.py:514
  59.5 10.4 %all_to_all.25.got_ref = bf16[8,4,16,128]{3,2,1,0:T(8,128)(2,1)S(1)} all-to-all(bf16[8,4,16,128]{3,2,1,0:T(8,128)(2,1)S(1)} %forward.1), channel_id=1, replica_groups=mesh['rows'=32,'cols'=8] {'cols'}, dimensions={0} | all-to-all | bytes 262144 | tf_op jit(solution)/shard_map/forward/all_to_all | solution.py:523
  69.9 1.3 %dense.1 = (bf16[8,6,16,128]{3,2,1,0:T(8,128)(2,1)S(1)}, bf16[8,4,16,128]{3,2,1,0:T(8,128)(2,1)}) custom-call(s32[1]{0:T(128)} %bitcast.here_ref, bf16[128,128]{1,0:T(8,128)(2,1)S(1)} %copy-done.1, bf16[8,4,16,128]{3,2,1,0:T(8,128)(2,1)S(1)} %all_to_all.25.got_ref, bf16[4,2,4,16,128]{4,3,2,1,0:T(8,128)(2,1)S(1)} %pad_maximum_fusion.grad_ref), custom_call_target="tpu_custom_call" | custom-call | tf_op jit(solution)/shard_map/dense/pallas_call | solution.py:526
  71.2 9.2 %all_to_all.26.got_ref = bf16[8,6,16,128]{3,2,1,0:T(8,128)(2,1)S(1)} all-to-all(bf16[8,6,16,128]{3,2,1,0:T(8,128)(2,1)S(1)} %get-tuple-element.26), channel_id=1, replica_groups=mesh['rows'=32,'cols'=8] {'cols'}, dimensions={0} | all-to-all | bytes 393216 | tf_op jit(solution)/shard_map/dense/all_to_all | solution.py:538
  80.4 3.7 %backward.1 = bf16[32,9,16,128]{3,2,1,0:T(8,128)(2,1)} custom-call(s32[8,128]{1,0:T(8,128)S(1)} %index.2.plan_ref, bf16[8,6,16,128]{3,2,1,0:T(8,128)(2,1)S(1)} %all_to_all.26.got_ref, bf16[128,128,128]{2,1,0:T(8,128)(2,1)} %get-tuple-element.23.tiles_hbm), custom_call_target="tpu_custom_call" | custom-call | flops 1073741824 | bytes 4194304 | tf_op jit(solution)/shard_map/backward/pallas_call | solution.py:541
  84.1 5.3 %all-to-all-start.4 = ((bf16[32,9,16,128]{3,2,1,0:T(8,128)(2,1)}), bf16[32,9,16,128]{3,2,1,0:T(8,128)(2,1)S(1)}, u32[]{:S(2)}, u32[]{:S(2)}) async-start(bf16[32,9,16,128]{3,2,1,0:T(8,128)(2,1)} %backward.1), calls=%async_computation.4 | async-start | bytes 2359296 | tf_op jit(solution)/shard_map/backward/all_to_all | solution.py:557
  89.5 5.1 %backward_own.1 = (f32[32,16,128]{2,1,0:T(8,128)}, s32[32,128]{1,0:T(8,128)S(1)}, bf16[256,4096]{1,0:T(8,128)(2,1)S(1)}, s32[1,256]{1,0:T(1,128)S(1)}) custom-call(s32[8,128]{1,0:T(8,128)S(1)} %index.2.plan_ref, bf16[8,6,16,128]{3,2,1,0:T(8,128)(2,1)S(1)} %all_to_all.26.got_ref, bf16[128,128,128]{2,1,0:T(8,128)(2,1)} %get-tuple-element.23.tiles_hbm, ...), custom_call_target="tpu_custom_call" | custom-call | flops 2147483648 | bytes 4194304 | tf_op jit(solution)/shard_map/backward_own/pallas_call | solution.py:560
  94.7 1.2 %collective-permute-done.4 = bf16[4,4,16,128]{3,2,1,0:T(8,128)(2,1)S(1)} collective-permute-done((bf16[4,4,16,128]{3,2,1,0:T(8,128)(2,1)S(1)}, bf16[4,4,16,128]{3,2,1,0:T(8,128)(2,1)S(1)}, u32[]{:S(2)}, u32[]{:S(2)}) %collective-permute-start.4) | collective-permute-done | bytes 65568 | tf_op jit(solution)/shard_map/activated/ppermute | solution.py:46
  96.0 1.2 %collective-permute-start.7 = (bf16[2,4,16,128]{3,2,1,0:T(8,128)(2,1)S(1)}, bf16[2,4,16,128]{3,2,1,0:T(8,128)(2,1)S(1)}, u32[]{:S(2)}, u32[]{:S(2)}) collective-permute-start(bf16[2,4,16,128]{3,2,1,0:T(8,128)(2,1)S(1)} %get-tuple-element.38), channel_id=1, source_target_pairs={{0,6},{1,7},{2,0},{3,1},{4,2},{5,3},{6,4},{7,5},{8,14},{9,15},{10,... | collective-permute-start | bytes 98312 | tf_op jit(solution)/shard_map/activated/ppermute | solution.py:53
  97.2 1.5 %collective-permute-start.6 = (bf16[2,4,16,128]{3,2,1,0:T(8,128)(2,1)S(1)}, bf16[2,4,16,128]{3,2,1,0:T(8,128)(2,1)S(1)}, u32[]{:S(2)}, u32[]{:S(2)}) collective-permute-start(bf16[2,4,16,128]{3,2,1,0:T(8,128)(2,1)S(1)} %get-tuple-element.37), channel_id=1, source_target_pairs={{0,4},{1,5},{2,6},{3,7},{4,0},{5,1},{6,2},{7,3},{8,12},{9,13},{10,... | collective-permute-start | bytes 98312 | tf_op jit(solution)/shard_map/activated/ppermute | solution.py:53
  98.7 1.3 %collective-permute-done.7 = bf16[2,4,16,128]{3,2,1,0:T(8,128)(2,1)S(1)} collective-permute-done((bf16[2,4,16,128]{3,2,1,0:T(8,128)(2,1)S(1)}, bf16[2,4,16,128]{3,2,1,0:T(8,128)(2,1)S(1)}, u32[]{:S(2)}, u32[]{:S(2)}) %collective-permute-start.7) | collective-permute-done | bytes 32800 | tf_op jit(solution)/shard_map/activated/ppermute | solution.py:53
  100.0 2.9 %collective-permute-done.6 = bf16[2,4,16,128]{3,2,1,0:T(8,128)(2,1)S(1)} collective-permute-done((bf16[2,4,16,128]{3,2,1,0:T(8,128)(2,1)S(1)}, bf16[2,4,16,128]{3,2,1,0:T(8,128)(2,1)S(1)}, u32[]{:S(2)}, u32[]{:S(2)}) %collective-permute-start.6) | collective-permute-done | bytes 32800 | tf_op jit(solution)/shard_map/activated/ppermute | solution.py:53
  102.9 0.9 collective-permute-done.5
  103.8 0.7 activated.1
  104.5 15.8 %all-to-all-done.4.got_ref = bf16[32,9,16,128]{3,2,1,0:T(8,128)(2,1)S(1)} async-done(((bf16[32,9,16,128]{3,2,1,0:T(8,128)(2,1)}), bf16[32,9,16,128]{3,2,1,0:T(8,128)(2,1)S(1)}, u32[]{:S(2)}, u32[]{:S(2)}) %all-to-all-start.4) | async-done | bytes 1179680 | tf_op jit(solution)/shard_map/backward/all_to_all | solution.py:557
  120.4 2.9 %final.1 = (bf16[16,4096]{1,0:T(8,128)(2,1)}, f32[16,128]{1,0:T(8,128)}) custom-call(s32[1,256]{1,0:T(1,128)S(1)} %get-tuple-element.29.asked_ref, bf16[32,9,16,128]{3,2,1,0:T(8,128)(2,1)S(1)} %all-to-all-done.4.got_ref, f32[32,16,128]{2,1,0:T(8,128)} %get-tuple-element.30.own_hbm, s32[32,128]{1,0:T(8,128)S(1)} %get-tuple-element.31.inverse_ref, ...), custom_call_target="tpu_custom_call" | custom-call | tf_op jit(solution)/shard_map/final/pallas_call | solution.py:594
  (26 shorter events, 0.9 us)
Async XLA Ops:
  2.3 19.7 %all-to-all-start = ((s32[32,1,128]{2,1,0:T(1,128)}), s32[32,1,128]{2,1,0:T(1,128)S(1)}, u32[]{:S(2)}, u32[]{:S(2)}) async-start(s32[32,1,128]{2,1,0:T(1,128)} %index.3), calls=%async_computation | async-start | bytes 32768 | tf_op jit(solution)/shard_map/index/all_to_all | solution.py:458
  13.5 0.9 copy-start.3
  14.4 0.7 copy-start.4
  16.5 12.5 %copy-start.2 = (s32[128]{0:T(128)S(1)}, s32[128]{0:T(128)}, u32[]{:S(2)}) copy-start(s32[128]{0:T(128)} %param.10) | copy-start | bytes 1540
  16.5 12.5 %copy-start.6 = (s32[128]{0:T(128)S(1)}, s32[128]{0:T(128)}, u32[]{:S(2)}) copy-start(s32[128]{0:T(128)} %param.9) | copy-start | bytes 1540
  24.0 32.5 %all-to-all-start.1 = ((bf16[32,8,16,128]{3,2,1,0:T(8,128)(2,1)}), bf16[32,8,16,128]{3,2,1,0:T(8,128)(2,1)S(1)}, u32[]{:S(2)}, u32[]{:S(2)}) async-start(bf16[32,8,16,128]{3,2,1,0:T(8,128)(2,1)} %pack.1), calls=%async_computation.1 | async-start | bytes 2097152 | tf_op jit(solution)/shard_map/pack/all_to_all | solution.py:487
  29.6 5.1 %copy-start = (bf16[16,4096]{1,0:T(8,128)(2,1)S(1)}, bf16[16,4096]{1,0:T(8,128)(2,1)}, u32[]{:S(2)}) copy-start(bf16[16,4096]{1,0:T(8,128)(2,1)} %grad_ref) | copy-start | bytes 393220
  34.8 1.3 %collective-permute-start = (bf16[4,4,16,128]{3,2,1,0:T(8,128)(2,1)S(1)}, bf16[4,4,16,128]{3,2,1,0:T(8,128)(2,1)S(1)}, u32[]{:S(2)}, u32[]{:S(2)}) collective-permute-start(bf16[4,4,16,128]{3,2,1,0:T(8,128)(2,1)S(1)} %get-tuple-element.45), channel_id=1, source_target_pairs={{0,1},{1,0},{2,3},{3,2},{4,5},{5,4},{6,7},{7,6},{8,9},{9,8},{10,11... | collective-permute-start | bytes 196616 | tf_op jit(solution)/shard_map/grads/ppermute | solution.py:46
  36.2 4.9 %collective-permute-start.3 = (bf16[2,4,16,128]{3,2,1,0:T(8,128)(2,1)S(1)}, bf16[2,4,16,128]{3,2,1,0:T(8,128)(2,1)S(1)}, u32[]{:S(2)}, u32[]{:S(2)}) collective-permute-start(bf16[2,4,16,128]{3,2,1,0:T(8,128)(2,1)S(1)} %get-tuple-element.44), channel_id=1, source_target_pairs={{0,6},{1,7},{2,0},{3,1},{4,2},{5,3},{6,4},{7,5},{8,14},{9,15},{10,... | collective-permute-start | bytes 98312 | tf_op jit(solution)/shard_map/grads/ppermute | solution.py:53
  39.3 5.4 %collective-permute-start.2 = (bf16[2,4,16,128]{3,2,1,0:T(8,128)(2,1)S(1)}, bf16[2,4,16,128]{3,2,1,0:T(8,128)(2,1)S(1)}, u32[]{:S(2)}, u32[]{:S(2)}) collective-permute-start(bf16[2,4,16,128]{3,2,1,0:T(8,128)(2,1)S(1)} %get-tuple-element.43), channel_id=1, source_target_pairs={{0,4},{1,5},{2,6},{3,7},{4,0},{5,1},{6,2},{7,3},{8,12},{9,13},{10,... | collective-permute-start | bytes 98312 | tf_op jit(solution)/shard_map/grads/ppermute | solution.py:53
  39.9 5.1 %collective-permute-start.1 = (bf16[2,4,16,128]{3,2,1,0:T(8,128)(2,1)S(1)}, bf16[2,4,16,128]{3,2,1,0:T(8,128)(2,1)S(1)}, u32[]{:S(2)}, u32[]{:S(2)}) collective-permute-start(bf16[2,4,16,128]{3,2,1,0:T(8,128)(2,1)S(1)} %get-tuple-element.42), channel_id=1, source_target_pairs={{0,2},{1,3},{2,4},{3,5},{4,6},{5,7},{6,0},{7,1},{8,10},{9,11},{10,... | collective-permute-start | bytes 98312 | tf_op jit(solution)/shard_map/grads/ppermute | solution.py:53
  56.6 13.3 %copy-start.1 = (bf16[128,128]{1,0:T(8,128)(2,1)S(1)}, bf16[128,128]{1,0:T(8,128)(2,1)}, u32[]{:S(2)}) copy-start(bf16[128,128]{1,0:T(8,128)(2,1)} %weight_ref.1) | copy-start | bytes 98308
  84.1 5.3 %copy-start.5 = (s32[4096]{0:T(1024)S(1)}, s32[4096]{0:T(1024)}, u32[]{:S(2)}) copy-start(s32[4096]{0:T(1024)} %param.8) | copy-start | bytes 49156
  84.1 36.2 %all-to-all-start.4 = ((bf16[32,9,16,128]{3,2,1,0:T(8,128)(2,1)}), bf16[32,9,16,128]{3,2,1,0:T(8,128)(2,1)S(1)}, u32[]{:S(2)}, u32[]{:S(2)}) async-start(bf16[32,9,16,128]{3,2,1,0:T(8,128)(2,1)} %backward.1), calls=%async_computation.4 | async-start | bytes 2359296 | tf_op jit(solution)/shard_map/backward/all_to_all | solution.py:557
  89.4 5.1 %copy-start.7 = (bf16[8,4,16,128]{3,2,1,0:T(8,128)(2,1)S(1)}, bf16[8,4,16,128]{3,2,1,0:T(8,128)(2,1)}, u32[]{:S(2)}) copy-start(bf16[8,4,16,128]{3,2,1,0:T(8,128)(2,1)} %get-tuple-element.28) | copy-start | bytes 393220
  94.6 1.3 %collective-permute-start.4 = (bf16[4,4,16,128]{3,2,1,0:T(8,128)(2,1)S(1)}, bf16[4,4,16,128]{3,2,1,0:T(8,128)(2,1)S(1)}, u32[]{:S(2)}, u32[]{:S(2)}) collective-permute-start(bf16[4,4,16,128]{3,2,1,0:T(8,128)(2,1)S(1)} %get-tuple-element.39), channel_id=1, source_target_pairs={{0,1},{1,0},{2,3},{3,2},{4,5},{5,4},{6,7},{7,6},{8,9},{9,8},{10,11... | collective-permute-start | bytes 196616 | tf_op jit(solution)/shard_map/activated/ppermute | solution.py:46
  96.0 4.0 %collective-permute-start.7 = (bf16[2,4,16,128]{3,2,1,0:T(8,128)(2,1)S(1)}, bf16[2,4,16,128]{3,2,1,0:T(8,128)(2,1)S(1)}, u32[]{:S(2)}, u32[]{:S(2)}) collective-permute-start(bf16[2,4,16,128]{3,2,1,0:T(8,128)(2,1)S(1)} %get-tuple-element.38), channel_id=1, source_target_pairs={{0,6},{1,7},{2,0},{3,1},{4,2},{5,3},{6,4},{7,5},{8,14},{9,15},{10,... | collective-permute-start | bytes 98312 | tf_op jit(solution)/shard_map/activated/ppermute | solution.py:53
  97.2 5.7 %collective-permute-start.6 = (bf16[2,4,16,128]{3,2,1,0:T(8,128)(2,1)S(1)}, bf16[2,4,16,128]{3,2,1,0:T(8,128)(2,1)S(1)}, u32[]{:S(2)}, u32[]{:S(2)}) collective-permute-start(bf16[2,4,16,128]{3,2,1,0:T(8,128)(2,1)S(1)} %get-tuple-element.37), channel_id=1, source_target_pairs={{0,4},{1,5},{2,6},{3,7},{4,0},{5,1},{6,2},{7,3},{8,12},{9,13},{10,... | collective-permute-start | bytes 98312 | tf_op jit(solution)/shard_map/activated/ppermute | solution.py:53
  98.7 5.1 %collective-permute-start.5 = (bf16[2,4,16,128]{3,2,1,0:T(8,128)(2,1)S(1)}, bf16[2,4,16,128]{3,2,1,0:T(8,128)(2,1)S(1)}, u32[]{:S(2)}, u32[]{:S(2)}) collective-permute-start(bf16[2,4,16,128]{3,2,1,0:T(8,128)(2,1)S(1)} %get-tuple-element.36), channel_id=1, source_target_pairs={{0,2},{1,3},{2,4},{3,5},{4,6},{5,7},{6,0},{7,1},{8,10},{9,11},{10,... | collective-permute-start | bytes 98312 | tf_op jit(solution)/shard_map/activated/ppermute | solution.py:53

commit v4 on v3

--- a/solution.py
+++ b/solution.py
@@ -13,6 +13,7 @@
 SLOTS = 8
 STEP = 16
 WAYS = 4
+LONG = 8
 PIECES = 8
 VMEM = pl.BlockSpec(memory_space=pltpu.VMEM)
 HBM = pl.BlockSpec(memory_space=pltpu.HBM)
@@ -55,6 +56,13 @@
     return jnp.stack(parts)
 
 
+def along(value, steps, peers):
+    if not steps:
+        return value
+    pairs = [(i, i // LONG * LONG + (i + steps) % LONG) for i in range(peers)]
+    return lax.ppermute(value, "rows", pairs)
+
+
 def in_hbm(x):
     return pltpu.with_memory_space_constraint(x, pltpu.HBM)
 
@@ -63,8 +71,12 @@
     return lax.dot_general(a, b, dims, preferred_element_type=F32)
 
 
+def position(col):
+    return ((col >> 8) * 2 + ((col >> 5) & 1)) * (LONG // 2) + ((col >> 6) & 3)
+
+
 def ranks(col, peers):
-    peer, block = col >> 5, col & 31
+    peer, block = position(col), col & 31
     of_peer = (lax.broadcasted_iota(I32, (peers, col.shape[1]), 0) == peer).astype(F32)
     of_block = (lax.broadcasted_iota(I32, (32, col.shape[1]), 0) == block).astype(F32)
     counts = dot(of_peer.astype(BF16), of_block.astype(BF16), NT)
@@ -81,7 +93,8 @@
     copy = pltpu.make_async_copy(col_hbm, col_buf, sem)
     copy.start()
     copy.wait()
-    peers = want_ref.shape[0]
+    relays, turns, _ = want_ref.shape
+    peers = relays * turns
     _, _, present, rank = ranks(col_buf[...], peers)
     number = lax.broadcasted_iota(I32, (peers, 32), 1).astype(F32)
     lane = lax.broadcasted_iota(I32, (peers, 128), 1)
@@ -91,7 +104,9 @@
             jnp.where(rank == float(s), present * number, 0.0), axis=1, keepdims=True
         )
         want = jnp.where(lane == s, chosen, want)
-    want_ref[...] = want.astype(I32).reshape(peers, 1, 128)
+    want = want.astype(I32)
+    for m in range(relays):
+        want_ref[m] = want[m * turns : (m + 1) * turns, :]
 
 
 def plan_kernel(peers, row_ref, col_ref, plan_ref):
@@ -118,7 +133,7 @@
     values = jnp.concatenate(
         [
             lax.broadcasted_iota(I32, (1, tiles), 1).astype(F32),
-            jnp.where(own > 0.5, float(peers), (col >> 5).astype(F32)),
+            jnp.where(own > 0.5, float(peers), position(col).astype(F32)),
             jnp.where(own > 0.5, (col & 31).astype(F32), tile_rank),
             (row & 31).astype(F32),
             jnp.zeros((4, tiles), F32),
@@ -167,10 +182,19 @@
         out_ref[j + 1] = total[:, 128:]
 
 
-def pack_kernel(asked_ref, blocks_ref, buf):
-    for p in range(buf.shape[0]):
-        for s in range(SLOTS):
-            buf[p, s] = blocks_ref[asked_ref[p, 0, s]]
+def pack_kernel(here_ref, asked_ref, *refs):
+    held, (send_hbm, buf, sems) = refs[:-3], refs[-3:]
+    pieces = sems.shape[0]
+    members = buf.shape[0] // pieces
+    for piece in range(pieces):
+        for m in range(piece * members, (piece + 1) * members):
+            for far, blocks_ref in enumerate(held):
+                k = (here_ref[0] + far) % len(held)
+                for s in range(SLOTS):
+                    buf[m, k * SLOTS + s] = blocks_ref[asked_ref[m, k, s]]
+        send_out(buf, send_hbm, sems, piece).start()
+    for piece in range(pieces):
+        send_out(buf, send_hbm, sems, piece).wait()
 
 
 def chunk_copy(tiles_hbm, tiles, sems, i):
@@ -296,17 +320,18 @@
     fetch_tiles(begin, last, tiles_hbm, tiles, tile_sems)
     groups = got_ref.shape[0]
     per = got_ref.shape[1] - 2
-    peers = buf.shape[0]
+    relays = buf.shape[0]
+    each = buf.shape[1] - 1
     pieces = sems.shape[0]
-    share = peers // pieces
-    slots = peers * SLOTS
+    share = relays // pieces
+    slots = relays * each
     total[...] = jnp.zeros_like(total)
     part = got_ref[0, per].astype(F32) + got_ref[0, per + 1].astype(F32)
     for c in range(1, groups):
         part = part + got_ref[c, per].astype(F32) + got_ref[c, per + 1].astype(F32)
     part = part.astype(BF16)
-    for p in range(peers):
-        buf[p, SLOTS] = part
+    for m in range(relays):
+        buf[m, each] = part
 
     def step(i, carry):
         chunk_copy(tiles_hbm, tiles, tile_sems, i).wait()
@@ -319,12 +344,12 @@
             total[at] = total[at] + prod[u]
         done = (i + 1) * STEP
         for piece in range(pieces):
-            until = plan_ref[4, (piece + 1) * share] if piece + 1 < pieces else last * STEP
+            until = plan_ref[4, (piece + 1) * share * each // SLOTS] if piece + 1 < pieces else last * STEP
 
             @pl.when((until <= done) & ((until > i * STEP) | (i == begin)))
             def _():
-                for p in range(piece * share, (piece + 1) * share):
-                    buf[p, :SLOTS] = total[p * SLOTS : (p + 1) * SLOTS].astype(BF16)
+                for m in range(piece * share, (piece + 1) * share):
+                    buf[m, :each] = total[m * each : (m + 1) * each].astype(BF16)
                 send_out(buf, send_hbm, sems, piece).start()
 
         return carry
@@ -335,7 +360,7 @@
 
 
 def backward_own_kernel(
-    base, plan_ref, got_ref, tiles_hbm, order_ref, asked_ref, out_hbm, inverse_ref, pick_ref, flat_ref, prod, total, tiles, sems, spots, low_pick, out_sem
+    base, plan_ref, got_ref, tiles_hbm, order_ref, out_hbm, inverse_ref, pick_ref, prod, total, tiles, sems, spots, low_pick, out_sem
 ):
     fetch_tiles(0, (plan_ref[3, 0] + STEP - 1) // STEP, tiles_hbm, tiles, sems)
     count, width = out_hbm.shape[:2]
@@ -372,16 +397,6 @@
         at = inverse[count + j : count + j + 1, :] + (inverse[j : j + 1, :] & 1) * 128
         pick_ref[:, j * 128 : (j + 1) * 128] = jnp.where(odd == at, 1.0, 0.0).astype(BF16)
     inverse_ref[...] = inverse[:count] >> 1
-    peers = asked_ref.shape[0]
-    spread = dot(
-        asked_ref[...].reshape(peers, 128).astype(F32).astype(BF16),
-        (
-            lax.broadcasted_iota(I32, (128, 256), 0) == lax.broadcasted_iota(I32, (128, 256), 1) % SLOTS
-        ).astype(F32).astype(BF16),
-        NN,
-    )
-    mine = lax.broadcasted_iota(I32, (peers, 256), 0) == lax.broadcasted_iota(I32, (peers, 256), 1) // SLOTS
-    flat_ref[...] = jnp.sum(jnp.where(mine, spread, 0.0), axis=0, keepdims=True).astype(I32)
     store.wait()
 
 
@@ -401,28 +416,50 @@
                 out_ref[:, pl.ds(pl.multiple_of((at + b) * 128, 128), 128)] = got_ref[far, core, b]
 
 
-def final_kernel(scale, asked_ref, got_ref, own_hbm, inverse_ref, pick_ref, grads_ref, weight_ref, own, sem, *totals):
-    fetch = pltpu.make_async_copy(own_hbm, own, sem)
-    fetch.start()
-    peers = got_ref.shape[0]
-    count, width = own.shape[:2]
-    ways = len(totals)
+def relay_kernel(turn_ref, asked_ref, got_ref, own_ref, *refs):
+    outs, totals = refs[: -WAYS], refs[-WAYS:]
+    members, each = got_ref.shape[:2]
+    each = each - 1
+    turns = each // SLOTS
+    count = own_ref.shape[0] - 1
     for total in totals:
         total[...] = jnp.zeros_like(total)
-    part = got_ref[0, SLOTS].astype(F32)
-    for p in range(1, peers):
-        part = part + got_ref[p, SLOTS].astype(F32)
+    for m in range(0, members, WAYS):
+        for k in range(turns):
+            for s in range(SLOTS):
+                for w, total in enumerate(totals):
+                    at = k * count + asked_ref[m + w, k, s]
+                    total[at] = total[at] + got_ref[m + w, k * SLOTS + s].astype(F32)
+    part = got_ref[0, each].astype(F32)
+    for m in range(1, members):
+        part = part + got_ref[m, each].astype(F32)
+    own_ref[count] = part
+    high = part.astype(BF16)
+    low = (part - high.astype(F32)).astype(BF16)
+    for far in range(turns):
+        at = pl.ds((turn_ref[0] + far) % turns * count, count)
+        value = totals[0][at]
+        for total in totals[1:]:
+            value = value + total[at]
+        if far:
+            outs[far - 1][:count] = value.astype(BF16)
+            outs[far - 1][count] = high
+            outs[far - 1][count + 1] = low
+        else:
+            own_ref[:count] = value
+
+
+def final_kernel(scale, kept_hbm, own_ref, one_ref, two_ref, three_ref, inverse_ref, pick_ref, grads_ref, weight_ref, kept, sem):
+    fetch = pltpu.make_async_copy(kept_hbm, kept, sem)
+    fetch.start()
+    count = kept.shape[0]
+    part, node = own_ref[count], own_ref[:count]
+    for ref in (one_ref, two_ref, three_ref):
+        part = part + ref[count].astype(F32) + ref[count + 1].astype(F32)
+        node = node + ref[:count].astype(F32)
     weight_ref[...] = part * scale
-    for p in range(0, peers, ways):
-        for s in range(SLOTS):
-            for w, total in enumerate(totals):
-                at = asked_ref[0, (p + w) * SLOTS + s]
-                total[at] = total[at] + got_ref[p + w, s].astype(F32)
     fetch.wait()
-    node = own[...]
-    for total in totals:
-        node = node + total[...]
-    node = node.astype(BF16)
+    node = (node + kept[...]).astype(BF16)
     blocked = jnp.concatenate(
         [jnp.concatenate([node[j], node[j + 1]], axis=1) for j in range(0, count, 2)], axis=0
     )
@@ -445,25 +482,13 @@
     tile_buf = pltpu.VMEM(tile_vals.shape, BF16)
     sums = lambda n: pltpu.VMEM((n + 1, width, size), F32)
 
-    with jax.named_scope("index"):
-        rows, cols = tile_row.reshape(1, tiles), tile_col.reshape(1, tiles)
-        want = pl.pallas_call(
-            want_kernel,
-            out_shape=shape((peers, 1, 128), I32),
-            in_specs=[HBM],
-            out_specs=VMEM,
-            scratch_shapes=[pltpu.VMEM((1, tiles), I32), pltpu.SemaphoreType.DMA],
-            compiler_params=params(),
-        )(in_hbm(cols))
-        asked = lax.all_to_all(want, "rows", 0, 0, tiled=True)
-        plan = pl.pallas_call(
-            functools.partial(plan_kernel, peers),
-            out_shape=shape((8, tiles), I32),
-            in_specs=[VMEM, VMEM],
-            out_specs=VMEM,
-            compiler_params=params(),
-            cost_estimate=cost(1 << 30, 1 << 21),
-        )(rows, cols)
+    relays, turns = 2 * (peers // LONG), LONG // 2
+    turn = lax.axis_index("rows") % LONG // 2
+    turn_at = turn.reshape(1)
+    near = [
+        [x * LONG + 2 * j + q for x in range(peers // LONG) for q in range(2)] for j in range(turns)
+    ]
+    swap = lambda v: lax.all_to_all(v, "rows", 0, 0, tiled=True, axis_index_groups=near)
 
     with jax.named_scope("permute"):
         own = pl.pallas_call(
@@ -475,16 +500,41 @@
             compiler_params=params(),
             cost_estimate=cost(1 << 31, 1 << 22),
         )(features, order)
+        held = [own] + [along(own, -2 * far, peers) for far in range(1, turns)]
+
+    with jax.named_scope("index"):
+        rows, cols = tile_row.reshape(1, tiles), tile_col.reshape(1, tiles)
+        want = pl.pallas_call(
+            want_kernel,
+            out_shape=shape((relays, turns, 128), I32),
+            in_specs=[HBM],
+            out_specs=VMEM,
+            scratch_shapes=[pltpu.VMEM((1, tiles), I32), pltpu.SemaphoreType.DMA],
+            compiler_params=params(),
+        )(in_hbm(cols))
+        asked = swap(want)
+        plan = pl.pallas_call(
+            functools.partial(plan_kernel, peers),
+            out_shape=shape((8, tiles), I32),
+            in_specs=[VMEM, VMEM],
+            out_specs=VMEM,
+            compiler_params=params(),
+            cost_estimate=cost(1 << 30, 1 << 21),
+        )(rows, cols)
 
     with jax.named_scope("pack"):
         send = pl.pallas_call(
             pack_kernel,
-            out_shape=pltpu.VMEM((peers, SLOTS, width, size), BF16),
-            in_specs=[SMEM, VMEM],
-            out_specs=VMEM,
-            compiler_params=params(),
-        )(asked, own)
-        got = lax.all_to_all(send, "rows", 0, 0, tiled=True)
+            out_shape=shape((relays, turns * SLOTS, width, size), BF16),
+            in_specs=[SMEM, SMEM] + [VMEM] * turns,
+            out_specs=HBM,
+            scratch_shapes=[
+                pltpu.VMEM((relays, turns * SLOTS, width, size), BF16),
+                pltpu.SemaphoreType.DMA((min(PIECES, relays),)),
+            ],
+            compiler_params=params(),
+        )(turn_at, asked, *held)
+        got = swap(send)
 
     with jax.named_scope("forward_own"):
         part, tile_list = pl.pallas_call(
@@ -540,33 +590,32 @@
     with jax.named_scope("backward"):
         parts = pl.pallas_call(
             backward_kernel,
-            out_shape=shape((peers, SLOTS + 1, width, size), BF16),
+            out_shape=shape((relays, turns * SLOTS + 1, width, size), BF16),
             in_specs=[SMEM, VMEM, HBM],
             out_specs=HBM,
             scratch_shapes=[
                 prod,
                 sums(peers * SLOTS),
-                pltpu.VMEM((peers, SLOTS + 1, width, size), BF16),
-                pltpu.SemaphoreType.DMA((min(4, peers),)),
+                pltpu.VMEM((relays, turns * SLOTS + 1, width, size), BF16),
+                pltpu.SemaphoreType.DMA((4,)),
                 tile_buf,
                 pltpu.SemaphoreType.DMA((tiles // STEP,)),
             ],
             compiler_params=params(),
             cost_estimate=cost(1 << 30, 1 << 22),
         )(plan, back, in_hbm(tile_list))
-        parts = lax.all_to_all(parts, "rows", 0, 0, tiled=True)
+        parts = swap(parts)
 
     with jax.named_scope("backward_own"):
-        kept, inverse, pick, flat = pl.pallas_call(
+        kept, inverse, pick = pl.pallas_call(
             functools.partial(backward_own_kernel, peers * SLOTS),
             out_shape=(
                 pltpu.HBM((count, width, size), F32),
                 shape((count, size), I32),
                 shape((2 * size, span), BF16),
-                shape((1, 256), I32),
             ),
-            in_specs=[SMEM, VMEM, HBM, VMEM, VMEM],
-            out_specs=(HBM, VMEM, VMEM, VMEM),
+            in_specs=[SMEM, VMEM, HBM, VMEM],
+            out_specs=(HBM, VMEM, VMEM),
             scratch_shapes=[
                 prod,
                 sums(count),
@@ -578,7 +627,7 @@
             ],
             compiler_params=params(),
             cost_estimate=cost(1 << 31, 1 << 22),
-        )(plan, back, in_hbm(tile_list), order, asked)
+        )(plan, back, in_hbm(tile_list), order)
 
     with jax.named_scope("activated"):
         act, kept = lax.optimization_barrier((act, kept))
@@ -590,16 +639,27 @@
             compiler_params=params(),
         )(here_at, over_cols(act, here))
 
+    with jax.named_scope("relay"):
+        sums_of = pl.pallas_call(
+            relay_kernel,
+            out_shape=(shape((count + 1, width, size), F32),)
+            + (shape((count + 2, width, size), BF16),) * (turns - 1),
+            in_specs=[SMEM, SMEM, VMEM],
+            out_specs=(VMEM,) * turns,
+            scratch_shapes=[pltpu.VMEM((turns * count, width, size), F32)] * WAYS,
+            compiler_params=params(),
+        )(turn_at, asked, parts)
+        sums_of = [along(v, 2 * far, peers) for far, v in enumerate(sums_of)]
+
     with jax.named_scope("final"):
         feat_grads, weight_grad = pl.pallas_call(
             functools.partial(final_kernel, float(peers * span) ** -0.5),
             out_shape=(shape((width, span), BF16), shape((width, size), F32)),
-            in_specs=[SMEM, VMEM, HBM, VMEM, VMEM],
+            in_specs=[HBM] + [VMEM] * (turns + 2),
             out_specs=(VMEM, VMEM),
-            scratch_shapes=[pltpu.VMEM((count, width, size), F32), pltpu.SemaphoreType.DMA]
-            + [pltpu.VMEM((count, width, size), F32)] * WAYS,
-            compiler_params=params(),
-        )(flat, parts, in_hbm(kept), inverse, pick)
+            scratch_shapes=[pltpu.VMEM((count, width, size), F32), pltpu.SemaphoreType.DMA],
+            compiler_params=params(),
+        )(in_hbm(kept), *sums_of, inverse, pick)
     return activated, feat_grads, weight_grad.T
 
 

time: 124 us -> 120 us (0.968)
  the two profiles are of different devices: /device:TPU:32 before, /device:TPU:2 now
where the time goes in v4:
time: 120 us; the launch traced here: 119 us
  starting transfers between devices  43.7 us (36%)
  Pallas kernels  28.7 us (24%)
  waiting for transfers between devices  23.1 us (19%)
  blocking collectives  19 us (16%)
  local copies, waits for them, and re-layouts  1.68 us (1%)
  other arithmetic  1.44 us (1%)
    ppermute x6, starting transfers between devices, along(): return lax.ppermute(value, 'rows', pairs)  18.2 us
    all_to_all x3, starting transfers between devices, shards(): lax.all_to_all(v, 'rows', 0, 0, tiled=True, axis_index_groups=near)  16.2 us
    ppermute x6, waiting for transfers between devices, along(): return lax.ppermute(value, 'rows', pairs)  10.1 us
    all_to_all x1, blocking collectives, shards(): mixed = lax.all_to_all(mixed, 'cols', 0, 0, tiled=True)  9.77 us
    all_to_all x1, blocking collectives, shards(): back = lax.all_to_all(back, 'cols', 0, 0, tiled=True)  9.23 us
    ppermute x6, starting transfers between devices, over_cols(): part = lax.ppermute(part, 'cols', pairs)  9.15 us
    all_to_all x3, waiting for transfers between devices, shards(): lax.all_to_all(v, 'rows', 0, 0, tiled=True, axis_index_groups=near)  8.11 us
    pallas_call x1, Pallas kernels, shards(): pl.pallas_call(functools.partial(forward_own_kernel, peers * SLOTS), out_...  5.13 us
  transfers between devices with their start and end apart: 17, of which 9 were waited for; matrix products, arithmetic and copies ran while one was open for 1% of the time, Pallas kernels for 13%

profile of v4, /device:TPU:2, one launch (start us, length us, event | category | flops | bytes accessed | tf_op | source)
XLA Modules:
  0.0 118.8 jit_solution(14633801799329983134)
XLA Ops:
  2.3 1.4 %permute.1.refs_0_.own_ref = bf16[32,16,128]{2,1,0:T(8,128)(2,1)S(1)} custom-call(bf16[16,4096]{1,0:T(8,128)(2,1)S(1)} %copy-done.3, s32[32,128]{1,0:T(8,128)S(1)} %bitcast.37), custom_call_target="tpu_custom_call" | custom-call | flops 2147483648 | bytes 4194304 | tf_op jit(solution)/shard_map/permute/pallas_call | solution.py:494
  3.7 6.4 %collective-permute-start = (bf16[32,16,128]{2,1,0:T(8,128)(2,1)S(1)}, bf16[32,16,128]{2,1,0:T(8,128)(2,1)S(1)}, u32[]{:S(2)}, u32[]{:S(2)}) collective-permute-start(bf16[32,16,128]{2,1,0:T(8,128)(2,1)S(1)} %permute.1.refs_0_.own_ref), channel_id=1, source_target_pairs={{0,48},{8,56},{16,0},{24,8},{32,16},{40,24},{48,32},{56,40},{64,11... | collective-permute-start | bytes 393224 | tf_op jit(solution)/shard_map/permute/ppermute | solution.py:63
  11.0 2.8 %collective-permute-start.2 = (bf16[32,16,128]{2,1,0:T(8,128)(2,1)S(1)}, bf16[32,16,128]{2,1,0:T(8,128)(2,1)S(1)}, u32[]{:S(2)}, u32[]{:S(2)}) collective-permute-start(bf16[32,16,128]{2,1,0:T(8,128)(2,1)S(1)} %permute.1.refs_0_.own_ref), channel_id=1, source_target_pairs={{0,16},{8,24},{16,32},{24,40},{32,48},{40,56},{48,0},{56,8},{64,80... | collective-permute-start | bytes 393224 | tf_op jit(solution)/shard_map/permute/ppermute | solution.py:63
  13.9 1.6 %index.3 = s32[8,4,128]{2,1,0:T(4,128)} custom-call(s32[1,128]{1,0:T(1,128)} %bitcast.35), custom_call_target="tpu_custom_call" | custom-call | tf_op jit(solution)/shard_map/index/pallas_call | solution.py:507
  15.5 5.3 %all-to-all-start = ((s32[8,4,128]{2,1,0:T(4,128)}), s32[8,4,128]{2,1,0:T(4,128)S(1)}, u32[]{:S(2)}, u32[]{:S(2)}) async-start(s32[8,4,128]{2,1,0:T(4,128)} %index.3), calls=%async_computation | async-start | bytes 32768 | tf_op jit(solution)/shard_map/index/all_to_all | solution.py:491
  20.8 4.8 %all-to-all-done.asked_ref = s32[8,4,128]{2,1,0:T(4,128)S(1)} async-done(((s32[8,4,128]{2,1,0:T(4,128)}), s32[8,4,128]{2,1,0:T(4,128)S(1)}, u32[]{:S(2)}, u32[]{:S(2)}) %all-to-all-start) | async-done | bytes 16416 | tf_op jit(solution)/shard_map/index/all_to_all | solution.py:491
  25.6 2.3 %pack.1 = bf16[8,32,16,128]{3,2,1,0:T(8,128)(2,1)} custom-call(s32[1]{0:T(128)} %bitcast.3.here_ref.turn_ref, s32[8,4,128]{2,1,0:T(4,128)S(1)} %all-to-all-done.asked_ref, bf16[32,16,128]{2,1,0:T(8,128)(2,1)S(1)} %permute.1.refs_0_.own_ref, bf16[32,16,128]{2,1,0:T(8,128)(2,1)S(1)} %collective-permute-done.refs_1_, ...), custom_call_target="tpu_custom_call" | custom-call | tf_op jit(solution)/shard_map/pack/pallas_call | solution.py:526
  27.8 4.9 %all-to-all-start.1 = ((bf16[8,32,16,128]{3,2,1,0:T(8,128)(2,1)}), bf16[8,32,16,128]{3,2,1,0:T(8,128)(2,1)S(1)}, u32[]{:S(2)}, u32[]{:S(2)}) async-start(bf16[8,32,16,128]{3,2,1,0:T(8,128)(2,1)} %pack.1), calls=%async_computation.1 | async-start | bytes 2097152 | tf_op jit(solution)/shard_map/pack/all_to_all | solution.py:491
  33.3 5.1 %forward_own.1 = (f32[32,16,128]{2,1,0:T(8,128)S(1)}, bf16[128,128,128]{2,1,0:T(8,128)(2,1)}) custom-call(s32[8,128]{1,0:T(8,128)S(1)} %index.2.plan_ref, bf16[32,16,128]{2,1,0:T(8,128)(2,1)S(1)} %permute.1.refs_0_.own_ref, bf16[128,128,128]{2,1,0:T(8,128)(2,1)} %tiles_hbm.1), custom_call_target="tpu_custom_call" | custom-call | flops 2147483648 | bytes 4194304 | tf_op jit(solution)/shard_map/forward_own/pallas_call | solution.py:540
  39.9 1.7 %collective-permute-start.4 = (bf16[2,4,16,128]{3,2,1,0:T(8,128)(2,1)S(1)}, bf16[2,4,16,128]{3,2,1,0:T(8,128)(2,1)S(1)}, u32[]{:S(2)}, u32[]{:S(2)}) collective-permute-start(bf16[2,4,16,128]{3,2,1,0:T(8,128)(2,1)S(1)} %get-tuple-element.48), channel_id=1, source_target_pairs={{0,2},{1,3},{2,4},{3,5},{4,6},{5,7},{6,0},{7,1},{8,10},{9,11},{10,... | collective-permute-start | bytes 98312 | tf_op jit(solution)/shard_map/grads/ppermute | solution.py:54
  41.6 2.9 %collective-permute-start.5 = (bf16[2,4,16,128]{3,2,1,0:T(8,128)(2,1)S(1)}, bf16[2,4,16,128]{3,2,1,0:T(8,128)(2,1)S(1)}, u32[]{:S(2)}, u32[]{:S(2)}) collective-permute-start(bf16[2,4,16,128]{3,2,1,0:T(8,128)(2,1)S(1)} %get-tuple-element.49), channel_id=1, source_target_pairs={{0,4},{1,5},{2,6},{3,7},{4,0},{5,1},{6,2},{7,3},{8,12},{9,13},{10,... | collective-permute-start | bytes 98312 | tf_op jit(solution)/shard_map/grads/ppermute | solution.py:54
  44.5 1.3 %collective-permute-start.6 = (bf16[2,4,16,128]{3,2,1,0:T(8,128)(2,1)S(1)}, bf16[2,4,16,128]{3,2,1,0:T(8,128)(2,1)S(1)}, u32[]{:S(2)}, u32[]{:S(2)}) collective-permute-start(bf16[2,4,16,128]{3,2,1,0:T(8,128)(2,1)S(1)} %get-tuple-element.50), channel_id=1, source_target_pairs={{0,6},{1,7},{2,0},{3,1},{4,2},{5,3},{6,4},{7,5},{8,14},{9,15},{10,... | collective-permute-start | bytes 98312 | tf_op jit(solution)/shard_map/grads/ppermute | solution.py:54
  45.8 1.2 collective-permute-done.5
  47.0 1.4 %collective-permute-done.6 = bf16[2,4,16,128]{3,2,1,0:T(8,128)(2,1)S(1)} collective-permute-done((bf16[2,4,16,128]{3,2,1,0:T(8,128)(2,1)S(1)}, bf16[2,4,16,128]{3,2,1,0:T(8,128)(2,1)S(1)}, u32[]{:S(2)}, u32[]{:S(2)}) %collective-permute-start.6) | collective-permute-done | bytes 32800 | tf_op jit(solution)/shard_map/grads/ppermute | solution.py:54
  48.4 2.9 %forward.1 = bf16[8,4,16,128]{3,2,1,0:T(8,128)(2,1)S(1)} custom-call(s32[8,128]{1,0:T(8,128)S(1)} %index.2.plan_ref, bf16[256,16,128]{2,1,0:T(8,128)(2,1)S(1)} %bitcast.33, f32[32,16,128]{2,1,0:T(8,128)S(1)} %get-tuple-element.25.part_ref, bf16[128,128,128]{2,1,0:T(8,128)(2,1)} %get-tuple-element.26.tiles_hbm), custom_call_target="tpu_custom_call" | custom-call | flops 1073741824 | bytes 4194304 | tf_op jit(solution)/shard_map/forward/pallas_call | solution.py:564
  51.4 9.8 %all_to_all.25.got_ref = bf16[8,4,16,128]{3,2,1,0:T(8,128)(2,1)S(1)} all-to-all(bf16[8,4,16,128]{3,2,1,0:T(8,128)(2,1)S(1)} %forward.1), channel_id=1, replica_groups=mesh['rows'=32,'cols'=8] {'cols'}, dimensions={0} | all-to-all | bytes 262144 | tf_op jit(solution)/shard_map/forward/all_to_all | solution.py:573
  61.1 1.3 %dense.1 = (bf16[8,6,16,128]{3,2,1,0:T(8,128)(2,1)S(1)}, bf16[8,4,16,128]{3,2,1,0:T(8,128)(2,1)}) custom-call(s32[1]{0:T(128)} %bitcast.here_ref, bf16[128,128]{1,0:T(8,128)(2,1)S(1)} %copy-done.1, bf16[8,4,16,128]{3,2,1,0:T(8,128)(2,1)S(1)} %all_to_all.25.got_ref, bf16[4,2,4,16,128]{4,3,2,1,0:T(8,128)(2,1)S(1)} %pad_maximum_fusion.grad_ref), custom_call_target="tpu_custom_call" | custom-call | tf_op jit(solution)/shard_map/dense/pallas_call | solution.py:576
  62.4 9.2 %all_to_all.26.got_ref = bf16[8,6,16,128]{3,2,1,0:T(8,128)(2,1)S(1)} all-to-all(bf16[8,6,16,128]{3,2,1,0:T(8,128)(2,1)S(1)} %get-tuple-element.29), channel_id=1, replica_groups=mesh['rows'=32,'cols'=8] {'cols'}, dimensions={0} | all-to-all | bytes 393216 | tf_op jit(solution)/shard_map/dense/all_to_all | solution.py:588
  71.6 3.6 %backward.1 = bf16[8,33,16,128]{3,2,1,0:T(8,128)(2,1)} custom-call(s32[8,128]{1,0:T(8,128)S(1)} %index.2.plan_ref, bf16[8,6,16,128]{3,2,1,0:T(8,128)(2,1)S(1)} %all_to_all.26.got_ref, bf16[128,128,128]{2,1,0:T(8,128)(2,1)} %get-tuple-element.26.tiles_hbm), custom_call_target="tpu_custom_call" | custom-call | flops 1073741824 | bytes 4194304 | tf_op jit(solution)/shard_map/backward/pallas_call | solution.py:591
  75.2 5.9 %all-to-all-start.4 = ((bf16[8,33,16,128]{3,2,1,0:T(8,128)(2,1)}), bf16[8,33,16,128]{3,2,1,0:T(8,128)(2,1)S(1)}, u32[]{:S(2)}, u32[]{:S(2)}) async-start(bf16[8,33,16,128]{3,2,1,0:T(8,128)(2,1)} %backward.1), calls=%async_computation.4 | async-start | bytes 2162688 | tf_op jit(solution)/shard_map/backward/all_to_all | solution.py:491
  81.2 5.1 %backward_own.1 = (f32[32,16,128]{2,1,0:T(8,128)}, s32[32,128]{1,0:T(8,128)S(1)}, bf16[256,4096]{1,0:T(8,128)(2,1)S(1)}) custom-call(s32[8,128]{1,0:T(8,128)S(1)} %index.2.plan_ref, bf16[8,6,16,128]{3,2,1,0:T(8,128)(2,1)S(1)} %all_to_all.26.got_ref, bf16[128,128,128]{2,1,0:T(8,128)(2,1)} %get-tuple-element.26.tiles_hbm, s32[32,128]{1,0:T(8,128)S(1)} %bitcast.38), custom_call_target="tpu_custom_call" | custom-call | flops 2147483648 | bytes 4194304 | tf_op jit(solution)/shard_map/backward_own/pallas_call | solution.py:610
  86.4 1.2 %collective-permute-done.7 = bf16[4,4,16,128]{3,2,1,0:T(8,128)(2,1)S(1)} collective-permute-done((bf16[4,4,16,128]{3,2,1,0:T(8,128)(2,1)S(1)}, bf16[4,4,16,128]{3,2,1,0:T(8,128)(2,1)S(1)}, u32[]{:S(2)}, u32[]{:S(2)}) %collective-permute-start.7) | collective-permute-done | bytes 65568 | tf_op jit(solution)/shard_map/activated/ppermute | solution.py:47
  88.9 2.1 %collective-permute-start.9 = (bf16[2,4,16,128]{3,2,1,0:T(8,128)(2,1)S(1)}, bf16[2,4,16,128]{3,2,1,0:T(8,128)(2,1)S(1)}, u32[]{:S(2)}, u32[]{:S(2)}) collective-permute-start(bf16[2,4,16,128]{3,2,1,0:T(8,128)(2,1)S(1)} %get-tuple-element.43), channel_id=1, source_target_pairs={{0,4},{1,5},{2,6},{3,7},{4,0},{5,1},{6,2},{7,3},{8,12},{9,13},{10,... | collective-permute-start | bytes 98312 | tf_op jit(solution)/shard_map/activated/ppermute | solution.py:54
  91.5 3.4 %all-to-all-done.4.got_ref = bf16[8,33,16,128]{3,2,1,0:T(8,128)(2,1)S(1)} async-done(((bf16[8,33,16,128]{3,2,1,0:T(8,128)(2,1)}), bf16[8,33,16,128]{3,2,1,0:T(8,128)(2,1)S(1)}, u32[]{:S(2)}, u32[]{:S(2)}) %all-to-all-start.4) | async-done | bytes 1081376 | tf_op jit(solution)/shard_map/backward/all_to_all | solution.py:491
  94.9 1.8 %relay.1 = (f32[33,16,128]{2,1,0:T(8,128)S(1)}, bf16[34,16,128]{2,1,0:T(8,128)(2,1)S(1)}, bf16[34,16,128]{2,1,0:T(8,128)(2,1)S(1)}, bf16[34,16,128]{2,1,0:T(8,128)(2,1)S(1)}) custom-call(s32[1]{0:T(128)} %bitcast.3.here_ref.turn_ref, s32[8,4,128]{2,1,0:T(4,128)S(1)} %all-to-all-done.asked_ref, bf16[8,33,16,128]{3,2,1,0:T(8,128)(2,1)S(1)} %all-to-all-done.4.got_ref), custom_call_target="tpu_custom_call" | custom-call | tf_op jit(solution)/shard_map/relay/pallas_call | solution.py:643
  96.7 2.8 %collective-permute-start.11 = (bf16[34,16,128]{2,1,0:T(8,128)(2,1)S(1)}, bf16[34,16,128]{2,1,0:T(8,128)(2,1)S(1)}, u32[]{:S(2)}, u32[]{:S(2)}) collective-permute-start(bf16[34,16,128]{2,1,0:T(8,128)(2,1)S(1)} %get-tuple-element.34), channel_id=1, source_target_pairs={{0,16},{8,24},{16,32},{24,40},{32,48},{40,56},{48,0},{56,8},{64,80... | collective-permute-start | bytes 417800 | tf_op jit(solution)/shard_map/relay/ppermute | solution.py:63
  99.5 2.3 %collective-permute-start.12 = (bf16[34,16,128]{2,1,0:T(8,128)(2,1)S(1)}, bf16[34,16,128]{2,1,0:T(8,128)(2,1)S(1)}, u32[]{:S(2)}, u32[]{:S(2)}) collective-permute-start(bf16[34,16,128]{2,1,0:T(8,128)(2,1)S(1)} %get-tuple-element.35), channel_id=1, source_target_pairs={{0,32},{8,40},{16,48},{24,56},{32,0},{40,8},{48,16},{56,24},{64,96... | collective-permute-start | bytes 417800 | tf_op jit(solution)/shard_map/relay/ppermute | solution.py:63
  101.9 2.8 %collective-permute-start.13 = (bf16[34,16,128]{2,1,0:T(8,128)(2,1)S(1)}, bf16[34,16,128]{2,1,0:T(8,128)(2,1)S(1)}, u32[]{:S(2)}, u32[]{:S(2)}) collective-permute-start(bf16[34,16,128]{2,1,0:T(8,128)(2,1)S(1)} %get-tuple-element.36), channel_id=1, source_target_pairs={{0,48},{8,56},{16,0},{24,8},{32,16},{40,24},{48,32},{56,40},{64,11... | collective-permute-start | bytes 417800 | tf_op jit(solution)/shard_map/relay/ppermute | solution.py:63
  106.2 3.2 %collective-permute-done.11.one_ref = bf16[34,16,128]{2,1,0:T(8,128)(2,1)S(1)} collective-permute-done((bf16[34,16,128]{2,1,0:T(8,128)(2,1)S(1)}, bf16[34,16,128]{2,1,0:T(8,128)(2,1)S(1)}, u32[]{:S(2)}, u32[]{:S(2)}) %collective-permute-start.11) | collective-permute-done | bytes 139296 | tf_op jit(solution)/shard_map/relay/ppermute | solution.py:63
  109.4 3.5 %collective-permute-done.12.two_ref = bf16[34,16,128]{2,1,0:T(8,128)(2,1)S(1)} collective-permute-done((bf16[34,16,128]{2,1,0:T(8,128)(2,1)S(1)}, bf16[34,16,128]{2,1,0:T(8,128)(2,1)S(1)}, u32[]{:S(2)}, u32[]{:S(2)}) %collective-permute-start.12) | collective-permute-done | bytes 139296 | tf_op jit(solution)/shard_map/relay/ppermute | solution.py:63
  112.9 3.4 %collective-permute-done.13.three_ref = bf16[34,16,128]{2,1,0:T(8,128)(2,1)S(1)} collective-permute-done((bf16[34,16,128]{2,1,0:T(8,128)(2,1)S(1)}, bf16[34,16,128]{2,1,0:T(8,128)(2,1)S(1)}, u32[]{:S(2)}, u32[]{:S(2)}) %collective-permute-start.13) | collective-permute-done | bytes 139296 | tf_op jit(solution)/shard_map/relay/ppermute | solution.py:63
  116.2 2.4 %final.1 = (bf16[16,4096]{1,0:T(8,128)(2,1)}, f32[16,128]{1,0:T(8,128)}) custom-call(f32[32,16,128]{2,1,0:T(8,128)} %get-tuple-element.32.kept_hbm, f32[33,16,128]{2,1,0:T(8,128)S(1)} %get-tuple-element.33.own_ref, bf16[34,16,128]{2,1,0:T(8,128)(2,1)S(1)} %collective-permute-done.11.one_ref, bf16[34,16,128]{2,1,0:T(8,128)(2,1)S(1)} %collective-permute-done.12.two_ref, ...), custom_call_target="tpu_custom_call" | custom-call | tf_op jit(solution)/shard_map/final/pallas_call | solution.py:655
  (39 shorter events, 7.9 us)
Async XLA Ops:
  0.6 0.9 copy-start.3
  1.5 0.7 copy-start.4
  3.7 29.1 %copy-start.2 = (s32[128]{0:T(128)S(1)}, s32[128]{0:T(128)}, u32[]{:S(2)}) copy-start(s32[128]{0:T(128)} %param.10) | copy-start | bytes 1540
  3.7 29.1 %copy-start.6 = (s32[128]{0:T(128)S(1)}, s32[128]{0:T(128)}, u32[]{:S(2)}) copy-start(s32[128]{0:T(128)} %param.9) | copy-start | bytes 1540
  3.7 21.9 %collective-permute-start = (bf16[32,16,128]{2,1,0:T(8,128)(2,1)S(1)}, bf16[32,16,128]{2,1,0:T(8,128)(2,1)S(1)}, u32[]{:S(2)}, u32[]{:S(2)}) collective-permute-start(bf16[32,16,128]{2,1,0:T(8,128)(2,1)S(1)} %permute.1.refs_0_.own_ref), channel_id=1, source_target_pairs={{0,48},{8,56},{16,0},{24,8},{32,16},{40,24},{48,32},{56,40},{64,11... | collective-permute-start | bytes 393224 | tf_op jit(solution)/shard_map/permute/ppermute | solution.py:63
  10.1 15.5 %collective-permute-start.1 = (bf16[32,16,128]{2,1,0:T(8,128)(2,1)S(1)}, bf16[32,16,128]{2,1,0:T(8,128)(2,1)S(1)}, u32[]{:S(2)}, u32[]{:S(2)}) collective-permute-start(bf16[32,16,128]{2,1,0:T(8,128)(2,1)S(1)} %permute.1.refs_0_.own_ref), channel_id=1, source_target_pairs={{0,32},{8,40},{16,48},{24,56},{32,0},{40,8},{48,16},{56,24},{64,96... | collective-permute-start | bytes 393224 | tf_op jit(solution)/shard_map/permute/ppermute | solution.py:63
  11.0 14.5 %collective-permute-start.2 = (bf16[32,16,128]{2,1,0:T(8,128)(2,1)S(1)}, bf16[32,16,128]{2,1,0:T(8,128)(2,1)S(1)}, u32[]{:S(2)}, u32[]{:S(2)}) collective-permute-start(bf16[32,16,128]{2,1,0:T(8,128)(2,1)S(1)} %permute.1.refs_0_.own_ref), channel_id=1, source_target_pairs={{0,16},{8,24},{16,32},{24,40},{32,48},{40,56},{48,0},{56,8},{64,80... | collective-permute-start | bytes 393224 | tf_op jit(solution)/shard_map/permute/ppermute | solution.py:63
  15.5 10.1 %all-to-all-start = ((s32[8,4,128]{2,1,0:T(4,128)}), s32[8,4,128]{2,1,0:T(4,128)S(1)}, u32[]{:S(2)}, u32[]{:S(2)}) async-start(s32[8,4,128]{2,1,0:T(4,128)} %index.3), calls=%async_computation | async-start | bytes 32768 | tf_op jit(solution)/shard_map/index/all_to_all | solution.py:491
  27.8 20.6 %all-to-all-start.1 = ((bf16[8,32,16,128]{3,2,1,0:T(8,128)(2,1)}), bf16[8,32,16,128]{3,2,1,0:T(8,128)(2,1)S(1)}, u32[]{:S(2)}, u32[]{:S(2)}) async-start(bf16[8,32,16,128]{3,2,1,0:T(8,128)(2,1)} %pack.1), calls=%async_computation.1 | async-start | bytes 2097152 | tf_op jit(solution)/shard_map/pack/all_to_all | solution.py:491
  33.3 5.1 %copy-start = (bf16[16,4096]{1,0:T(8,128)(2,1)S(1)}, bf16[16,4096]{1,0:T(8,128)(2,1)}, u32[]{:S(2)}) copy-start(bf16[16,4096]{1,0:T(8,128)(2,1)} %grad_ref) | copy-start | bytes 393220
  38.5 1.3 %collective-permute-start.3 = (bf16[4,4,16,128]{3,2,1,0:T(8,128)(2,1)S(1)}, bf16[4,4,16,128]{3,2,1,0:T(8,128)(2,1)S(1)}, u32[]{:S(2)}, u32[]{:S(2)}) collective-permute-start(bf16[4,4,16,128]{3,2,1,0:T(8,128)(2,1)S(1)} %get-tuple-element.51), channel_id=1, source_target_pairs={{0,1},{1,0},{2,3},{3,2},{4,5},{5,4},{6,7},{7,6},{8,9},{9,8},{10,11... | collective-permute-start | bytes 196616 | tf_op jit(solution)/shard_map/grads/ppermute | solution.py:47
  39.9 5.9 %collective-permute-start.4 = (bf16[2,4,16,128]{3,2,1,0:T(8,128)(2,1)S(1)}, bf16[2,4,16,128]{3,2,1,0:T(8,128)(2,1)S(1)}, u32[]{:S(2)}, u32[]{:S(2)}) collective-permute-start(bf16[2,4,16,128]{3,2,1,0:T(8,128)(2,1)S(1)} %get-tuple-element.48), channel_id=1, source_target_pairs={{0,2},{1,3},{2,4},{3,5},{4,6},{5,7},{6,0},{7,1},{8,10},{9,11},{10,... | collective-permute-start | bytes 98312 | tf_op jit(solution)/shard_map/grads/ppermute | solution.py:54
  41.6 5.4 %collective-permute-start.5 = (bf16[2,4,16,128]{3,2,1,0:T(8,128)(2,1)S(1)}, bf16[2,4,16,128]{3,2,1,0:T(8,128)(2,1)S(1)}, u32[]{:S(2)}, u32[]{:S(2)}) collective-permute-start(bf16[2,4,16,128]{3,2,1,0:T(8,128)(2,1)S(1)} %get-tuple-element.49), channel_id=1, source_target_pairs={{0,4},{1,5},{2,6},{3,7},{4,0},{5,1},{6,2},{7,3},{8,12},{9,13},{10,... | collective-permute-start | bytes 98312 | tf_op jit(solution)/shard_map/grads/ppermute | solution.py:54
  44.5 3.9 %collective-permute-start.6 = (bf16[2,4,16,128]{3,2,1,0:T(8,128)(2,1)S(1)}, bf16[2,4,16,128]{3,2,1,0:T(8,128)(2,1)S(1)}, u32[]{:S(2)}, u32[]{:S(2)}) collective-permute-start(bf16[2,4,16,128]{3,2,1,0:T(8,128)(2,1)S(1)} %get-tuple-element.50), channel_id=1, source_target_pairs={{0,6},{1,7},{2,0},{3,1},{4,2},{5,3},{6,4},{7,5},{8,14},{9,15},{10,... | collective-permute-start | bytes 98312 | tf_op jit(solution)/shard_map/grads/ppermute | solution.py:54
  48.4 12.7 %copy-start.1 = (bf16[128,128]{1,0:T(8,128)(2,1)S(1)}, bf16[128,128]{1,0:T(8,128)(2,1)}, u32[]{:S(2)}) copy-start(bf16[128,128]{1,0:T(8,128)(2,1)} %weight_ref.1) | copy-start | bytes 98308
  75.2 6.0 %copy-start.5 = (s32[4096]{0:T(1024)S(1)}, s32[4096]{0:T(1024)}, u32[]{:S(2)}) copy-start(s32[4096]{0:T(1024)} %param.8) | copy-start | bytes 49156
  75.2 19.7 %all-to-all-start.4 = ((bf16[8,33,16,128]{3,2,1,0:T(8,128)(2,1)}), bf16[8,33,16,128]{3,2,1,0:T(8,128)(2,1)S(1)}, u32[]{:S(2)}, u32[]{:S(2)}) async-start(bf16[8,33,16,128]{3,2,1,0:T(8,128)(2,1)} %backward.1), calls=%async_computation.4 | async-start | bytes 2162688 | tf_op jit(solution)/shard_map/backward/all_to_all | solution.py:491
  81.2 5.1 %copy-start.7 = (bf16[8,4,16,128]{3,2,1,0:T(8,128)(2,1)S(1)}, bf16[8,4,16,128]{3,2,1,0:T(8,128)(2,1)}, u32[]{:S(2)}) copy-start(bf16[8,4,16,128]{3,2,1,0:T(8,128)(2,1)} %get-tuple-element.31) | copy-start | bytes 393220
  86.3 1.3 %collective-permute-start.7 = (bf16[4,4,16,128]{3,2,1,0:T(8,128)(2,1)S(1)}, bf16[4,4,16,128]{3,2,1,0:T(8,128)(2,1)S(1)}, u32[]{:S(2)}, u32[]{:S(2)}) collective-permute-start(bf16[4,4,16,128]{3,2,1,0:T(8,128)(2,1)S(1)} %get-tuple-element.45), channel_id=1, source_target_pairs={{0,1},{1,0},{2,3},{3,2},{4,5},{5,4},{6,7},{7,6},{8,9},{9,8},{10,11... | collective-permute-start | bytes 196616 | tf_op jit(solution)/shard_map/activated/ppermute | solution.py:47
  88.3 13.6 %collective-permute-start.8 = (bf16[2,4,16,128]{3,2,1,0:T(8,128)(2,1)}, bf16[2,4,16,128]{3,2,1,0:T(8,128)(2,1)S(1)}, u32[]{:S(2)}, u32[]{:S(2)}) collective-permute-start(bf16[2,4,16,128]{3,2,1,0:T(8,128)(2,1)} %get-tuple-element.42), channel_id=1, source_target_pairs={{0,2},{1,3},{2,4},{3,5},{4,6},{5,7},{6,0},{7,1},{8,10},{9,11},{10,... | collective-permute-start | bytes 98312 | tf_op jit(solution)/shard_map/activated/ppermute | solution.py:54
  88.9 15.8 %collective-permute-start.9 = (bf16[2,4,16,128]{3,2,1,0:T(8,128)(2,1)S(1)}, bf16[2,4,16,128]{3,2,1,0:T(8,128)(2,1)S(1)}, u32[]{:S(2)}, u32[]{:S(2)}) collective-permute-start(bf16[2,4,16,128]{3,2,1,0:T(8,128)(2,1)S(1)} %get-tuple-element.43), channel_id=1, source_target_pairs={{0,4},{1,5},{2,6},{3,7},{4,0},{5,1},{6,2},{7,3},{8,12},{9,13},{10,... | collective-permute-start | bytes 98312 | tf_op jit(solution)/shard_map/activated/ppermute | solution.py:54
  90.9 13.8 %collective-permute-start.10 = (bf16[2,4,16,128]{3,2,1,0:T(8,128)(2,1)S(1)}, bf16[2,4,16,128]{3,2,1,0:T(8,128)(2,1)}, u32[]{:S(2)}, u32[]{:S(2)}) collective-permute-start(bf16[2,4,16,128]{3,2,1,0:T(8,128)(2,1)S(1)} %get-tuple-element.44), channel_id=1, source_target_pairs={{0,6},{1,7},{2,0},{3,1},{4,2},{5,3},{6,4},{7,5},{8,14},{9,15},{10,... | collective-permute-start | bytes 98312 | tf_op jit(solution)/shard_map/activated/ppermute | solution.py:54
  96.7 12.7 %collective-permute-start.11 = (bf16[34,16,128]{2,1,0:T(8,128)(2,1)S(1)}, bf16[34,16,128]{2,1,0:T(8,128)(2,1)S(1)}, u32[]{:S(2)}, u32[]{:S(2)}) collective-permute-start(bf16[34,16,128]{2,1,0:T(8,128)(2,1)S(1)} %get-tuple-element.34), channel_id=1, source_target_pairs={{0,16},{8,24},{16,32},{24,40},{32,48},{40,56},{48,0},{56,8},{64,80... | collective-permute-start | bytes 417800 | tf_op jit(solution)/shard_map/relay/ppermute | solution.py:63
  99.5 13.4 %collective-permute-start.12 = (bf16[34,16,128]{2,1,0:T(8,128)(2,1)S(1)}, bf16[34,16,128]{2,1,0:T(8,128)(2,1)S(1)}, u32[]{:S(2)}, u32[]{:S(2)}) collective-permute-start(bf16[34,16,128]{2,1,0:T(8,128)(2,1)S(1)} %get-tuple-element.35), channel_id=1, source_target_pairs={{0,32},{8,40},{16,48},{24,56},{32,0},{40,8},{48,16},{56,24},{64,96... | collective-permute-start | bytes 417800 | tf_op jit(solution)/shard_map/relay/ppermute | solution.py:63
  101.9 14.4 %collective-permute-start.13 = (bf16[34,16,128]{2,1,0:T(8,128)(2,1)S(1)}, bf16[34,16,128]{2,1,0:T(8,128)(2,1)S(1)}, u32[]{:S(2)}, u32[]{:S(2)}) collective-permute-start(bf16[34,16,128]{2,1,0:T(8,128)(2,1)S(1)} %get-tuple-element.36), channel_id=1, source_target_pairs={{0,48},{8,56},{16,0},{24,8},{32,16},{40,24},{48,32},{56,40},{64,11... | collective-permute-start | bytes 417800 | tf_op jit(solution)/shard_map/relay/ppermute | solution.py:63

commit v5 on v4

--- a/solution.py
+++ b/solution.py
@@ -89,13 +89,34 @@
     return lax.broadcasted_iota(I32, (n, n), 0) < lax.broadcasted_iota(I32, (n, n), 1)
 
 
-def want_kernel(col_hbm, want_ref, col_buf, sem):
-    copy = pltpu.make_async_copy(col_hbm, col_buf, sem)
-    copy.start()
-    copy.wait()
+def start_kernel(
+    row_hbm,
+    col_hbm,
+    features_hbm,
+    order_hbm,
+    want_hbm,
+    out_ref,
+    plan_ref,
+    row_ref,
+    col_ref,
+    features_ref,
+    order_ref,
+    want_ref,
+    blocked,
+    sems,
+):
+    copies = [
+        pltpu.make_async_copy(col_hbm, col_ref, sems.at[0]),
+        pltpu.make_async_copy(features_hbm, features_ref, sems.at[1]),
+        pltpu.make_async_copy(order_hbm, order_ref, sems.at[2]),
+        pltpu.make_async_copy(row_hbm, row_ref, sems.at[4]),
+    ]
+    for copy in copies:
+        copy.start()
+    copies[0].wait()
     relays, turns, _ = want_ref.shape
     peers = relays * turns
-    _, _, present, rank = ranks(col_buf[...], peers)
+    of_peer, of_block, present, rank = ranks(col_ref[...], peers)
     number = lax.broadcasted_iota(I32, (peers, 32), 1).astype(F32)
     lane = lax.broadcasted_iota(I32, (peers, 128), 1)
     want = jnp.zeros((peers, 128), F32)
@@ -107,12 +128,17 @@
     want = want.astype(I32)
     for m in range(relays):
         want_ref[m] = want[m * turns : (m + 1) * turns, :]
-
-
-def plan_kernel(peers, row_ref, col_ref, plan_ref):
-    col, row = col_ref[...], row_ref[...]
+    store = pltpu.make_async_copy(want_ref, want_hbm, sems.at[3])
+    store.start()
+    for copy in copies[1:]:
+        copy.wait()
+    plan_ref[...] = lay_out(peers, row_ref[...], col_ref[...], of_peer, of_block, rank)
+    permute(features_ref, order_ref, out_ref, blocked)
+    store.wait()
+
+
+def lay_out(peers, row, col, of_peer, of_block, rank):
     tiles = col.shape[1]
-    of_peer, of_block, _, rank = ranks(col, peers)
     rank_of = dot(rank.astype(BF16), of_peer.astype(BF16), TN)
     tile_rank = jnp.sum(rank_of * of_block, axis=0, keepdims=True)
     own = ((col >> 5) == (row >> 5)).astype(F32)
@@ -155,7 +181,7 @@
         ],
         axis=0,
     )
-    plan_ref[...] = plan.astype(I32)
+    return plan.astype(I32)
 
 
 def pick_lanes(blocked, pick, high):
@@ -167,7 +193,7 @@
     return total.astype(BF16)
 
 
-def permute_kernel(features_ref, order_ref, out_ref, blocked):
+def permute(features_ref, order_ref, out_ref, blocked):
     count = order_ref.shape[0]
     width = features_ref.shape[0]
     for s in range(count):
@@ -291,7 +317,7 @@
     weight = weight_ref[...]
     weight_t = weight.astype(F32).T.astype(BF16)
     part = jnp.zeros((inputs, inputs), F32)
-    stores = []
+    stores, pre_grads = [], []
     for b in range(per):
         agg = got_ref[:, b].reshape(inputs, 128)
         grad = grads[:, b].reshape(inputs, 128).astype(F32)
@@ -299,13 +325,15 @@
         logistic = jax.nn.sigmoid(pre)
         act = (pre * logistic).astype(BF16)
         pre_grad = (grad * logistic * (1.0 + pre * (1.0 - logistic))).astype(BF16)
-        agg_grad = dot(weight, pre_grad, NN).astype(BF16)
-        part = part + dot(pre_grad, agg, NT)
-        out_ref[:, b] = agg_grad.reshape(groups, width, 128)
+        pre_grads.append(pre_grad)
         act_ref[:, b] = act.reshape(groups, width, 128)
         store = pltpu.make_async_copy(act_ref.at[:, b], act_hbm.at[:, b], sems.at[b])
         store.start()
         stores.append(store)
+    for b, pre_grad in enumerate(pre_grads):
+        agg_grad = dot(weight, pre_grad, NN).astype(BF16)
+        part = part + dot(pre_grad, got_ref[:, b].reshape(inputs, 128), NT)
+        out_ref[:, b] = agg_grad.reshape(groups, width, 128)
     high = part.astype(BF16)
     out_ref[:, per] = high.reshape(groups, width, 128)
     out_ref[:, per + 1] = (part - high.astype(F32)).astype(BF16).reshape(groups, width, 128)
@@ -490,37 +518,31 @@
     ]
     swap = lambda v: lax.all_to_all(v, "rows", 0, 0, tiled=True, axis_index_groups=near)
 
-    with jax.named_scope("permute"):
-        own = pl.pallas_call(
-            permute_kernel,
-            out_shape=shape((count, width, size), BF16),
-            in_specs=[VMEM, VMEM],
-            out_specs=VMEM,
-            scratch_shapes=[pltpu.VMEM((count * width, size), BF16)],
-            compiler_params=params(),
-            cost_estimate=cost(1 << 31, 1 << 22),
-        )(features, order)
-        held = [own] + [along(own, -2 * far, peers) for far in range(1, turns)]
-
-    with jax.named_scope("index"):
+    with jax.named_scope("start"):
         rows, cols = tile_row.reshape(1, tiles), tile_col.reshape(1, tiles)
-        want = pl.pallas_call(
-            want_kernel,
-            out_shape=shape((relays, turns, 128), I32),
-            in_specs=[HBM],
-            out_specs=VMEM,
-            scratch_shapes=[pltpu.VMEM((1, tiles), I32), pltpu.SemaphoreType.DMA],
-            compiler_params=params(),
-        )(in_hbm(cols))
+        want, own, plan = pl.pallas_call(
+            start_kernel,
+            out_shape=(
+                pltpu.HBM((relays, turns, 128), I32),
+                shape((count, width, size), BF16),
+                shape((8, tiles), I32),
+            ),
+            in_specs=[HBM] * 4,
+            out_specs=(HBM, VMEM, VMEM),
+            scratch_shapes=[
+                pltpu.VMEM((1, tiles), I32),
+                pltpu.VMEM((1, tiles), I32),
+                pltpu.VMEM((width, span), BF16),
+                pltpu.VMEM((count, size), I32),
+                pltpu.VMEM((relays, turns, 128), I32),
+                pltpu.VMEM((count * width, size), BF16),
+                pltpu.SemaphoreType.DMA((5,)),
+            ],
+            compiler_params=params(),
+        )(in_hbm(rows), in_hbm(cols), in_hbm(features), in_hbm(order))
+        held = [own] + [along(own, -2 * far, peers) for far in (2, 1, 3)]
+        held = [held[0], held[2], held[1], held[3]]
         asked = swap(want)
-        plan = pl.pallas_call(
-            functools.partial(plan_kernel, peers),
-            out_shape=shape((8, tiles), I32),
-            in_specs=[VMEM, VMEM],
-            out_specs=VMEM,
-            compiler_params=params(),
-            cost_estimate=cost(1 << 30, 1 << 21),
-        )(rows, cols)
 
     with jax.named_scope("pack"):
         send = pl.pallas_call(
@@ -534,6 +556,9 @@
             ],
             compiler_params=params(),
         )(turn_at, asked, *held)
+    with jax.named_scope("grads"):
+        here = lax.axis_index("cols")
+        grad_out, send = lax.optimization_barrier((grad_out, send))
         got = swap(send)
 
     with jax.named_scope("forward_own"):
@@ -548,8 +573,6 @@
         )(plan, own, in_hbm(tile_vals))
 
     with jax.named_scope("grads"):
-        here = lax.axis_index("cols")
-        grad_out, part = lax.optimization_barrier((grad_out, part))
         grads = pl.pallas_call(
             blocks_kernel,
             out_shape=shape((groups, per, width, size), BF16),
@@ -649,7 +672,8 @@
             scratch_shapes=[pltpu.VMEM((turns * count, width, size), F32)] * WAYS,
             compiler_params=params(),
         )(turn_at, asked, parts)
-        sums_of = [along(v, 2 * far, peers) for far, v in enumerate(sums_of)]
+        passed = {far: along(sums_of[far], 2 * far, peers) for far in (2, 1, 3)}
+        sums_of = [sums_of[0]] + [passed[far] for far in (1, 2, 3)]
 
     with jax.named_scope("final"):
         feat_grads, weight_grad = pl.pallas_call(

time: 120 us -> 116 us (0.967); the launches traced: 119 us -> 116 us
  local copies, waits for them, and re-layouts: 1.68 us -> 0.05 us
  waiting for transfers between devices: 23.1 us -> 21.6 us
    ppermute x6, waiting for transfers between devices: 2.57 us -> 0.02 us  [over_cols(): part = lax.ppermute(part, 'cols', pairs)]
    all_to_all x3, waiting for transfers between devices: 8.11 us -> 10.2 us  [shards(): lax.all_to_all(v, 'rows', 0, 0, tiled=True, axis_index_groups=near)]
    ppermute x6, starting transfers between devices: 18.2 us -> 20.1 us  [along(): return lax.ppermute(value, 'rows', pairs)]
    unnamed x16 -> x8, local copies, waits for them, and re-layouts: 1.65 us -> 0.02 us
    pallas_call x3 -> x1, Pallas kernels: 3.56 us -> 2.68 us  [shards(): pl.pallas_call(start_kernel, out_shape=(pltpu.HBM((relays, turns, 128), I...]
  transfers between devices with their start and end apart: 17 -> 17, of which waited for: 9 -> 7; matrix products, arithmetic and copies ran while one was open for 1% -> 1% of each run, Pallas kernels for 13% -> 10%
where the time goes in v5:
time: 116 us
  starting transfers between devices  44.9 us (39%)
  Pallas kernels  27.5 us (24%)
  waiting for transfers between devices  21.6 us (19%)
  blocking collectives  19.6 us (17%)
  other arithmetic  1.44 us (1%)
    ppermute x6, starting transfers between devices, along(): return lax.ppermute(value, 'rows', pairs)  20.1 us
    all_to_all x3, starting transfers between devices, shards(): lax.all_to_all(v, 'rows', 0, 0, tiled=True, axis_index_groups=near)  15.5 us
    all_to_all x1, blocking collectives, shards(): mixed = lax.all_to_all(mixed, 'cols', 0, 0, tiled=True)  10.4 us
    all_to_all x3, waiting for transfers between devices, shards(): lax.all_to_all(v, 'rows', 0, 0, tiled=True, axis_index_groups=near)  10.2 us
    all_to_all x1, blocking collectives, shards(): back = lax.all_to_all(back, 'cols', 0, 0, tiled=True)  9.23 us
    ppermute x6, starting transfers between devices, over_cols(): part = lax.ppermute(part, 'cols', pairs)  9.15 us
    ppermute x6, waiting for transfers between devices, along(): return lax.ppermute(value, 'rows', pairs)  9.05 us
    pallas_call x1, Pallas kernels, shards(): pl.pallas_call(functools.partial(backward_own_kernel, peers * SLOTS), out...  4.8 us
  transfers between devices with their start and end apart: 17, of which 7 were waited for; matrix products, arithmetic and copies ran while one was open for 1% of the time, Pallas kernels for 10%

profile of v5, /device:TPU:2, one launch (start us, length us, event | category | flops | bytes accessed | tf_op | source)
XLA Modules:
  0.0 116.2 jit_solution(16007448357002329966)
XLA Ops:
  0.6 2.7 %start.1 = (s32[8,4,128]{2,1,0:T(4,128)}, bf16[32,16,128]{2,1,0:T(8,128)(2,1)S(1)}, s32[8,128]{1,0:T(8,128)S(1)}) custom-call(s32[1,128]{1,0:T(1,128)} %bitcast.45, s32[1,128]{1,0:T(1,128)} %bitcast.46, bf16[16,4096]{1,0:T(8,128)(2,1)} %features_hbm.1, s32[32,128]{1,0:T(8,128)} %bitcast.35), custom_call_target="tpu_custom_call" | custom-call | tf_op jit(solution)/shard_map/start/pallas_call | solution.py:523
  3.3 6.4 %collective-permute-start = (bf16[32,16,128]{2,1,0:T(8,128)(2,1)S(1)}, bf16[32,16,128]{2,1,0:T(8,128)(2,1)S(1)}, u32[]{:S(2)}, u32[]{:S(2)}) collective-permute-start(bf16[32,16,128]{2,1,0:T(8,128)(2,1)S(1)} %get-tuple-element.27.refs_0_.own_ref), channel_id=1, source_target_pairs={{0,48},{8,56},{16,0},{24,8},{32,16},{40,24},{48,32},{56,40},{64,11... | collective-permute-start | bytes 393224 | tf_op jit(solution)/shard_map/start/ppermute | solution.py:63
  9.7 1.0 collective-permute-start.1
  10.7 2.8 %collective-permute-start.2 = (bf16[32,16,128]{2,1,0:T(8,128)(2,1)S(1)}, bf16[32,16,128]{2,1,0:T(8,128)(2,1)S(1)}, u32[]{:S(2)}, u32[]{:S(2)}) collective-permute-start(bf16[32,16,128]{2,1,0:T(8,128)(2,1)S(1)} %get-tuple-element.27.refs_0_.own_ref), channel_id=1, source_target_pairs={{0,16},{8,24},{16,32},{24,40},{32,48},{40,56},{48,0},{56,8},{64,80... | collective-permute-start | bytes 393224 | tf_op jit(solution)/shard_map/start/ppermute | solution.py:63
  13.5 5.3 %all-to-all-start = ((s32[8,4,128]{2,1,0:T(4,128)}), s32[8,4,128]{2,1,0:T(4,128)S(1)}, u32[]{:S(2)}, u32[]{:S(2)}) async-start(s32[8,4,128]{2,1,0:T(4,128)} %get-tuple-element.26), calls=%async_computation | async-start | bytes 32768 | tf_op jit(solution)/shard_map/start/all_to_all | solution.py:519
  18.8 4.8 %all-to-all-done.asked_ref = s32[8,4,128]{2,1,0:T(4,128)S(1)} async-done(((s32[8,4,128]{2,1,0:T(4,128)}), s32[8,4,128]{2,1,0:T(4,128)S(1)}, u32[]{:S(2)}, u32[]{:S(2)}) %all-to-all-start) | async-done | bytes 16416 | tf_op jit(solution)/shard_map/start/all_to_all | solution.py:519
  23.6 2.3 %pack.1 = bf16[8,32,16,128]{3,2,1,0:T(8,128)(2,1)} custom-call(s32[1]{0:T(128)} %bitcast.4.here_ref.turn_ref, s32[8,4,128]{2,1,0:T(4,128)S(1)} %all-to-all-done.asked_ref, bf16[32,16,128]{2,1,0:T(8,128)(2,1)S(1)} %get-tuple-element.27.refs_0_.own_ref, bf16[32,16,128]{2,1,0:T(8,128)(2,1)S(1)} %collective-permute-done.refs_1_, ...), custom_call_target="tpu_custom_call" | custom-call | tf_op jit(solution)/shard_map/pack/pallas_call | solution.py:548
  25.8 5.3 %all-to-all-start.1 = ((bf16[8,32,16,128]{3,2,1,0:T(8,128)(2,1)}), bf16[8,32,16,128]{3,2,1,0:T(8,128)(2,1)S(1)}, u32[]{:S(2)}, u32[]{:S(2)}) async-start(bf16[8,32,16,128]{3,2,1,0:T(8,128)(2,1)} %pack.1), calls=%async_computation.1 | async-start | bytes 2097152 | tf_op jit(solution)/shard_map/grads/all_to_all | solution.py:519
  31.4 1.1 collective-permute-done.3
  32.5 1.7 %collective-permute-start.4 = (bf16[2,4,16,128]{3,2,1,0:T(8,128)(2,1)S(1)}, bf16[2,4,16,128]{3,2,1,0:T(8,128)(2,1)S(1)}, u32[]{:S(2)}, u32[]{:S(2)}) collective-permute-start(bf16[2,4,16,128]{3,2,1,0:T(8,128)(2,1)S(1)} %get-tuple-element.54), channel_id=1, source_target_pairs={{0,2},{1,3},{2,4},{3,5},{4,6},{5,7},{6,0},{7,1},{8,10},{9,11},{10,... | collective-permute-start | bytes 98312 | tf_op jit(solution)/shard_map/grads/ppermute | solution.py:54
  34.2 2.9 %collective-permute-start.5 = (bf16[2,4,16,128]{3,2,1,0:T(8,128)(2,1)S(1)}, bf16[2,4,16,128]{3,2,1,0:T(8,128)(2,1)S(1)}, u32[]{:S(2)}, u32[]{:S(2)}) collective-permute-start(bf16[2,4,16,128]{3,2,1,0:T(8,128)(2,1)S(1)} %get-tuple-element.55), channel_id=1, source_target_pairs={{0,4},{1,5},{2,6},{3,7},{4,0},{5,1},{6,2},{7,3},{8,12},{9,13},{10,... | collective-permute-start | bytes 98312 | tf_op jit(solution)/shard_map/grads/ppermute | solution.py:54
  37.1 1.3 %collective-permute-start.6 = (bf16[2,4,16,128]{3,2,1,0:T(8,128)(2,1)S(1)}, bf16[2,4,16,128]{3,2,1,0:T(8,128)(2,1)S(1)}, u32[]{:S(2)}, u32[]{:S(2)}) collective-permute-start(bf16[2,4,16,128]{3,2,1,0:T(8,128)(2,1)S(1)} %get-tuple-element.56), channel_id=1, source_target_pairs={{0,6},{1,7},{2,0},{3,1},{4,2},{5,3},{6,4},{7,5},{8,14},{9,15},{10,... | collective-permute-start | bytes 98312 | tf_op jit(solution)/shard_map/grads/ppermute | solution.py:54
  38.4 4.7 %forward_own.1 = (f32[32,16,128]{2,1,0:T(8,128)S(1)}, bf16[128,128,128]{2,1,0:T(8,128)(2,1)}) custom-call(s32[8,128]{1,0:T(8,128)S(1)} %get-tuple-element.25.plan_ref, bf16[32,16,128]{2,1,0:T(8,128)(2,1)S(1)} %get-tuple-element.27.refs_0_.own_ref, bf16[128,128,128]{2,1,0:T(8,128)(2,1)} %tiles_hbm.1), custom_call_target="tpu_custom_call" | custom-call | flops 2147483648 | bytes 4194304 | tf_op jit(solution)/shard_map/forward_own/pallas_call | solution.py:565
  43.2 1.4 %all-to-all-done.1 = bf16[8,32,16,128]{3,2,1,0:T(8,128)(2,1)S(1)} async-done(((bf16[8,32,16,128]{3,2,1,0:T(8,128)(2,1)}), bf16[8,32,16,128]{3,2,1,0:T(8,128)(2,1)S(1)}, u32[]{:S(2)}, u32[]{:S(2)}) %all-to-all-start.1) | async-done | bytes 1048608 | tf_op jit(solution)/shard_map/grads/all_to_all | solution.py:519
  44.7 3.3 %forward.1 = bf16[8,4,16,128]{3,2,1,0:T(8,128)(2,1)S(1)} custom-call(s32[8,128]{1,0:T(8,128)S(1)} %get-tuple-element.25.plan_ref, bf16[256,16,128]{2,1,0:T(8,128)(2,1)S(1)} %bitcast.33, f32[32,16,128]{2,1,0:T(8,128)S(1)} %get-tuple-element.31.part_ref, bf16[128,128,128]{2,1,0:T(8,128)(2,1)} %get-tuple-element.32.tiles_hbm), custom_call_target="tpu_custom_call" | custom-call | flops 1073741824 | bytes 4194304 | tf_op jit(solution)/shard_map/forward/pallas_call | solution.py:587
  48.0 10.4 %all_to_all.25.got_ref = bf16[8,4,16,128]{3,2,1,0:T(8,128)(2,1)S(1)} all-to-all(bf16[8,4,16,128]{3,2,1,0:T(8,128)(2,1)S(1)} %forward.1), channel_id=1, replica_groups=mesh['rows'=32,'cols'=8] {'cols'}, dimensions={0} | all-to-all | bytes 262144 | tf_op jit(solution)/shard_map/forward/all_to_all | solution.py:596
  58.4 0.9 dense.1
  59.3 9.2 %all_to_all.26.got_ref = bf16[8,6,16,128]{3,2,1,0:T(8,128)(2,1)S(1)} all-to-all(bf16[8,6,16,128]{3,2,1,0:T(8,128)(2,1)S(1)} %get-tuple-element.35), channel_id=1, replica_groups=mesh['rows'=32,'cols'=8] {'cols'}, dimensions={0} | all-to-all | bytes 393216 | tf_op jit(solution)/shard_map/dense/all_to_all | solution.py:611
  68.6 3.9 %backward.1 = bf16[8,33,16,128]{3,2,1,0:T(8,128)(2,1)} custom-call(s32[8,128]{1,0:T(8,128)S(1)} %get-tuple-element.25.plan_ref, bf16[8,6,16,128]{3,2,1,0:T(8,128)(2,1)S(1)} %all_to_all.26.got_ref, bf16[128,128,128]{2,1,0:T(8,128)(2,1)} %get-tuple-element.32.tiles_hbm), custom_call_target="tpu_custom_call" | custom-call | flops 1073741824 | bytes 4194304 | tf_op jit(solution)/shard_map/backward/pallas_call | solution.py:614
  72.5 4.9 %all-to-all-start.4 = ((bf16[8,33,16,128]{3,2,1,0:T(8,128)(2,1)}), bf16[8,33,16,128]{3,2,1,0:T(8,128)(2,1)S(1)}, u32[]{:S(2)}, u32[]{:S(2)}) async-start(bf16[8,33,16,128]{3,2,1,0:T(8,128)(2,1)} %backward.1), calls=%async_computation.4 | async-start | bytes 2162688 | tf_op jit(solution)/shard_map/backward/all_to_all | solution.py:519
  77.4 4.8 %backward_own.1 = (f32[32,16,128]{2,1,0:T(8,128)}, s32[32,128]{1,0:T(8,128)S(1)}, bf16[256,4096]{1,0:T(8,128)(2,1)S(1)}) custom-call(s32[8,128]{1,0:T(8,128)S(1)} %get-tuple-element.25.plan_ref, bf16[8,6,16,128]{3,2,1,0:T(8,128)(2,1)S(1)} %all_to_all.26.got_ref, bf16[128,128,128]{2,1,0:T(8,128)(2,1)} %get-tuple-element.32.tiles_hbm, s32[32,128]{1,0:T(8,128)S(1)} %bitcast.36), custom_call_target="tpu_custom_call" | custom-call | flops 2147483648 | bytes 4194304 | tf_op jit(solution)/shard_map/backward_own/pallas_call | solution.py:633
  82.4 1.2 %collective-permute-done.7 = bf16[4,4,16,128]{3,2,1,0:T(8,128)(2,1)S(1)} collective-permute-done((bf16[4,4,16,128]{3,2,1,0:T(8,128)(2,1)S(1)}, bf16[4,4,16,128]{3,2,1,0:T(8,128)(2,1)S(1)}, u32[]{:S(2)}, u32[]{:S(2)}) %collective-permute-start.7) | collective-permute-done | bytes 65568 | tf_op jit(solution)/shard_map/activated/ppermute | solution.py:47
  84.8 2.1 %collective-permute-start.9 = (bf16[2,4,16,128]{3,2,1,0:T(8,128)(2,1)S(1)}, bf16[2,4,16,128]{3,2,1,0:T(8,128)(2,1)S(1)}, u32[]{:S(2)}, u32[]{:S(2)}) collective-permute-start(bf16[2,4,16,128]{3,2,1,0:T(8,128)(2,1)S(1)} %get-tuple-element.49), channel_id=1, source_target_pairs={{0,4},{1,5},{2,6},{3,7},{4,0},{5,1},{6,2},{7,3},{8,12},{9,13},{10,... | collective-permute-start | bytes 98312 | tf_op jit(solution)/shard_map/activated/ppermute | solution.py:54
  87.5 3.9 %all-to-all-done.4.got_ref = bf16[8,33,16,128]{3,2,1,0:T(8,128)(2,1)S(1)} async-done(((bf16[8,33,16,128]{3,2,1,0:T(8,128)(2,1)}), bf16[8,33,16,128]{3,2,1,0:T(8,128)(2,1)S(1)}, u32[]{:S(2)}, u32[]{:S(2)}) %all-to-all-start.4) | async-done | bytes 1081376 | tf_op jit(solution)/shard_map/backward/all_to_all | solution.py:519
  91.4 1.8 %relay.1 = (f32[33,16,128]{2,1,0:T(8,128)S(1)}, bf16[34,16,128]{2,1,0:T(8,128)(2,1)S(1)}, bf16[34,16,128]{2,1,0:T(8,128)(2,1)S(1)}, bf16[34,16,128]{2,1,0:T(8,128)(2,1)S(1)}) custom-call(s32[1]{0:T(128)} %bitcast.4.here_ref.turn_ref, s32[8,4,128]{2,1,0:T(4,128)S(1)} %all-to-all-done.asked_ref, bf16[8,33,16,128]{3,2,1,0:T(8,128)(2,1)S(1)} %all-to-all-done.4.got_ref), custom_call_target="tpu_custom_call" | custom-call | tf_op jit(solution)/shard_map/relay/pallas_call | solution.py:666
  93.2 2.1 %collective-permute-start.11 = (bf16[34,16,128]{2,1,0:T(8,128)(2,1)S(1)}, bf16[34,16,128]{2,1,0:T(8,128)(2,1)S(1)}, u32[]{:S(2)}, u32[]{:S(2)}) collective-permute-start(bf16[34,16,128]{2,1,0:T(8,128)(2,1)S(1)} %get-tuple-element.40), channel_id=1, source_target_pairs={{0,16},{8,24},{16,32},{24,40},{32,48},{40,56},{48,0},{56,8},{64,80... | collective-permute-start | bytes 417800 | tf_op jit(solution)/shard_map/relay/ppermute | solution.py:63
  95.3 4.8 %collective-permute-start.12 = (bf16[34,16,128]{2,1,0:T(8,128)(2,1)S(1)}, bf16[34,16,128]{2,1,0:T(8,128)(2,1)S(1)}, u32[]{:S(2)}, u32[]{:S(2)}) collective-permute-start(bf16[34,16,128]{2,1,0:T(8,128)(2,1)S(1)} %get-tuple-element.41), channel_id=1, source_target_pairs={{0,32},{8,40},{16,48},{24,56},{32,0},{40,8},{48,16},{56,24},{64,96... | collective-permute-start | bytes 417800 | tf_op jit(solution)/shard_map/relay/ppermute | solution.py:63
  100.1 3.0 %collective-permute-start.13 = (bf16[34,16,128]{2,1,0:T(8,128)(2,1)S(1)}, bf16[34,16,128]{2,1,0:T(8,128)(2,1)S(1)}, u32[]{:S(2)}, u32[]{:S(2)}) collective-permute-start(bf16[34,16,128]{2,1,0:T(8,128)(2,1)S(1)} %get-tuple-element.42), channel_id=1, source_target_pairs={{0,48},{8,56},{16,0},{24,8},{32,16},{40,24},{48,32},{56,40},{64,11... | collective-permute-start | bytes 417800 | tf_op jit(solution)/shard_map/relay/ppermute | solution.py:63
  103.1 0.8 pad_maximum_fusion.1.got_ref
  104.6 1.2 %collective-permute-done.12.two_ref = bf16[34,16,128]{2,1,0:T(8,128)(2,1)S(1)} collective-permute-done((bf16[34,16,128]{2,1,0:T(8,128)(2,1)S(1)}, bf16[34,16,128]{2,1,0:T(8,128)(2,1)S(1)}, u32[]{:S(2)}, u32[]{:S(2)}) %collective-permute-start.12) | collective-permute-done | bytes 139296 | tf_op jit(solution)/shard_map/relay/ppermute | solution.py:63
  105.8 7.8 %collective-permute-done.13.three_ref = bf16[34,16,128]{2,1,0:T(8,128)(2,1)S(1)} collective-permute-done((bf16[34,16,128]{2,1,0:T(8,128)(2,1)S(1)}, bf16[34,16,128]{2,1,0:T(8,128)(2,1)S(1)}, u32[]{:S(2)}, u32[]{:S(2)}) %collective-permute-start.13) | collective-permute-done | bytes 139296 | tf_op jit(solution)/shard_map/relay/ppermute | solution.py:63
  113.6 2.4 %final.1 = (bf16[16,4096]{1,0:T(8,128)(2,1)}, f32[16,128]{1,0:T(8,128)}) custom-call(f32[32,16,128]{2,1,0:T(8,128)} %get-tuple-element.38.kept_hbm, f32[33,16,128]{2,1,0:T(8,128)S(1)} %get-tuple-element.39.own_ref, bf16[34,16,128]{2,1,0:T(8,128)(2,1)S(1)} %collective-permute-done.11.one_ref, bf16[34,16,128]{2,1,0:T(8,128)(2,1)S(1)} %collective-permute-done.12.two_ref, ...), custom_call_target="tpu_custom_call" | custom-call | tf_op jit(solution)/shard_map/final/pallas_call | solution.py:679
  (29 shorter events, 2.9 us)
Async XLA Ops:
  0.6 30.5 %copy-start = (bf16[16,4096]{1,0:T(8,128)(2,1)S(1)}, bf16[16,4096]{1,0:T(8,128)(2,1)}, u32[]{:S(2)}) copy-start(bf16[16,4096]{1,0:T(8,128)(2,1)} %grad_ref) | copy-start | bytes 393220
  3.3 20.2 %collective-permute-start = (bf16[32,16,128]{2,1,0:T(8,128)(2,1)S(1)}, bf16[32,16,128]{2,1,0:T(8,128)(2,1)S(1)}, u32[]{:S(2)}, u32[]{:S(2)}) collective-permute-start(bf16[32,16,128]{2,1,0:T(8,128)(2,1)S(1)} %get-tuple-element.27.refs_0_.own_ref), channel_id=1, source_target_pairs={{0,48},{8,56},{16,0},{24,8},{32,16},{40,24},{48,32},{56,40},{64,11... | collective-permute-start | bytes 393224 | tf_op jit(solution)/shard_map/start/ppermute | solution.py:63
  9.7 13.9 %collective-permute-start.1 = (bf16[32,16,128]{2,1,0:T(8,128)(2,1)S(1)}, bf16[32,16,128]{2,1,0:T(8,128)(2,1)S(1)}, u32[]{:S(2)}, u32[]{:S(2)}) collective-permute-start(bf16[32,16,128]{2,1,0:T(8,128)(2,1)S(1)} %get-tuple-element.27.refs_0_.own_ref), channel_id=1, source_target_pairs={{0,32},{8,40},{16,48},{24,56},{32,0},{40,8},{48,16},{56,24},{64,96... | collective-permute-start | bytes 393224 | tf_op jit(solution)/shard_map/start/ppermute | solution.py:63
  10.7 12.9 %collective-permute-start.2 = (bf16[32,16,128]{2,1,0:T(8,128)(2,1)S(1)}, bf16[32,16,128]{2,1,0:T(8,128)(2,1)S(1)}, u32[]{:S(2)}, u32[]{:S(2)}) collective-permute-start(bf16[32,16,128]{2,1,0:T(8,128)(2,1)S(1)} %get-tuple-element.27.refs_0_.own_ref), channel_id=1, source_target_pairs={{0,16},{8,24},{16,32},{24,40},{32,48},{40,56},{48,0},{56,8},{64,80... | collective-permute-start | bytes 393224 | tf_op jit(solution)/shard_map/start/ppermute | solution.py:63
  13.5 10.0 %all-to-all-start = ((s32[8,4,128]{2,1,0:T(4,128)}), s32[8,4,128]{2,1,0:T(4,128)S(1)}, u32[]{:S(2)}, u32[]{:S(2)}) async-start(s32[8,4,128]{2,1,0:T(4,128)} %get-tuple-element.26), calls=%async_computation | async-start | bytes 32768 | tf_op jit(solution)/shard_map/start/all_to_all | solution.py:519
  25.8 18.8 %all-to-all-start.1 = ((bf16[8,32,16,128]{3,2,1,0:T(8,128)(2,1)}), bf16[8,32,16,128]{3,2,1,0:T(8,128)(2,1)S(1)}, u32[]{:S(2)}, u32[]{:S(2)}) async-start(bf16[8,32,16,128]{3,2,1,0:T(8,128)(2,1)} %pack.1), calls=%async_computation.1 | async-start | bytes 2097152 | tf_op jit(solution)/shard_map/grads/all_to_all | solution.py:519
  31.2 1.3 %collective-permute-start.3 = (bf16[4,4,16,128]{3,2,1,0:T(8,128)(2,1)S(1)}, bf16[4,4,16,128]{3,2,1,0:T(8,128)(2,1)S(1)}, u32[]{:S(2)}, u32[]{:S(2)}) collective-permute-start(bf16[4,4,16,128]{3,2,1,0:T(8,128)(2,1)S(1)} %get-tuple-element.57), channel_id=1, source_target_pairs={{0,1},{1,0},{2,3},{3,2},{4,5},{5,4},{6,7},{7,6},{8,9},{9,8},{10,11... | collective-permute-start | bytes 196616 | tf_op jit(solution)/shard_map/grads/ppermute | solution.py:47
  32.5 10.6 %collective-permute-start.4 = (bf16[2,4,16,128]{3,2,1,0:T(8,128)(2,1)S(1)}, bf16[2,4,16,128]{3,2,1,0:T(8,128)(2,1)S(1)}, u32[]{:S(2)}, u32[]{:S(2)}) collective-permute-start(bf16[2,4,16,128]{3,2,1,0:T(8,128)(2,1)S(1)} %get-tuple-element.54), channel_id=1, source_target_pairs={{0,2},{1,3},{2,4},{3,5},{4,6},{5,7},{6,0},{7,1},{8,10},{9,11},{10,... | collective-permute-start | bytes 98312 | tf_op jit(solution)/shard_map/grads/ppermute | solution.py:54
  34.2 9.0 %collective-permute-start.5 = (bf16[2,4,16,128]{3,2,1,0:T(8,128)(2,1)S(1)}, bf16[2,4,16,128]{3,2,1,0:T(8,128)(2,1)S(1)}, u32[]{:S(2)}, u32[]{:S(2)}) collective-permute-start(bf16[2,4,16,128]{3,2,1,0:T(8,128)(2,1)S(1)} %get-tuple-element.55), channel_id=1, source_target_pairs={{0,4},{1,5},{2,6},{3,7},{4,0},{5,1},{6,2},{7,3},{8,12},{9,13},{10,... | collective-permute-start | bytes 98312 | tf_op jit(solution)/shard_map/grads/ppermute | solution.py:54
  37.1 6.1 %collective-permute-start.6 = (bf16[2,4,16,128]{3,2,1,0:T(8,128)(2,1)S(1)}, bf16[2,4,16,128]{3,2,1,0:T(8,128)(2,1)S(1)}, u32[]{:S(2)}, u32[]{:S(2)}) collective-permute-start(bf16[2,4,16,128]{3,2,1,0:T(8,128)(2,1)S(1)} %get-tuple-element.56), channel_id=1, source_target_pairs={{0,6},{1,7},{2,0},{3,1},{4,2},{5,3},{6,4},{7,5},{8,14},{9,15},{10,... | collective-permute-start | bytes 98312 | tf_op jit(solution)/shard_map/grads/ppermute | solution.py:54
  44.7 13.7 %copy-start.1 = (bf16[128,128]{1,0:T(8,128)(2,1)S(1)}, bf16[128,128]{1,0:T(8,128)(2,1)}, u32[]{:S(2)}) copy-start(bf16[128,128]{1,0:T(8,128)(2,1)} %weight_ref.1) | copy-start | bytes 98308
  72.5 4.9 %copy-start.2 = (s32[4096]{0:T(1024)S(1)}, s32[4096]{0:T(1024)}, u32[]{:S(2)}) copy-start(s32[4096]{0:T(1024)} %param.8) | copy-start | bytes 49156
  72.5 18.9 %all-to-all-start.4 = ((bf16[8,33,16,128]{3,2,1,0:T(8,128)(2,1)}), bf16[8,33,16,128]{3,2,1,0:T(8,128)(2,1)S(1)}, u32[]{:S(2)}, u32[]{:S(2)}) async-start(bf16[8,33,16,128]{3,2,1,0:T(8,128)(2,1)} %backward.1), calls=%async_computation.4 | async-start | bytes 2162688 | tf_op jit(solution)/shard_map/backward/all_to_all | solution.py:519
  77.4 4.8 %copy-start.3 = (bf16[8,4,16,128]{3,2,1,0:T(8,128)(2,1)S(1)}, bf16[8,4,16,128]{3,2,1,0:T(8,128)(2,1)}, u32[]{:S(2)}) copy-start(bf16[8,4,16,128]{3,2,1,0:T(8,128)(2,1)} %get-tuple-element.37) | copy-start | bytes 393220
  82.2 1.3 %collective-permute-start.7 = (bf16[4,4,16,128]{3,2,1,0:T(8,128)(2,1)S(1)}, bf16[4,4,16,128]{3,2,1,0:T(8,128)(2,1)S(1)}, u32[]{:S(2)}, u32[]{:S(2)}) collective-permute-start(bf16[4,4,16,128]{3,2,1,0:T(8,128)(2,1)S(1)} %get-tuple-element.51), channel_id=1, source_target_pairs={{0,1},{1,0},{2,3},{3,2},{4,5},{5,4},{6,7},{7,6},{8,9},{9,8},{10,11... | collective-permute-start | bytes 196616 | tf_op jit(solution)/shard_map/activated/ppermute | solution.py:47
  84.2 15.9 %collective-permute-start.8 = (bf16[2,4,16,128]{3,2,1,0:T(8,128)(2,1)}, bf16[2,4,16,128]{3,2,1,0:T(8,128)(2,1)S(1)}, u32[]{:S(2)}, u32[]{:S(2)}) collective-permute-start(bf16[2,4,16,128]{3,2,1,0:T(8,128)(2,1)} %get-tuple-element.48), channel_id=1, source_target_pairs={{0,2},{1,3},{2,4},{3,5},{4,6},{5,7},{6,0},{7,1},{8,10},{9,11},{10,... | collective-permute-start | bytes 98312 | tf_op jit(solution)/shard_map/activated/ppermute | solution.py:54
  84.8 18.3 %collective-permute-start.9 = (bf16[2,4,16,128]{3,2,1,0:T(8,128)(2,1)S(1)}, bf16[2,4,16,128]{3,2,1,0:T(8,128)(2,1)S(1)}, u32[]{:S(2)}, u32[]{:S(2)}) collective-permute-start(bf16[2,4,16,128]{3,2,1,0:T(8,128)(2,1)S(1)} %get-tuple-element.49), channel_id=1, source_target_pairs={{0,4},{1,5},{2,6},{3,7},{4,0},{5,1},{6,2},{7,3},{8,12},{9,13},{10,... | collective-permute-start | bytes 98312 | tf_op jit(solution)/shard_map/activated/ppermute | solution.py:54
  86.8 16.2 %collective-permute-start.10 = (bf16[2,4,16,128]{3,2,1,0:T(8,128)(2,1)S(1)}, bf16[2,4,16,128]{3,2,1,0:T(8,128)(2,1)}, u32[]{:S(2)}, u32[]{:S(2)}) collective-permute-start(bf16[2,4,16,128]{3,2,1,0:T(8,128)(2,1)S(1)} %get-tuple-element.50), channel_id=1, source_target_pairs={{0,6},{1,7},{2,0},{3,1},{4,2},{5,3},{6,4},{7,5},{8,14},{9,15},{10,... | collective-permute-start | bytes 98312 | tf_op jit(solution)/shard_map/activated/ppermute | solution.py:54
  93.2 11.4 %collective-permute-start.11 = (bf16[34,16,128]{2,1,0:T(8,128)(2,1)S(1)}, bf16[34,16,128]{2,1,0:T(8,128)(2,1)S(1)}, u32[]{:S(2)}, u32[]{:S(2)}) collective-permute-start(bf16[34,16,128]{2,1,0:T(8,128)(2,1)S(1)} %get-tuple-element.40), channel_id=1, source_target_pairs={{0,16},{8,24},{16,32},{24,40},{32,48},{40,56},{48,0},{56,8},{64,80... | collective-permute-start | bytes 417800 | tf_op jit(solution)/shard_map/relay/ppermute | solution.py:63
  95.3 10.5 %collective-permute-start.12 = (bf16[34,16,128]{2,1,0:T(8,128)(2,1)S(1)}, bf16[34,16,128]{2,1,0:T(8,128)(2,1)S(1)}, u32[]{:S(2)}, u32[]{:S(2)}) collective-permute-start(bf16[34,16,128]{2,1,0:T(8,128)(2,1)S(1)} %get-tuple-element.41), channel_id=1, source_target_pairs={{0,32},{8,40},{16,48},{24,56},{32,0},{40,8},{48,16},{56,24},{64,96... | collective-permute-start | bytes 417800 | tf_op jit(solution)/shard_map/relay/ppermute | solution.py:63
  100.1 13.5 %collective-permute-start.13 = (bf16[34,16,128]{2,1,0:T(8,128)(2,1)S(1)}, bf16[34,16,128]{2,1,0:T(8,128)(2,1)S(1)}, u32[]{:S(2)}, u32[]{:S(2)}) collective-permute-start(bf16[34,16,128]{2,1,0:T(8,128)(2,1)S(1)} %get-tuple-element.42), channel_id=1, source_target_pairs={{0,48},{8,56},{16,0},{24,8},{32,16},{40,24},{48,32},{56,40},{64,11... | collective-permute-start | bytes 417800 | tf_op jit(solution)/shard_map/relay/ppermute | solution.py:63

commit v6 on v5

--- a/solution.py
+++ b/solution.py
@@ -341,11 +341,10 @@
         store.wait()
 
 
-def backward_kernel(plan_ref, got_ref, tiles_hbm, send_hbm, prod, total, buf, sems, tiles, tile_sems):
+def backward_kernel(plan_ref, got_ref, tiles, send_hbm, prod, total, buf, sems):
     last = tiles.shape[0] // STEP
     begin = jnp.minimum(plan_ref[3, 0] // STEP, last - 1)
 
-    fetch_tiles(begin, last, tiles_hbm, tiles, tile_sems)
     groups = got_ref.shape[0]
     per = got_ref.shape[1] - 2
     relays = buf.shape[0]
@@ -362,7 +361,6 @@
         buf[m, each] = part
 
     def step(i, carry):
-        chunk_copy(tiles_hbm, tiles, tile_sems, i).wait()
         for u in range(STEP):
             r = plan_ref[2, i * STEP + u]
             prod[u] = dot(got_ref[r // per, r % per], tiles[i * STEP + u], NN)
@@ -614,19 +612,17 @@
         parts = pl.pallas_call(
             backward_kernel,
             out_shape=shape((relays, turns * SLOTS + 1, width, size), BF16),
-            in_specs=[SMEM, VMEM, HBM],
+            in_specs=[SMEM, VMEM, VMEM],
             out_specs=HBM,
             scratch_shapes=[
                 prod,
                 sums(peers * SLOTS),
                 pltpu.VMEM((relays, turns * SLOTS + 1, width, size), BF16),
                 pltpu.SemaphoreType.DMA((4,)),
-                tile_buf,
-                pltpu.SemaphoreType.DMA((tiles // STEP,)),
             ],
             compiler_params=params(),
             cost_estimate=cost(1 << 30, 1 << 22),
-        )(plan, back, in_hbm(tile_list))
+        )(plan, back, tile_list)
         parts = swap(parts)
 
     with jax.named_scope("backward_own"):

time: 116 us -> 115 us (level)
  no operation moved by 1% of the time
where the time goes in v6:
time: 115 us
  starting transfers between devices  44.9 us (39%)
  Pallas kernels  26.8 us (23%)
  waiting for transfers between devices  21.4 us (19%)
  blocking collectives  19.6 us (17%)
  other arithmetic  1.44 us (1%)
    ppermute x6, starting transfers between devices, along(): return lax.ppermute(value, 'rows', pairs)  20.1 us
    all_to_all x3, starting transfers between devices, shards(): lax.all_to_all(v, 'rows', 0, 0, tiled=True, axis_index_groups=near)  15.5 us
    all_to_all x1, blocking collectives, shards(): mixed = lax.all_to_all(mixed, 'cols', 0, 0, tiled=True)  10.4 us
    all_to_all x3, waiting for transfers between devices, shards(): lax.all_to_all(v, 'rows', 0, 0, tiled=True, axis_index_groups=near)  10.2 us
    all_to_all x1, blocking collectives, shards(): back = lax.all_to_all(back, 'cols', 0, 0, tiled=True)  9.23 us
    ppermute x6, starting transfers between devices, over_cols(): part = lax.ppermute(part, 'cols', pairs)  9.15 us
    ppermute x6, waiting for transfers between devices, along(): return lax.ppermute(value, 'rows', pairs)  8.82 us
    pallas_call x1, Pallas kernels, shards(): pl.pallas_call(functools.partial(backward_own_kernel, peers * SLOTS), out...  4.8 us
  transfers between devices with their start and end apart: 17, of which 7 were waited for; matrix products, arithmetic and copies ran while one was open for 1% of the time, Pallas kernels for 10%

profile of v6, /device:TPU:2, one launch (start us, length us, event | category | flops | bytes accessed | tf_op | source)
XLA Modules:
  0.0 115.3 jit_solution(11434667347468996439)
XLA Ops:
  0.6 2.7 %start.1 = (s32[8,4,128]{2,1,0:T(4,128)}, bf16[32,16,128]{2,1,0:T(8,128)(2,1)S(1)}, s32[8,128]{1,0:T(8,128)S(1)}) custom-call(s32[1,128]{1,0:T(1,128)} %bitcast.45, s32[1,128]{1,0:T(1,128)} %bitcast.46, bf16[16,4096]{1,0:T(8,128)(2,1)} %features_hbm.1, s32[32,128]{1,0:T(8,128)} %bitcast.35), custom_call_target="tpu_custom_call" | custom-call | tf_op jit(solution)/shard_map/start/pallas_call | solution.py:521
  3.3 6.4 %collective-permute-start = (bf16[32,16,128]{2,1,0:T(8,128)(2,1)S(1)}, bf16[32,16,128]{2,1,0:T(8,128)(2,1)S(1)}, u32[]{:S(2)}, u32[]{:S(2)}) collective-permute-start(bf16[32,16,128]{2,1,0:T(8,128)(2,1)S(1)} %get-tuple-element.27.refs_0_.own_ref), channel_id=1, source_target_pairs={{0,48},{8,56},{16,0},{24,8},{32,16},{40,24},{48,32},{56,40},{64,11... | collective-permute-start | bytes 393224 | tf_op jit(solution)/shard_map/start/ppermute | solution.py:63
  9.7 1.0 collective-permute-start.1
  10.7 2.8 %collective-permute-start.2 = (bf16[32,16,128]{2,1,0:T(8,128)(2,1)S(1)}, bf16[32,16,128]{2,1,0:T(8,128)(2,1)S(1)}, u32[]{:S(2)}, u32[]{:S(2)}) collective-permute-start(bf16[32,16,128]{2,1,0:T(8,128)(2,1)S(1)} %get-tuple-element.27.refs_0_.own_ref), channel_id=1, source_target_pairs={{0,16},{8,24},{16,32},{24,40},{32,48},{40,56},{48,0},{56,8},{64,80... | collective-permute-start | bytes 393224 | tf_op jit(solution)/shard_map/start/ppermute | solution.py:63
  13.5 5.3 %all-to-all-start = ((s32[8,4,128]{2,1,0:T(4,128)}), s32[8,4,128]{2,1,0:T(4,128)S(1)}, u32[]{:S(2)}, u32[]{:S(2)}) async-start(s32[8,4,128]{2,1,0:T(4,128)} %get-tuple-element.26), calls=%async_computation | async-start | bytes 32768 | tf_op jit(solution)/shard_map/start/all_to_all | solution.py:517
  18.8 4.8 %all-to-all-done.asked_ref = s32[8,4,128]{2,1,0:T(4,128)S(1)} async-done(((s32[8,4,128]{2,1,0:T(4,128)}), s32[8,4,128]{2,1,0:T(4,128)S(1)}, u32[]{:S(2)}, u32[]{:S(2)}) %all-to-all-start) | async-done | bytes 16416 | tf_op jit(solution)/shard_map/start/all_to_all | solution.py:517
  23.6 2.3 %pack.1 = bf16[8,32,16,128]{3,2,1,0:T(8,128)(2,1)} custom-call(s32[1]{0:T(128)} %bitcast.4.here_ref.turn_ref, s32[8,4,128]{2,1,0:T(4,128)S(1)} %all-to-all-done.asked_ref, bf16[32,16,128]{2,1,0:T(8,128)(2,1)S(1)} %get-tuple-element.27.refs_0_.own_ref, bf16[32,16,128]{2,1,0:T(8,128)(2,1)S(1)} %collective-permute-done.refs_1_, ...), custom_call_target="tpu_custom_call" | custom-call | tf_op jit(solution)/shard_map/pack/pallas_call | solution.py:546
  25.9 5.3 %all-to-all-start.1 = ((bf16[8,32,16,128]{3,2,1,0:T(8,128)(2,1)}), bf16[8,32,16,128]{3,2,1,0:T(8,128)(2,1)S(1)}, u32[]{:S(2)}, u32[]{:S(2)}) async-start(bf16[8,32,16,128]{3,2,1,0:T(8,128)(2,1)} %pack.1), calls=%async_computation.1 | async-start | bytes 2097152 | tf_op jit(solution)/shard_map/grads/all_to_all | solution.py:517
  31.4 1.1 collective-permute-done.3
  32.5 1.7 %collective-permute-start.4 = (bf16[2,4,16,128]{3,2,1,0:T(8,128)(2,1)S(1)}, bf16[2,4,16,128]{3,2,1,0:T(8,128)(2,1)S(1)}, u32[]{:S(2)}, u32[]{:S(2)}) collective-permute-start(bf16[2,4,16,128]{3,2,1,0:T(8,128)(2,1)S(1)} %get-tuple-element.54), channel_id=1, source_target_pairs={{0,2},{1,3},{2,4},{3,5},{4,6},{5,7},{6,0},{7,1},{8,10},{9,11},{10,... | collective-permute-start | bytes 98312 | tf_op jit(solution)/shard_map/grads/ppermute | solution.py:54
  34.2 2.9 %collective-permute-start.5 = (bf16[2,4,16,128]{3,2,1,0:T(8,128)(2,1)S(1)}, bf16[2,4,16,128]{3,2,1,0:T(8,128)(2,1)S(1)}, u32[]{:S(2)}, u32[]{:S(2)}) collective-permute-start(bf16[2,4,16,128]{3,2,1,0:T(8,128)(2,1)S(1)} %get-tuple-element.55), channel_id=1, source_target_pairs={{0,4},{1,5},{2,6},{3,7},{4,0},{5,1},{6,2},{7,3},{8,12},{9,13},{10,... | collective-permute-start | bytes 98312 | tf_op jit(solution)/shard_map/grads/ppermute | solution.py:54
  37.1 1.3 %collective-permute-start.6 = (bf16[2,4,16,128]{3,2,1,0:T(8,128)(2,1)S(1)}, bf16[2,4,16,128]{3,2,1,0:T(8,128)(2,1)S(1)}, u32[]{:S(2)}, u32[]{:S(2)}) collective-permute-start(bf16[2,4,16,128]{3,2,1,0:T(8,128)(2,1)S(1)} %get-tuple-element.56), channel_id=1, source_target_pairs={{0,6},{1,7},{2,0},{3,1},{4,2},{5,3},{6,4},{7,5},{8,14},{9,15},{10,... | collective-permute-start | bytes 98312 | tf_op jit(solution)/shard_map/grads/ppermute | solution.py:54
  38.4 4.7 %forward_own.1 = (f32[32,16,128]{2,1,0:T(8,128)S(1)}, bf16[128,128,128]{2,1,0:T(8,128)(2,1)}) custom-call(s32[8,128]{1,0:T(8,128)S(1)} %get-tuple-element.25.plan_ref, bf16[32,16,128]{2,1,0:T(8,128)(2,1)S(1)} %get-tuple-element.27.refs_0_.own_ref, bf16[128,128,128]{2,1,0:T(8,128)(2,1)} %tiles_hbm.1), custom_call_target="tpu_custom_call" | custom-call | flops 2147483648 | bytes 4194304 | tf_op jit(solution)/shard_map/forward_own/pallas_call | solution.py:563
  43.2 1.4 %all-to-all-done.1 = bf16[8,32,16,128]{3,2,1,0:T(8,128)(2,1)S(1)} async-done(((bf16[8,32,16,128]{3,2,1,0:T(8,128)(2,1)}), bf16[8,32,16,128]{3,2,1,0:T(8,128)(2,1)S(1)}, u32[]{:S(2)}, u32[]{:S(2)}) %all-to-all-start.1) | async-done | bytes 1048608 | tf_op jit(solution)/shard_map/grads/all_to_all | solution.py:517
  44.7 3.6 %forward.1 = bf16[8,4,16,128]{3,2,1,0:T(8,128)(2,1)S(1)} custom-call(s32[8,128]{1,0:T(8,128)S(1)} %get-tuple-element.25.plan_ref, bf16[256,16,128]{2,1,0:T(8,128)(2,1)S(1)} %bitcast.33, f32[32,16,128]{2,1,0:T(8,128)S(1)} %get-tuple-element.31.part_ref, bf16[128,128,128]{2,1,0:T(8,128)(2,1)} %get-tuple-element.32.tiles_hbm.tiles), custom_call_target="tpu_custom_call" | custom-call | flops 1073741824 | bytes 4194304 | tf_op jit(solution)/shard_map/forward/pallas_call | solution.py:585
  48.3 10.4 %all_to_all.25.got_ref = bf16[8,4,16,128]{3,2,1,0:T(8,128)(2,1)S(1)} all-to-all(bf16[8,4,16,128]{3,2,1,0:T(8,128)(2,1)S(1)} %forward.1), channel_id=1, replica_groups=mesh['rows'=32,'cols'=8] {'cols'}, dimensions={0} | all-to-all | bytes 262144 | tf_op jit(solution)/shard_map/forward/all_to_all | solution.py:594
  58.7 0.9 dense.1
  59.6 9.2 %all_to_all.26.got_ref = bf16[8,6,16,128]{3,2,1,0:T(8,128)(2,1)S(1)} all-to-all(bf16[8,6,16,128]{3,2,1,0:T(8,128)(2,1)S(1)} %get-tuple-element.35), channel_id=1, replica_groups=mesh['rows'=32,'cols'=8] {'cols'}, dimensions={0} | all-to-all | bytes 393216 | tf_op jit(solution)/shard_map/dense/all_to_all | solution.py:609
  68.9 2.9 %backward.1 = bf16[8,33,16,128]{3,2,1,0:T(8,128)(2,1)} custom-call(s32[8,128]{1,0:T(8,128)S(1)} %get-tuple-element.25.plan_ref, bf16[8,6,16,128]{3,2,1,0:T(8,128)(2,1)S(1)} %all_to_all.26.got_ref, bf16[128,128,128]{2,1,0:T(8,128)(2,1)S(1)} %copy-done), custom_call_target="tpu_custom_call" | custom-call | flops 1073741824 | bytes 4194304 | tf_op jit(solution)/shard_map/backward/pallas_call | solution.py:612
  71.8 4.9 %all-to-all-start.4 = ((bf16[8,33,16,128]{3,2,1,0:T(8,128)(2,1)}), bf16[8,33,16,128]{3,2,1,0:T(8,128)(2,1)S(1)}, u32[]{:S(2)}, u32[]{:S(2)}) async-start(bf16[8,33,16,128]{3,2,1,0:T(8,128)(2,1)} %backward.1), calls=%async_computation.4 | async-start | bytes 2162688 | tf_op jit(solution)/shard_map/backward/all_to_all | solution.py:517
  76.8 4.8 %backward_own.1 = (f32[32,16,128]{2,1,0:T(8,128)}, s32[32,128]{1,0:T(8,128)S(1)}, bf16[256,4096]{1,0:T(8,128)(2,1)S(1)}) custom-call(s32[8,128]{1,0:T(8,128)S(1)} %get-tuple-element.25.plan_ref, bf16[8,6,16,128]{3,2,1,0:T(8,128)(2,1)S(1)} %all_to_all.26.got_ref, bf16[128,128,128]{2,1,0:T(8,128)(2,1)} %get-tuple-element.32.tiles_hbm.tiles, s32[32,128]{1,0:T(8,128)S(1)} %bitcast.36), custom_call_target="tpu_custom_call" | custom-call | flops 2147483648 | bytes 4194304 | tf_op jit(solution)/shard_map/backward_own/pallas_call | solution.py:629
  81.7 1.2 %collective-permute-done.7 = bf16[4,4,16,128]{3,2,1,0:T(8,128)(2,1)S(1)} collective-permute-done((bf16[4,4,16,128]{3,2,1,0:T(8,128)(2,1)S(1)}, bf16[4,4,16,128]{3,2,1,0:T(8,128)(2,1)S(1)}, u32[]{:S(2)}, u32[]{:S(2)}) %collective-permute-start.7) | collective-permute-done | bytes 65568 | tf_op jit(solution)/shard_map/activated/ppermute | solution.py:47
  84.1 2.1 %collective-permute-start.9 = (bf16[2,4,16,128]{3,2,1,0:T(8,128)(2,1)S(1)}, bf16[2,4,16,128]{3,2,1,0:T(8,128)(2,1)S(1)}, u32[]{:S(2)}, u32[]{:S(2)}) collective-permute-start(bf16[2,4,16,128]{3,2,1,0:T(8,128)(2,1)S(1)} %get-tuple-element.49), channel_id=1, source_target_pairs={{0,4},{1,5},{2,6},{3,7},{4,0},{5,1},{6,2},{7,3},{8,12},{9,13},{10,... | collective-permute-start | bytes 98312 | tf_op jit(solution)/shard_map/activated/ppermute | solution.py:54
  86.8 3.9 %all-to-all-done.4.got_ref = bf16[8,33,16,128]{3,2,1,0:T(8,128)(2,1)S(1)} async-done(((bf16[8,33,16,128]{3,2,1,0:T(8,128)(2,1)}), bf16[8,33,16,128]{3,2,1,0:T(8,128)(2,1)S(1)}, u32[]{:S(2)}, u32[]{:S(2)}) %all-to-all-start.4) | async-done | bytes 1081376 | tf_op jit(solution)/shard_map/backward/all_to_all | solution.py:517
  90.8 1.8 %relay.1 = (f32[33,16,128]{2,1,0:T(8,128)S(1)}, bf16[34,16,128]{2,1,0:T(8,128)(2,1)S(1)}, bf16[34,16,128]{2,1,0:T(8,128)(2,1)S(1)}, bf16[34,16,128]{2,1,0:T(8,128)(2,1)S(1)}) custom-call(s32[1]{0:T(128)} %bitcast.4.here_ref.turn_ref, s32[8,4,128]{2,1,0:T(4,128)S(1)} %all-to-all-done.asked_ref, bf16[8,33,16,128]{3,2,1,0:T(8,128)(2,1)S(1)} %all-to-all-done.4.got_ref), custom_call_target="tpu_custom_call" | custom-call | tf_op jit(solution)/shard_map/relay/pallas_call | solution.py:662
  92.5 2.1 %collective-permute-start.11 = (bf16[34,16,128]{2,1,0:T(8,128)(2,1)S(1)}, bf16[34,16,128]{2,1,0:T(8,128)(2,1)S(1)}, u32[]{:S(2)}, u32[]{:S(2)}) collective-permute-start(bf16[34,16,128]{2,1,0:T(8,128)(2,1)S(1)} %get-tuple-element.40), channel_id=1, source_target_pairs={{0,16},{8,24},{16,32},{24,40},{32,48},{40,56},{48,0},{56,8},{64,80... | collective-permute-start | bytes 417800 | tf_op jit(solution)/shard_map/relay/ppermute | solution.py:63
  94.6 4.8 %collective-permute-start.12 = (bf16[34,16,128]{2,1,0:T(8,128)(2,1)S(1)}, bf16[34,16,128]{2,1,0:T(8,128)(2,1)S(1)}, u32[]{:S(2)}, u32[]{:S(2)}) collective-permute-start(bf16[34,16,128]{2,1,0:T(8,128)(2,1)S(1)} %get-tuple-element.41), channel_id=1, source_target_pairs={{0,32},{8,40},{16,48},{24,56},{32,0},{40,8},{48,16},{56,24},{64,96... | collective-permute-start | bytes 417800 | tf_op jit(solution)/shard_map/relay/ppermute | solution.py:63
  99.4 3.0 %collective-permute-start.13 = (bf16[34,16,128]{2,1,0:T(8,128)(2,1)S(1)}, bf16[34,16,128]{2,1,0:T(8,128)(2,1)S(1)}, u32[]{:S(2)}, u32[]{:S(2)}) collective-permute-start(bf16[34,16,128]{2,1,0:T(8,128)(2,1)S(1)} %get-tuple-element.42), channel_id=1, source_target_pairs={{0,48},{8,56},{16,0},{24,8},{32,16},{40,24},{48,32},{56,40},{64,11... | collective-permute-start | bytes 417800 | tf_op jit(solution)/shard_map/relay/ppermute | solution.py:63
  102.4 0.8 pad_maximum_fusion.1.got_ref
  103.9 1.1 collective-permute-done.12.two_ref
  105.1 7.7 %collective-permute-done.13.three_ref = bf16[34,16,128]{2,1,0:T(8,128)(2,1)S(1)} collective-permute-done((bf16[34,16,128]{2,1,0:T(8,128)(2,1)S(1)}, bf16[34,16,128]{2,1,0:T(8,128)(2,1)S(1)}, u32[]{:S(2)}, u32[]{:S(2)}) %collective-permute-start.13) | collective-permute-done | bytes 139296 | tf_op jit(solution)/shard_map/relay/ppermute | solution.py:63
  112.8 2.4 %final.1 = (bf16[16,4096]{1,0:T(8,128)(2,1)}, f32[16,128]{1,0:T(8,128)}) custom-call(f32[32,16,128]{2,1,0:T(8,128)} %get-tuple-element.38.kept_hbm, f32[33,16,128]{2,1,0:T(8,128)S(1)} %get-tuple-element.39.own_ref, bf16[34,16,128]{2,1,0:T(8,128)(2,1)S(1)} %collective-permute-done.11.one_ref, bf16[34,16,128]{2,1,0:T(8,128)(2,1)S(1)} %collective-permute-done.12.two_ref, ...), custom_call_target="tpu_custom_call" | custom-call | tf_op jit(solution)/shard_map/final/pallas_call | solution.py:675
  (31 shorter events, 2.9 us)
Async XLA Ops:
  0.6 30.5 %copy-start.1 = (bf16[16,4096]{1,0:T(8,128)(2,1)S(1)}, bf16[16,4096]{1,0:T(8,128)(2,1)}, u32[]{:S(2)}) copy-start(bf16[16,4096]{1,0:T(8,128)(2,1)} %grad_ref) | copy-start | bytes 393220
  3.3 20.2 %collective-permute-start = (bf16[32,16,128]{2,1,0:T(8,128)(2,1)S(1)}, bf16[32,16,128]{2,1,0:T(8,128)(2,1)S(1)}, u32[]{:S(2)}, u32[]{:S(2)}) collective-permute-start(bf16[32,16,128]{2,1,0:T(8,128)(2,1)S(1)} %get-tuple-element.27.refs_0_.own_ref), channel_id=1, source_target_pairs={{0,48},{8,56},{16,0},{24,8},{32,16},{40,24},{48,32},{56,40},{64,11... | collective-permute-start | bytes 393224 | tf_op jit(solution)/shard_map/start/ppermute | solution.py:63
  9.7 13.9 %collective-permute-start.1 = (bf16[32,16,128]{2,1,0:T(8,128)(2,1)S(1)}, bf16[32,16,128]{2,1,0:T(8,128)(2,1)S(1)}, u32[]{:S(2)}, u32[]{:S(2)}) collective-permute-start(bf16[32,16,128]{2,1,0:T(8,128)(2,1)S(1)} %get-tuple-element.27.refs_0_.own_ref), channel_id=1, source_target_pairs={{0,32},{8,40},{16,48},{24,56},{32,0},{40,8},{48,16},{56,24},{64,96... | collective-permute-start | bytes 393224 | tf_op jit(solution)/shard_map/start/ppermute | solution.py:63
  10.7 12.9 %collective-permute-start.2 = (bf16[32,16,128]{2,1,0:T(8,128)(2,1)S(1)}, bf16[32,16,128]{2,1,0:T(8,128)(2,1)S(1)}, u32[]{:S(2)}, u32[]{:S(2)}) collective-permute-start(bf16[32,16,128]{2,1,0:T(8,128)(2,1)S(1)} %get-tuple-element.27.refs_0_.own_ref), channel_id=1, source_target_pairs={{0,16},{8,24},{16,32},{24,40},{32,48},{40,56},{48,0},{56,8},{64,80... | collective-permute-start | bytes 393224 | tf_op jit(solution)/shard_map/start/ppermute | solution.py:63
  13.5 10.0 %all-to-all-start = ((s32[8,4,128]{2,1,0:T(4,128)}), s32[8,4,128]{2,1,0:T(4,128)S(1)}, u32[]{:S(2)}, u32[]{:S(2)}) async-start(s32[8,4,128]{2,1,0:T(4,128)} %get-tuple-element.26), calls=%async_computation | async-start | bytes 32768 | tf_op jit(solution)/shard_map/start/all_to_all | solution.py:517
  25.9 18.8 %all-to-all-start.1 = ((bf16[8,32,16,128]{3,2,1,0:T(8,128)(2,1)}), bf16[8,32,16,128]{3,2,1,0:T(8,128)(2,1)S(1)}, u32[]{:S(2)}, u32[]{:S(2)}) async-start(bf16[8,32,16,128]{3,2,1,0:T(8,128)(2,1)} %pack.1), calls=%async_computation.1 | async-start | bytes 2097152 | tf_op jit(solution)/shard_map/grads/all_to_all | solution.py:517
  31.2 1.3 %collective-permute-start.3 = (bf16[4,4,16,128]{3,2,1,0:T(8,128)(2,1)S(1)}, bf16[4,4,16,128]{3,2,1,0:T(8,128)(2,1)S(1)}, u32[]{:S(2)}, u32[]{:S(2)}) collective-permute-start(bf16[4,4,16,128]{3,2,1,0:T(8,128)(2,1)S(1)} %get-tuple-element.57), channel_id=1, source_target_pairs={{0,1},{1,0},{2,3},{3,2},{4,5},{5,4},{6,7},{7,6},{8,9},{9,8},{10,11... | collective-permute-start | bytes 196616 | tf_op jit(solution)/shard_map/grads/ppermute | solution.py:47
  32.5 10.6 %collective-permute-start.4 = (bf16[2,4,16,128]{3,2,1,0:T(8,128)(2,1)S(1)}, bf16[2,4,16,128]{3,2,1,0:T(8,128)(2,1)S(1)}, u32[]{:S(2)}, u32[]{:S(2)}) collective-permute-start(bf16[2,4,16,128]{3,2,1,0:T(8,128)(2,1)S(1)} %get-tuple-element.54), channel_id=1, source_target_pairs={{0,2},{1,3},{2,4},{3,5},{4,6},{5,7},{6,0},{7,1},{8,10},{9,11},{10,... | collective-permute-start | bytes 98312 | tf_op jit(solution)/shard_map/grads/ppermute | solution.py:54
  34.2 9.0 %collective-permute-start.5 = (bf16[2,4,16,128]{3,2,1,0:T(8,128)(2,1)S(1)}, bf16[2,4,16,128]{3,2,1,0:T(8,128)(2,1)S(1)}, u32[]{:S(2)}, u32[]{:S(2)}) collective-permute-start(bf16[2,4,16,128]{3,2,1,0:T(8,128)(2,1)S(1)} %get-tuple-element.55), channel_id=1, source_target_pairs={{0,4},{1,5},{2,6},{3,7},{4,0},{5,1},{6,2},{7,3},{8,12},{9,13},{10,... | collective-permute-start | bytes 98312 | tf_op jit(solution)/shard_map/grads/ppermute | solution.py:54
  37.1 6.1 %collective-permute-start.6 = (bf16[2,4,16,128]{3,2,1,0:T(8,128)(2,1)S(1)}, bf16[2,4,16,128]{3,2,1,0:T(8,128)(2,1)S(1)}, u32[]{:S(2)}, u32[]{:S(2)}) collective-permute-start(bf16[2,4,16,128]{3,2,1,0:T(8,128)(2,1)S(1)} %get-tuple-element.56), channel_id=1, source_target_pairs={{0,6},{1,7},{2,0},{3,1},{4,2},{5,3},{6,4},{7,5},{8,14},{9,15},{10,... | collective-permute-start | bytes 98312 | tf_op jit(solution)/shard_map/grads/ppermute | solution.py:54
  44.7 14.0 %copy-start.2 = (bf16[128,128]{1,0:T(8,128)(2,1)S(1)}, bf16[128,128]{1,0:T(8,128)(2,1)}, u32[]{:S(2)}) copy-start(bf16[128,128]{1,0:T(8,128)(2,1)} %weight_ref.1) | copy-start | bytes 98308
  44.7 24.2 %copy-start = (bf16[128,128,128]{2,1,0:T(8,128)(2,1)S(1)}, bf16[128,128,128]{2,1,0:T(8,128)(2,1)}, u32[]{:S(2)}) copy-start(bf16[128,128,128]{2,1,0:T(8,128)(2,1)} %get-tuple-element.32.tiles_hbm.tiles) | copy-start | bytes 12582916
  71.8 5.0 %copy-start.3 = (s32[4096]{0:T(1024)S(1)}, s32[4096]{0:T(1024)}, u32[]{:S(2)}) copy-start(s32[4096]{0:T(1024)} %param.8) | copy-start | bytes 49156
  71.8 19.0 %all-to-all-start.4 = ((bf16[8,33,16,128]{3,2,1,0:T(8,128)(2,1)}), bf16[8,33,16,128]{3,2,1,0:T(8,128)(2,1)S(1)}, u32[]{:S(2)}, u32[]{:S(2)}) async-start(bf16[8,33,16,128]{3,2,1,0:T(8,128)(2,1)} %backward.1), calls=%async_computation.4 | async-start | bytes 2162688 | tf_op jit(solution)/shard_map/backward/all_to_all | solution.py:517
  76.7 4.8 %copy-start.4 = (bf16[8,4,16,128]{3,2,1,0:T(8,128)(2,1)S(1)}, bf16[8,4,16,128]{3,2,1,0:T(8,128)(2,1)}, u32[]{:S(2)}) copy-start(bf16[8,4,16,128]{3,2,1,0:T(8,128)(2,1)} %get-tuple-element.37) | copy-start | bytes 393220
  81.6 1.3 %collective-permute-start.7 = (bf16[4,4,16,128]{3,2,1,0:T(8,128)(2,1)S(1)}, bf16[4,4,16,128]{3,2,1,0:T(8,128)(2,1)S(1)}, u32[]{:S(2)}, u32[]{:S(2)}) collective-permute-start(bf16[4,4,16,128]{3,2,1,0:T(8,128)(2,1)S(1)} %get-tuple-element.51), channel_id=1, source_target_pairs={{0,1},{1,0},{2,3},{3,2},{4,5},{5,4},{6,7},{7,6},{8,9},{9,8},{10,11... | collective-permute-start | bytes 196616 | tf_op jit(solution)/shard_map/activated/ppermute | solution.py:47
  83.6 15.9 %collective-permute-start.8 = (bf16[2,4,16,128]{3,2,1,0:T(8,128)(2,1)}, bf16[2,4,16,128]{3,2,1,0:T(8,128)(2,1)S(1)}, u32[]{:S(2)}, u32[]{:S(2)}) collective-permute-start(bf16[2,4,16,128]{3,2,1,0:T(8,128)(2,1)} %get-tuple-element.48), channel_id=1, source_target_pairs={{0,2},{1,3},{2,4},{3,5},{4,6},{5,7},{6,0},{7,1},{8,10},{9,11},{10,... | collective-permute-start | bytes 98312 | tf_op jit(solution)/shard_map/activated/ppermute | solution.py:54
  84.1 18.3 %collective-permute-start.9 = (bf16[2,4,16,128]{3,2,1,0:T(8,128)(2,1)S(1)}, bf16[2,4,16,128]{3,2,1,0:T(8,128)(2,1)S(1)}, u32[]{:S(2)}, u32[]{:S(2)}) collective-permute-start(bf16[2,4,16,128]{3,2,1,0:T(8,128)(2,1)S(1)} %get-tuple-element.49), channel_id=1, source_target_pairs={{0,4},{1,5},{2,6},{3,7},{4,0},{5,1},{6,2},{7,3},{8,12},{9,13},{10,... | collective-permute-start | bytes 98312 | tf_op jit(solution)/shard_map/activated/ppermute | solution.py:54
  86.2 16.2 %collective-permute-start.10 = (bf16[2,4,16,128]{3,2,1,0:T(8,128)(2,1)S(1)}, bf16[2,4,16,128]{3,2,1,0:T(8,128)(2,1)}, u32[]{:S(2)}, u32[]{:S(2)}) collective-permute-start(bf16[2,4,16,128]{3,2,1,0:T(8,128)(2,1)S(1)} %get-tuple-element.50), channel_id=1, source_target_pairs={{0,6},{1,7},{2,0},{3,1},{4,2},{5,3},{6,4},{7,5},{8,14},{9,15},{10,... | collective-permute-start | bytes 98312 | tf_op jit(solution)/shard_map/activated/ppermute | solution.py:54
  92.5 11.4 %collective-permute-start.11 = (bf16[34,16,128]{2,1,0:T(8,128)(2,1)S(1)}, bf16[34,16,128]{2,1,0:T(8,128)(2,1)S(1)}, u32[]{:S(2)}, u32[]{:S(2)}) collective-permute-start(bf16[34,16,128]{2,1,0:T(8,128)(2,1)S(1)} %get-tuple-element.40), channel_id=1, source_target_pairs={{0,16},{8,24},{16,32},{24,40},{32,48},{40,56},{48,0},{56,8},{64,80... | collective-permute-start | bytes 417800 | tf_op jit(solution)/shard_map/relay/ppermute | solution.py:63
  94.6 10.5 %collective-permute-start.12 = (bf16[34,16,128]{2,1,0:T(8,128)(2,1)S(1)}, bf16[34,16,128]{2,1,0:T(8,128)(2,1)S(1)}, u32[]{:S(2)}, u32[]{:S(2)}) collective-permute-start(bf16[34,16,128]{2,1,0:T(8,128)(2,1)S(1)} %get-tuple-element.41), channel_id=1, source_target_pairs={{0,32},{8,40},{16,48},{24,56},{32,0},{40,8},{48,16},{56,24},{64,96... | collective-permute-start | bytes 417800 | tf_op jit(solution)/shard_map/relay/ppermute | solution.py:63
  99.4 13.3 %collective-permute-start.13 = (bf16[34,16,128]{2,1,0:T(8,128)(2,1)S(1)}, bf16[34,16,128]{2,1,0:T(8,128)(2,1)S(1)}, u32[]{:S(2)}, u32[]{:S(2)}) collective-permute-start(bf16[34,16,128]{2,1,0:T(8,128)(2,1)S(1)} %get-tuple-element.42), channel_id=1, source_target_pairs={{0,48},{8,56},{16,0},{24,8},{32,16},{40,24},{48,32},{56,40},{64,11... | collective-permute-start | bytes 417800 | tf_op jit(solution)/shard_map/relay/ppermute | solution.py:63
